TPU v7x, 512 devices: a whole 4x8x8 slice. The times are simulated.
512 devices in a mesh: group: 16 (over y, core), peer: 32 (over x, z).
Axes of the slice: x: 4, y: 8, z: 8, core: 2. Of those that a mesh axis runs over, the one named last changes fastest.
Arguments:
- trace_rows: bfloat16 [1024, 8, 32, 512], P(('group', 'peer')), may hold values from -40 to 40
- upstream: bfloat16 [1024, 8, 32, 512], P(('group', 'peer')), may hold values from -6 to 6
- counts: int32 [16, 64], P('group', 'peer'), may hold values from 1 to 8, 256 in all within a row
- w_query: bfloat16 [512, 512], P('peer'), may hold values from -0.25 to 0.25
- w_key: bfloat16 [512, 512], P('peer'), may hold values from -0.25 to 0.25
- w_value: bfloat16 [512, 512], P('peer'), may hold values from -0.25 to 0.25
- w_out: bfloat16 [512, 512], P('peer'), may hold values from -0.25 to 0.25
Outputs:
- trace_grads: bfloat16 [1024, 8, 32, 512], P(('group', 'peer'))
- query_grad: float32 [512, 512], P('peer')
- key_grad: float32 [512, 512], P('peer')
- value_grad: float32 [512, 512], P('peer')
- output_grad: float32 [512, 512], P('peer')
Inputs may be any that keep to these rules, and one draw needn't show every extreme that they name: In each row of counts (one group) the 64 counts sum to exactly 256, and the largest is 8.
All inputs are finite; a program needn't handle non-finite values.
Results may differ from a plain program's by a relative error of at most 0.03.
Values may be sent and summed in bfloat16 or wider, within the bound.
No kernel may reach another device: no remote copies, remote signals or barrier semaphores. Data moves between devices by JAX's collectives and lax.ppermute only.
A program may use at most 64 MiB of HBM per device.

v0:
```python
import math

import jax
import jax.numpy as jnp
from jax import lax
from jax.sharding import PartitionSpec as P

HEADS = 8


score_gain = 6.0
tiny_eps = 1e-06


def dot_rows(first_op, second_op):
    return lax.dot_general(
        first_op, second_op, (((1,), (1,)), ((), ())), preferred_element_type=jnp.float32
    )


def dot_cols(first_op, second_op):
    return lax.dot_general(
        first_op, second_op, (((0,), (0,)), ((), ())), preferred_element_type=jnp.float32
    )


def unit_heads(values):
    split_heads = values.reshape(values.shape[0], HEADS, values.shape[1] // HEADS)
    inv_scale = lax.rsqrt(jnp.mean(split_heads * split_heads, axis=-1, keepdims=True) + tiny_eps)
    return (split_heads * inv_scale, inv_scale)


def layer_backward(rows, grad_in, weights):
    w_query, w_key, w_value, w_out = weights
    row_count, row_length, feature_width = rows.shape
    token_count = row_count * row_length
    inner_width = w_query.shape[1]
    head_size = inner_width // HEADS
    flat_rows = rows.reshape(token_count, feature_width).astype(jnp.float32)
    inv_rms = lax.rsqrt(jnp.mean(flat_rows * flat_rows, axis=-1, keepdims=True) + tiny_eps)
    scaled = flat_rows * inv_rms
    normed = scaled.astype(jnp.bfloat16)
    queries = jnp.dot(normed, w_query, preferred_element_type=jnp.float32)
    keys_full = jnp.dot(normed, w_key, preferred_element_type=jnp.float32)
    values_full = jnp.dot(normed, w_value, preferred_element_type=jnp.float32)
    q_unit, q_scale = unit_heads(queries)
    k_unit, k_scale = unit_heads(keys_full)
    per_block = math.gcd(row_count, max(1, 128 // row_length))
    block_span = per_block * row_length
    block_count = token_count // block_span
    q_half = q_unit.astype(jnp.bfloat16).reshape(block_count, block_span, HEADS, head_size)
    k_half = k_unit.astype(jnp.bfloat16).reshape(block_count, block_span, HEADS, head_size)
    v_half = values_full.astype(jnp.bfloat16).reshape(block_count, block_span, HEADS, head_size)
    position = lax.iota(jnp.int32, block_span) // row_length
    same_row = position[:, None] == position[None, :]
    scores = jnp.einsum("bqhd,bkhd->bhqk", q_half, k_half, preferred_element_type=jnp.float32) * (
        score_gain / head_size
    )
    exp_scores = jnp.where(same_row, jnp.exp(scores), 0.0)
    att_probs = exp_scores / jnp.sum(exp_scores, axis=-1, keepdims=True)
    probs_half = att_probs.astype(jnp.bfloat16)
    attended = jnp.einsum("bhqk,bkhd->bqhd", probs_half, v_half, preferred_element_type=jnp.float32)
    attended_half = attended.astype(jnp.bfloat16).reshape(token_count, inner_width)
    grad_out = grad_in.reshape(token_count, feature_width)
    grad_att = dot_rows(grad_out, w_out).astype(jnp.bfloat16)
    grad_heads = grad_att.reshape(block_count, block_span, HEADS, head_size)
    grad_probs = jnp.einsum(
        "bqhd,bkhd->bhqk", grad_heads, v_half, preferred_element_type=jnp.float32
    )
    grad_value = jnp.einsum(
        "bhqk,bqhd->bkhd", probs_half, grad_heads, preferred_element_type=jnp.float32
    )
    weighted = jnp.sum(att_probs * grad_probs, axis=-1, keepdims=True)
    grad_scores = (score_gain / head_size * att_probs * (grad_probs - weighted)).astype(
        jnp.bfloat16
    )
    grad_qunit = jnp.einsum(
        "bhqk,bkhd->bqhd", grad_scores, k_half, preferred_element_type=jnp.float32
    ).reshape(token_count, HEADS, head_size)
    grad_kunit = jnp.einsum(
        "bhqk,bqhd->bkhd", grad_scores, q_half, preferred_element_type=jnp.float32
    ).reshape(token_count, HEADS, head_size)
    grad_query = q_scale * (
        grad_qunit - q_unit * jnp.mean(q_unit * grad_qunit, axis=-1, keepdims=True)
    )
    grad_key = k_scale * (
        grad_kunit - k_unit * jnp.mean(k_unit * grad_kunit, axis=-1, keepdims=True)
    )
    dq_half = grad_query.reshape(token_count, inner_width).astype(jnp.bfloat16)
    dk_half = grad_key.reshape(token_count, inner_width).astype(jnp.bfloat16)
    dv_half = grad_value.reshape(token_count, inner_width).astype(jnp.bfloat16)
    grad_norm = dot_rows(dq_half, w_query) + dot_rows(dk_half, w_key) + dot_rows(dv_half, w_value)
    grad_flat = grad_out.astype(jnp.float32) + inv_rms * (
        grad_norm - scaled * jnp.mean(scaled * grad_norm, axis=-1, keepdims=True)
    )
    saved_terms = (normed, attended_half, dq_half, dk_half, dv_half, grad_out)
    return (grad_flat.astype(jnp.bfloat16).reshape(rows.shape), saved_terms)


def grad_terms(saved_terms):
    normed, attended_half, dq_half, dk_half, dv_half, grad_out = saved_terms
    return jnp.concatenate(
        (
            dot_cols(normed, dq_half),
            dot_cols(normed, dk_half),
            dot_cols(normed, dv_half),
            dot_cols(attended_half, grad_out),
        ),
        axis=1,
    )


def local(trace_rows, upstream, counts, w_query, w_key, w_value, w_out):
    weights = (
        lax.all_gather(w_query, "peer", axis=0, tiled=True),
        lax.all_gather(w_key, "peer", axis=0, tiled=True),
        lax.all_gather(w_value, "peer", axis=0, tiled=True),
        lax.all_gather(w_out, "peer", axis=0, tiled=True),
    )
    peer_count = lax.axis_size("peer")
    group_count = lax.axis_size("group")
    view_count, most_rows, row_length, feature_width = trace_rows.shape
    slot_count = view_count * most_rows
    work_count = slot_count // 2
    view_counts = counts.reshape(view_count)
    is_live = lax.iota(jnp.int32, most_rows)[None, :] < view_counts[:, None]
    nothing = jnp.zeros((), trace_rows.dtype)
    masked = jnp.where(is_live[:, :, None, None], upstream, nothing)
    rows_flat = trace_rows.reshape(slot_count, row_length, feature_width)
    masked_flat = masked.reshape(slot_count, row_length, feature_width)
    pair_slots = -(-slot_count // peer_count)
    own_total = jnp.sum(view_counts)
    peer_totals = lax.all_gather(own_total.reshape(1), "peer", axis=0, tiled=True)
    peer_starts = jnp.cumsum(peer_totals) - peer_totals
    own_index = lax.axis_index("peer")
    peer_ids = lax.iota(jnp.int32, peer_count)
    own_base = jnp.sum(jnp.where(peer_ids == own_index, peer_starts, 0))
    view_starts = jnp.cumsum(view_counts) - view_counts
    position = lax.iota(jnp.int32, peer_count * pair_slots)
    target_peer = position // pair_slots
    row_order = (target_peer - own_base) % peer_count + position % pair_slots * peer_count
    sending = row_order < own_total
    which_view = jnp.sum((view_starts[None, :] <= row_order[:, None]).astype(jnp.int32), axis=1) - 1
    view_ids = lax.iota(jnp.int32, view_count)
    view_start = jnp.sum(
        jnp.where(view_ids[None, :] == which_view[:, None], view_starts[None, :], 0), axis=1
    )
    source_slot = jnp.where(sending, which_view * most_rows + row_order - view_start, 0)
    keep_mask = sending[:, None, None]
    rows_send = jnp.where(keep_mask, jnp.take(rows_flat, source_slot, axis=0), nothing)
    grads_send = jnp.where(keep_mask, jnp.take(masked_flat, source_slot, axis=0), nothing)
    rows_recv, grads_recv = (
        lax.all_to_all(rows_send, "peer", split_axis=0, concat_axis=0, tiled=True),
        lax.all_to_all(grads_send, "peer", split_axis=0, concat_axis=0, tiled=True),
    )
    global_rank = lax.iota(jnp.int32, work_count) * peer_count + own_index
    owner_peer = (
        jnp.sum((peer_starts[None, :] <= global_rank[:, None]).astype(jnp.int32), axis=1) - 1
    )
    owner_start = jnp.sum(
        jnp.where(peer_ids[None, :] == owner_peer[:, None], peer_starts[None, :], 0), axis=1
    )
    source_rows = owner_peer * pair_slots + (global_rank - owner_start) // peer_count
    work_rows = jnp.take(rows_recv, source_rows, axis=0)
    work_grads = jnp.take(grads_recv, source_rows, axis=0)
    done_rows, saved_terms = layer_backward(work_rows, work_grads, weights)
    sender = position // pair_slots
    sender_start = jnp.take(peer_starts, sender)
    sender_total = jnp.take(peer_totals, sender)
    offset = (own_index - sender_start) % peer_count + position % pair_slots * peer_count
    is_valid = offset < sender_total
    target_slot = jnp.where(is_valid, (sender_start + offset) // peer_count, 0)
    back_send = jnp.where(
        is_valid[:, None, None], jnp.take(done_rows, target_slot, axis=0), nothing
    )
    back_recv = lax.all_to_all(back_send, "peer", split_axis=0, concat_axis=0, tiled=True)
    local_order = (view_starts[:, None] + lax.iota(jnp.int32, most_rows)[None, :]).reshape(
        slot_count
    )
    live_flat = is_live.reshape(slot_count)
    slot_place = (own_base + local_order) % peer_count * pair_slots + local_order // peer_count
    slot_place = jnp.where(live_flat, slot_place, 0)
    trace_grads = jnp.where(
        live_flat[:, None, None], jnp.take(back_recv, slot_place, axis=0), nothing
    ).reshape(trace_rows.shape)
    peer_shard = lax.psum_scatter(
        grad_terms(saved_terms).astype(jnp.bfloat16), "peer", scatter_dimension=0, tiled=True
    )
    grad_shard = lax.psum(peer_shard, "group").astype(jnp.float32)
    grad_scale = 1.0 / math.sqrt(group_count * peer_count * work_count * row_length)
    scaled_shard = grad_shard * grad_scale
    return (
        trace_grads,
        scaled_shard[:, 0:feature_width],
        scaled_shard[:, feature_width : 2 * feature_width],
        scaled_shard[:, 2 * feature_width : 3 * feature_width],
        scaled_shard[:, 3 * feature_width : 4 * feature_width],
    )


def solution(mesh):
    in_specs = (
        P(("group", "peer"), None, None, None),
        P(("group", "peer"), None, None, None),
        P("group", "peer"),
        P("peer", None),
        P("peer", None),
        P("peer", None),
        P("peer", None),
    )
    out_specs = (
        P(("group", "peer"), None, None, None),
        P("peer", None),
        P("peer", None),
        P("peer", None),
        P("peer", None),
    )
    return jax.shard_map(local, mesh=mesh, in_specs=in_specs, out_specs=out_specs, check_vma=False)
```

profile of v0, /device:TPU:1, one launch (start us, length us, event | category | flops | bytes accessed | tf_op | source)
XLA Modules:
  0.0 674.2 jit_solution(12115238516462732850)
XLA Ops:
  7.2 0.9 reduce-window.15
  8.1 1.3 fusion.47
  10.0 1.3 dynamic-slice
  11.3 1.4 dynamic-update-slice
  12.7 22.7 %all-reduce = s32[32]{0:T(128)S(1)} all-reduce(s32[32]{0:T(128)S(1)} %dynamic-update-slice), channel_id=1, replica_groups=mesh['group'=16,'peer'=32] {'peer'}, use_global_device_ids=true, to_apply=%add | all-reduce | flops 32 | bytes 256
  37.2 1.3 compare_and_fusion.1
  38.5 1.4 compare_and_fusion.3
  39.9 1.1 broadcast_select_fusion
  42.3 1.7 select_select_fusion
  44.0 4.8 all-to-all-start.1
  48.8 53.8 %all_gather.17 = bf16[512,512]{1,0:T(8,128)(2,1)S(1)} all-gather(bf16[16,512]{1,0:T(8,128)(2,1)S(1)} %copy-done.20), channel_id=1, replica_groups=mesh['group'=16,'peer'=32] {'peer'}, dimensions={0}, use_global_device_ids=true | all-gather | bytes 540672 | tf_op jit(solution)/shard_map/all_gather | solution.py:116
  102.6 1.0 copy.85
  103.6 36.8 %all_gather.16 = bf16[512,512]{1,0:T(8,128)(2,1)S(1)} all-gather(bf16[16,512]{1,0:T(8,128)(2,1)S(1)} %copy-done.21), channel_id=1, replica_groups=mesh['group'=16,'peer'=32] {'peer'}, dimensions={0}, use_global_device_ids=true | all-gather | bytes 540672 | tf_op jit(solution)/shard_map/all_gather | solution.py:115
  141.1 36.6 %all_gather.19 = bf16[512,512]{1,0:T(8,128)(2,1)S(1)} all-gather(bf16[16,512]{1,0:T(8,128)(2,1)S(1)} %copy-done.22), channel_id=1, replica_groups=mesh['group'=16,'peer'=32] {'peer'}, dimensions={0}, use_global_device_ids=true | all-gather | bytes 540672 | tf_op jit(solution)/shard_map/all_gather | solution.py:117
  177.8 40.0 %all_gather.18 = bf16[512,512]{1,0:T(8,128)(2,1)} all-gather(bf16[16,512]{1,0:T(8,128)(2,1)S(1)} %copy-done.23), channel_id=1, replica_groups=mesh['group'=16,'peer'=32] {'peer'}, dimensions={0}, use_global_device_ids=true | all-gather | bytes 540672 | tf_op jit(solution)/shard_map/all_gather | solution.py:118
  217.8 6.9 %all-to-all-start = ((bf16[32,32,512]{2,1,0:T(8,128)(2,1)}), bf16[32,32,512]{2,1,0:T(8,128)(2,1)}, u32[]{:S(2)}, u32[]{:S(2)}) async-start(bf16[32,32,512]{2,1,0:T(8,128)(2,1)} %get-tuple-element.43), calls=%async_computation | async-start | bytes 2097152 | tf_op jit(solution)/shard_map/all_to_all | solution.py:154
  225.0 1.8 gather_fusion.7
  227.8 1.0 copy.91
  229.0 1.4 multiply_reduce_fusion.2
  230.8 10.9 %all-to-all-done = bf16[32,32,512]{2,1,0:T(8,128)(2,1)} async-done(((bf16[32,32,512]{2,1,0:T(8,128)(2,1)}), bf16[32,32,512]{2,1,0:T(8,128)(2,1)}, u32[]{:S(2)}, u32[]{:S(2)}) %all-to-all-start) | async-done | bytes 1048608 | tf_op jit(solution)/shard_map/all_to_all | solution.py:154
  241.7 1.8 gather_fusion.5
  243.6 2.2 convolution_convert_fusion.7
  245.8 1.3 reshape.572
  247.1 1.0 copy.90
  248.2 2.5 fusion.57
  250.7 2.8 multiply_reduce_fusion
  253.5 1.8 multiply_convert_fusion
  255.6 1.3 convolution_bitcast_fusion
  256.9 1.4 fusion.1
  258.2 2.8 fusion.2
  261.0 2.6 fusion.3
  263.9 0.8 copy-done.5
  267.2 2.5 copy.112
  269.8 0.7 gather_fusion.2
  270.5 0.7 gather_fusion.3
  273.4 1.2 select_select_fusion.2
  274.6 5.5 all-to-all-start.2
  280.5 0.7 fusion.46
  281.1 22.9 %all-to-all-done.2 = bf16[32,32,512]{2,1,0:T(8,128)(2,1)S(1)} async-done(((bf16[32,32,512]{2,1,0:T(8,128)(2,1)}), bf16[32,32,512]{2,1,0:T(8,128)(2,1)S(1)}, u32[]{:S(2)}, u32[]{:S(2)}) %all-to-all-start.2) | async-done | bytes 1048608 | tf_op jit(solution)/shard_map/all_to_all | solution.py:176
  304.6 238.3 %reduce-scatter.4.cloned.1.call-done = bf16[16,2048]{1,0:T(8,128)(2,1)} async-done(((bf16[512,2048]{1,0:T(8,128)(2,1)}), bf16[16,2048]{1,0:T(8,128)(2,1)}) %reduce-scatter.4.cloned.1.call-update) | async-done | bytes 65552
  543.0 1.8 copy.113
  544.9 0.9 select_select_fusion.3
  545.8 117.5 %all-reduce.3.cloned.1.call-done = bf16[16,2048]{0,1:T(8,128)(2,1)} async-done(((bf16[16,2048]{0,1:T(8,128)(2,1)}), bf16[16,2048]{0,1:T(8,128)(2,1)}) %all-reduce.3.cloned.1.call-update) | async-done | bytes 65552 | tf_op jit(solution)/shard_map/psum | solution.py:189
  663.3 1.1 convert_multiply_fusion
  664.5 0.7 copy.104
  665.2 0.7 copy.105
  665.9 0.7 copy.106
  666.6 0.7 copy.107
  (118 shorter events, 12.3 us)
Async XLA Ops:
  7.2 34.5 %copy-start = (bf16[2,8,32,512]{3,2,1,0:T(8,128)(2,1)S(1)}, bf16[2,8,32,512]{3,2,1,0:T(8,128)(2,1)}, u32[]{:S(2)}) copy-start(bf16[2,8,32,512]{3,2,1,0:T(8,128)(2,1)} %param.13) | copy-start | bytes 1572868
  44.0 4.8 copy-start.20
  44.0 59.7 %copy-start.21 = (bf16[16,512]{1,0:T(8,128)(2,1)S(1)}, bf16[16,512]{1,0:T(8,128)(2,1)}, u32[]{:S(2)}) copy-start(bf16[16,512]{1,0:T(8,128)(2,1)} %param.16) | copy-start | bytes 49156
  44.0 173.8 %all-to-all-start.1 = ((bf16[32,32,512]{2,1,0:T(8,128)(2,1)}), bf16[32,32,512]{2,1,0:T(8,128)(2,1)}, u32[]{:S(2)}, u32[]{:S(2)}) async-start(bf16[32,32,512]{2,1,0:T(8,128)(2,1)} %get-tuple-element.42), calls=%async_computation.1 | async-start | bytes 2097152 | tf_op jit(solution)/shard_map/all_to_all | solution.py:153
  48.8 92.3 %copy-start.22 = (bf16[16,512]{1,0:T(8,128)(2,1)S(1)}, bf16[16,512]{1,0:T(8,128)(2,1)}, u32[]{:S(2)}) copy-start(bf16[16,512]{1,0:T(8,128)(2,1)} %param.18) | copy-start | bytes 49156
  48.8 128.9 %copy-start.23 = (bf16[16,512]{1,0:T(8,128)(2,1)S(1)}, bf16[16,512]{1,0:T(8,128)(2,1)}, u32[]{:S(2)}) copy-start(bf16[16,512]{1,0:T(8,128)(2,1)} %param.19) | copy-start | bytes 49156
  140.5 77.3 %copy-start.1 = (bf16[512,512]{1,0:T(8,128)(2,1)}, bf16[512,512]{1,0:T(8,128)(2,1)S(1)}, u32[]{:S(2)}) copy-start(bf16[512,512]{1,0:T(8,128)(2,1)S(1)} %all_gather.16) | copy-start | bytes 1572868
  177.8 49.8 %copy-start.3 = (bf16[512,512]{1,0:T(8,128)(2,1)}, bf16[512,512]{1,0:T(8,128)(2,1)S(1)}, u32[]{:S(2)}) copy-start(bf16[512,512]{1,0:T(8,128)(2,1)S(1)} %all_gather.19) | copy-start | bytes 1572868
  217.8 24.0 %all-to-all-start = ((bf16[32,32,512]{2,1,0:T(8,128)(2,1)}), bf16[32,32,512]{2,1,0:T(8,128)(2,1)}, u32[]{:S(2)}, u32[]{:S(2)}) async-start(bf16[32,32,512]{2,1,0:T(8,128)(2,1)} %get-tuple-element.43), calls=%async_computation | async-start | bytes 2097152 | tf_op jit(solution)/shard_map/all_to_all | solution.py:154
  224.7 318.3 %reduce-scatter.4.cloned.1.call-start = ((), (), s32[]{:S(2)}) async-start(), calls=%async_computation.5 | async-start | bytes 2162688
  243.6 23.0 %copy-start.6 = (bf16[8,32,512]{2,1,0:T(8,128)(2,1)}, bf16[8,32,512]{2,1,0:T(8,128)(2,1)S(1)}, u32[]{:S(2)}) copy-start(bf16[8,32,512]{2,1,0:T(8,128)(2,1)S(1)} %broadcast_select_fusion.2) | copy-start | bytes 786436
  248.1 5.4 copy-start.14
  248.2 5.3 copy-start.16
  253.5 1.8 copy-start.15
  253.5 2.1 copy-start.17
  263.7 1.0 copy-start.5
  264.7 0.8 copy-start.8
  264.7 1.0 copy-start.19
  264.9 1.7 copy-start.10
  264.9 1.4 copy-start.18
  266.0 0.7 copy-start.12
  269.7 1.5 copy-start.2
  269.7 1.5 copy-start.9
  269.7 1.9 copy-start.11
  269.8 2.2 copy-start.4
  269.8 2.2 copy-start.13
  271.6 1.0 copy-start.7
  274.6 29.4 %all-to-all-start.2 = ((bf16[32,32,512]{2,1,0:T(8,128)(2,1)}), bf16[32,32,512]{2,1,0:T(8,128)(2,1)S(1)}, u32[]{:S(2)}, u32[]{:S(2)}) async-start(bf16[32,32,512]{2,1,0:T(8,128)(2,1)} %select_select_fusion.2), calls=%async_computation.2 | async-start | bytes 2097152 | tf_op jit(solution)/shard_map/all_to_all | solution.py:176
  280.2 383.1 %all-reduce.3.cloned.1.call-start = ((), (), s32[]{:S(2)}) async-start(), calls=%async_computation.4 | async-start | bytes 1048576 | tf_op jit(solution)/shard_map/psum | solution.py:189
Sparse Core Ops, SparseCore 0:
  269.9 273.0 reduce-scatter.3
  545.4 117.8 all-reduce.2
where the time goes:
time: 675 us; the launch traced here: 674 us
  waiting for transfers between devices  390 us (58%)
  blocking collectives  190 us (28%)
  local copies, waits for them, and re-layouts  24.4 us (4%)
  matrix products  20.2 us (3%)
  other arithmetic  17.7 us (3%)
  starting transfers between devices  17.5 us (3%)
  between operations  14.7 us (2%)
    unnamed x3, waiting for transfers between devices  238 us
    psum x1, waiting for transfers between devices, local(): grad_shard = lax.psum(peer_shard, 'group').astype(jnp.float32)  117 us
    all_gather x1, blocking collectives, local(): lax.all_gather(w_key, 'peer', axis=0, tiled=True)  53.8 us
    all_gather x1, blocking collectives, local(): lax.all_gather(w_out, 'peer', axis=0, tiled=True)  40 us
    all_gather x1, blocking collectives, local(): lax.all_gather(w_query, 'peer', axis=0, tiled=True)  36.8 us
    all_gather x1, blocking collectives, local(): lax.all_gather(w_value, 'peer', axis=0, tiled=True)  36.6 us
    all_to_all x1, waiting for transfers between devices, local(): lax.all_to_all(back_send, 'peer', split_axis=0, concat_axis=0, tiled=True)  22.9 us
    unnamed x1, blocking collectives  22.7 us
  transfers between devices with their start and end apart: 5, of which 4 were waited for; matrix products, arithmetic and copies ran while one was open for 2% of the time, Pallas kernels for 0%

commit v1 on v0

v1 whole, which is shorter than its diff:
```python
import math

import jax
import jax.numpy as jnp
from jax import lax
from jax.sharding import PartitionSpec as P

HEADS = 8


score_gain = 6.0
tiny_eps = 1e-06


def dot_rows(first_op, second_op):
    return lax.dot_general(
        first_op, second_op, (((1,), (1,)), ((), ())), preferred_element_type=jnp.float32
    )


def dot_cols(first_op, second_op):
    return lax.dot_general(
        first_op, second_op, (((0,), (0,)), ((), ())), preferred_element_type=jnp.float32
    )


def unit_heads(values):
    split_heads = values.reshape(values.shape[0], HEADS, values.shape[1] // HEADS)
    inv_scale = lax.rsqrt(jnp.mean(split_heads * split_heads, axis=-1, keepdims=True) + tiny_eps)
    return (split_heads * inv_scale, inv_scale)


def layer_backward(rows, grad_in, weights):
    w_query, w_key, w_value, w_out = weights
    row_count, row_length, feature_width = rows.shape
    token_count = row_count * row_length
    inner_width = w_query.shape[1]
    head_size = inner_width // HEADS
    flat_rows = rows.reshape(token_count, feature_width).astype(jnp.float32)
    inv_rms = lax.rsqrt(jnp.mean(flat_rows * flat_rows, axis=-1, keepdims=True) + tiny_eps)
    scaled = flat_rows * inv_rms
    normed = scaled.astype(jnp.bfloat16)
    queries = jnp.dot(normed, w_query, preferred_element_type=jnp.float32)
    keys_full = jnp.dot(normed, w_key, preferred_element_type=jnp.float32)
    values_full = jnp.dot(normed, w_value, preferred_element_type=jnp.float32)
    q_unit, q_scale = unit_heads(queries)
    k_unit, k_scale = unit_heads(keys_full)
    per_block = math.gcd(row_count, max(1, 128 // row_length))
    block_span = per_block * row_length
    block_count = token_count // block_span
    q_half = q_unit.astype(jnp.bfloat16).reshape(block_count, block_span, HEADS, head_size)
    k_half = k_unit.astype(jnp.bfloat16).reshape(block_count, block_span, HEADS, head_size)
    v_half = values_full.astype(jnp.bfloat16).reshape(block_count, block_span, HEADS, head_size)
    position = lax.iota(jnp.int32, block_span) // row_length
    same_row = position[:, None] == position[None, :]
    scores = jnp.einsum("bqhd,bkhd->bhqk", q_half, k_half, preferred_element_type=jnp.float32) * (
        score_gain / head_size
    )
    exp_scores = jnp.where(same_row, jnp.exp(scores), 0.0)
    att_probs = exp_scores / jnp.sum(exp_scores, axis=-1, keepdims=True)
    probs_half = att_probs.astype(jnp.bfloat16)
    attended = jnp.einsum("bhqk,bkhd->bqhd", probs_half, v_half, preferred_element_type=jnp.float32)
    attended_half = attended.astype(jnp.bfloat16).reshape(token_count, inner_width)
    grad_out = grad_in.reshape(token_count, feature_width)
    grad_att = dot_rows(grad_out, w_out).astype(jnp.bfloat16)
    grad_heads = grad_att.reshape(block_count, block_span, HEADS, head_size)
    grad_probs = jnp.einsum(
        "bqhd,bkhd->bhqk", grad_heads, v_half, preferred_element_type=jnp.float32
    )
    grad_value = jnp.einsum(
        "bhqk,bqhd->bkhd", probs_half, grad_heads, preferred_element_type=jnp.float32
    )
    weighted = jnp.sum(att_probs * grad_probs, axis=-1, keepdims=True)
    grad_scores = (score_gain / head_size * att_probs * (grad_probs - weighted)).astype(
        jnp.bfloat16
    )
    grad_qunit = jnp.einsum(
        "bhqk,bkhd->bqhd", grad_scores, k_half, preferred_element_type=jnp.float32
    ).reshape(token_count, HEADS, head_size)
    grad_kunit = jnp.einsum(
        "bhqk,bqhd->bkhd", grad_scores, q_half, preferred_element_type=jnp.float32
    ).reshape(token_count, HEADS, head_size)
    grad_query = q_scale * (
        grad_qunit - q_unit * jnp.mean(q_unit * grad_qunit, axis=-1, keepdims=True)
    )
    grad_key = k_scale * (
        grad_kunit - k_unit * jnp.mean(k_unit * grad_kunit, axis=-1, keepdims=True)
    )
    dq_half = grad_query.reshape(token_count, inner_width).astype(jnp.bfloat16)
    dk_half = grad_key.reshape(token_count, inner_width).astype(jnp.bfloat16)
    dv_half = grad_value.reshape(token_count, inner_width).astype(jnp.bfloat16)
    grad_norm = dot_rows(dq_half, w_query) + dot_rows(dk_half, w_key) + dot_rows(dv_half, w_value)
    grad_flat = grad_out.astype(jnp.float32) + inv_rms * (
        grad_norm - scaled * jnp.mean(scaled * grad_norm, axis=-1, keepdims=True)
    )
    saved_terms = (normed, attended_half, dq_half, dk_half, dv_half, grad_out)
    return (grad_flat.astype(jnp.bfloat16).reshape(rows.shape), saved_terms)


def grad_terms(saved_terms):
    normed, attended_half, dq_half, dk_half, dv_half, grad_out = saved_terms
    return jnp.concatenate(
        (
            dot_cols(normed, dq_half),
            dot_cols(normed, dk_half),
            dot_cols(normed, dv_half),
            dot_cols(attended_half, grad_out),
        ),
        axis=1,
    )


MESH_AXES = ("y", "core", "x", "z")
swap_pairs = [(0, 1), (1, 0)]


def spread(block, axis):
    count = lax.axis_size(axis)
    copies = jnp.broadcast_to(block[None], (count,) + block.shape)
    return lax.all_to_all(copies, axis, split_axis=0, concat_axis=0, tiled=True)


def shared_sum(blocks, axis):
    arrived = lax.all_to_all(blocks, axis, split_axis=0, concat_axis=0, tiled=True)
    return jnp.sum(arrived.astype(jnp.float32), axis=0)


def gather_weights(w_query, w_key, w_value, w_out, core):
    rows, width = w_query.shape
    both = jnp.stack(
        (
            jnp.concatenate((w_query, w_key), axis=1),
            jnp.concatenate((w_value, w_out), axis=1),
        )
    )
    half = lax.dynamic_index_in_dim(both, core, 0, keepdims=False)
    half = spread(half, "z").reshape(-1, 2 * width)
    half = spread(half, "x").reshape(-1, 2 * width)
    other = lax.ppermute(half, "core", swap_pairs)
    first = jnp.where(core == 0, half, other)
    second = jnp.where(core == 0, other, half)
    return (first[:, :width], first[:, width:], second[:, :width], second[:, width:])


def reduce_terms(first_half, second_half, core):
    mine = jnp.where(core == 0, first_half, second_half)
    theirs = jnp.where(core == 0, second_half, first_half)
    arrived = lax.ppermute(theirs.astype(jnp.bfloat16), "core", swap_pairs)
    total = (mine + arrived.astype(jnp.float32)).astype(jnp.bfloat16)
    depth, width = total.shape
    x_count, z_count = lax.axis_size("x"), lax.axis_size("z")
    total = shared_sum(total.reshape(x_count, depth // x_count, width), "x").astype(jnp.bfloat16)
    rows = depth // (x_count * z_count)
    total = shared_sum(total.reshape(z_count, rows, width), "z").astype(jnp.bfloat16)
    total = jnp.sum(spread(total, "y").astype(jnp.float32), axis=0)
    other = lax.ppermute(total, "core", swap_pairs)
    return (jnp.where(core == 0, total, other), jnp.where(core == 0, other, total))


def local(trace_rows, upstream, counts, w_query, w_key, w_value, w_out):
    core = lax.axis_index("core")
    weights = gather_weights(w_query, w_key, w_value, w_out, core)
    view_count, most_rows, row_length, feature_width = trace_rows.shape
    view_counts = counts.reshape(view_count)
    is_live = lax.iota(jnp.int32, most_rows)[None, :] < view_counts[:, None]
    masked = jnp.where(is_live[:, :, None, None], upstream, jnp.zeros((), upstream.dtype))
    slot_count = view_count * most_rows
    slot_shape = (slot_count, row_length, feature_width)
    done_rows, saved_terms = layer_backward(
        trace_rows.reshape(slot_shape), masked.reshape(slot_shape), weights
    )
    terms = grad_terms(saved_terms)
    first, second = reduce_terms(
        terms[:, : 2 * feature_width], terms[:, 2 * feature_width :], core
    )
    devices = math.prod(lax.axis_size(name) for name in MESH_AXES)
    grad_scale = 1.0 / math.sqrt(devices * (slot_count // 2) * row_length)
    first, second = first * grad_scale, second * grad_scale
    return (
        done_rows.reshape(trace_rows.shape),
        first[:, :feature_width],
        first[:, feature_width:],
        second[:, :feature_width],
        second[:, feature_width:],
    )


def solution(mesh):
    fine_mesh = jax.sharding.Mesh(mesh.devices.reshape(8, 2, 4, 8), MESH_AXES)
    every, peer = P(MESH_AXES), P(("x", "z"), None)
    in_specs = (every, every, P(("y", "core"), ("x", "z")), peer, peer, peer, peer)
    out_specs = (every, peer, peer, peer, peer)
    return jax.shard_map(
        local, mesh=fine_mesh, in_specs=in_specs, out_specs=out_specs, check_vma=False
    )
```

time: 675 us -> 138 us (0.20)
  waiting for transfers between devices: 390 us -> 27.2 us
  blocking collectives: 190 us -> 39 us
  between operations: 14.7 us -> 1.05 us
  starting transfers between devices: 17.5 us -> 28.7 us
  local copies, waits for them, and re-layouts: 24.4 us -> 15.9 us
  other arithmetic: 17.7 us -> 9.3 us
    unnamed x3 -> x0, waiting for transfers between devices: 238 us -> none
    all_gather x4 -> x0, blocking collectives: 167 us -> none  [the longest x1 53.8 us: local(): lax.all_gather(w_key, 'peer', axis=0, tiled=True)]
    psum x1 -> x0, waiting for transfers between devices: 117 us -> none  [local(): grad_shard = lax.psum(peer_shard, 'group').astype(jnp.float32)]
    all_to_all x0 -> x2, blocking collectives: none -> 39 us  [the longest x1 21 us: spread(): return lax.all_to_all(copies, axis, split_axis=0, concat_axis=0, tiled=True)]
    unnamed x1 -> x0, blocking collectives: 22.7 us -> none
    ppermute x0 -> x3, starting transfers between devices: none -> 14.3 us  [the longest x1 5.98 us: reduce_terms(): other = lax.ppermute(total, 'core', swap_pairs)]
    all_to_all x3, waiting for transfers between devices: 33.9 us -> 24.2 us  [the longest x2 18.1 us: spread(): return lax.all_to_all(copies, axis, split_axis=0, concat_axis=0, tiled=True)]
    unnamed x57 -> x36, local copies, waits for them, and re-layouts: 11.2 us -> 2.75 us
  transfers between devices with their start and end apart: 5 -> 6, of which waited for: 4 -> 5; matrix products, arithmetic and copies ran while one was open for 2% -> 8% of each run, Pallas kernels for 0% -> 0%
where the time goes in v1:
time: 138 us
  blocking collectives  39 us (28%)
  starting transfers between devices  28.7 us (21%)
  waiting for transfers between devices  27.2 us (20%)
  matrix products  16.4 us (12%)
  local copies, waits for them, and re-layouts  15.9 us (12%)
  other arithmetic  9.3 us (7%)
    all_to_all x1, blocking collectives, spread(): return lax.all_to_all(copies, axis, split_axis=0, concat_axis=0, tiled=True)  21 us
    all_to_all x2, waiting for transfers between devices, spread(): return lax.all_to_all(copies, axis, split_axis=0, concat_axis=0, tiled=True)  18.1 us
    all_to_all x1, blocking collectives, shared_sum(): lax.all_to_all(blocks, axis, split_axis=0, concat_axis=0, tiled=True)  18 us
    all_to_all x2, starting transfers between devices, spread(): return lax.all_to_all(copies, axis, split_axis=0, concat_axis=0, tiled=True)  11 us
    dot_general x4, matrix products, dot_rows(): lax.dot_general(first_op, second_op, (((1,), (1,)), ((), ())), preferred_...  8.2 us
    all_to_all x1, waiting for transfers between devices, shared_sum(): lax.all_to_all(blocks, axis, split_axis=0, concat_axis=0, tiled=True)  6.1 us
    ppermute x1, starting transfers between devices, reduce_terms(): other = lax.ppermute(total, 'core', swap_pairs)  5.98 us
    ppermute x1, starting transfers between devices, gather_weights(): other = lax.ppermute(half, 'core', swap_pairs)  5.87 us
  transfers between devices with their start and end apart: 6, of which 5 were waited for; matrix products, arithmetic and copies ran while one was open for 8% of the time, Pallas kernels for 0%

profile of v1, /device:TPU:1, one launch (start us, length us, event | category | flops | bytes accessed | tf_op | source)
XLA Modules:
  0.0 137.5 jit_solution(12700246941537576372)
XLA Ops:
  0.6 0.8 maximum_bitcast_fusion
  1.5 21.0 %all_to_all.25 = bf16[8,16,1024]{2,1,0:T(8,128)(2,1)S(1)} all-to-all(bf16[8,16,1024]{2,1,0:T(8,128)(2,1)S(1)} %broadcast_in_dim.33), channel_id=1, replica_groups=mesh['y'=8,'core'=2,'x'=4,'z'=8] {'z'}, dimensions={0} | all-to-all | bytes 524288 | tf_op jit(solution)/shard_map/all_to_all | solution.py:120
  22.7 1.1 broadcast_in_dim.58
  23.8 4.1 %all-to-all-start.1 = ((bf16[4,128,1024]{1,2,0:T(8,128)(2,1)}), bf16[4,128,1024]{1,2,0:T(8,128)(2,1)S(1)}, u32[]{:S(2)}, u32[]{:S(2)}) async-start(bf16[4,128,1024]{1,2,0:T(8,128)(2,1)} %broadcast_in_dim.58), calls=%async_computation.1 | async-start | bytes 2097152 | tf_op jit(solution)/shard_map/all_to_all | solution.py:120
  28.3 11.7 %all-to-all-done.1 = bf16[4,128,1024]{1,2,0:T(8,128)(2,1)S(1)} async-done(((bf16[4,128,1024]{1,2,0:T(8,128)(2,1)}), bf16[4,128,1024]{1,2,0:T(8,128)(2,1)S(1)}, u32[]{:S(2)}, u32[]{:S(2)}) %all-to-all-start.1) | async-done | bytes 1048608 | tf_op jit(solution)/shard_map/all_to_all | solution.py:120
  40.1 5.9 %collective-permute-start = (bf16[512,1024]{0,1:T(8,128)(2,1)S(1)}, bf16[512,1024]{0,1:T(8,128)(2,1)S(1)}, u32[]{:S(2)}, u32[]{:S(2)}) collective-permute-start(bf16[512,1024]{0,1:T(8,128)(2,1)S(1)} %copy_bitcast_fusion), channel_id=1, source_target_pairs={{0,32},{32,0},{1,33},{33,1},{2,34},{34,2},{3,35},{35,3},{4,36},{36... | collective-permute-start | bytes 3145736 | tf_op jit(solution)/shard_map/ppermute | solution.py:139
  46.3 1.0 fusion.12
  47.4 0.9 collective-permute-done
  48.7 0.9 copy-done.11
  49.6 1.2 convolution_convert_fusion.1
  50.9 1.6 %reshape.196 = bf16[4,128,8,64]{3,2,1,0:T(8,128)(2,1)S(1)} reshape(bf16[512,512]{1,0:T(8,128)(2,1)} %convolution_convert_fusion.1) | data formatting | bytes 1048576 | tf_op jit(solution)/shard_map/reshape | solution.py:66
  52.5 1.4 %copy.96 = bf16[4,128,8,64]{1,3,2,0:T(8,128)(2,1)} copy(bf16[4,128,8,64]{3,2,1,0:T(8,128)(2,1)S(1)} %reshape.196) | data formatting | bytes 1048576 | tf_op jit(solution)/shard_map/reshape | solution.py:66
  54.0 0.5 multiply_reduce_fusion.3
  54.5 0.5 multiply_reduce_fusion.2
  55.0 0.7 copy-done.12
  55.8 1.3 convolution_convert_fusion
  57.1 2.4 %reshape.197 = bf16[4,128,8,64]{3,2,1,0:T(8,128)(2,1)} reshape(bf16[512,512]{1,0:T(8,128)(2,1)} %convolution_convert_fusion) | data formatting | bytes 1048576 | tf_op jit(solution)/shard_map/reshape | solution.py:53
  59.5 2.5 %copy.97 = bf16[4,128,8,64]{1,3,2,0:T(8,128)(2,1)} copy(bf16[4,128,8,64]{3,2,1,0:T(8,128)(2,1)} %reshape.197) | data formatting | bytes 1048576 | tf_op jit(solution)/shard_map/reshape | solution.py:53
  62.0 0.7 fusion.1
  63.0 0.8 fusion.3
  64.1 0.8 multiply_reduce_fusion
  64.8 0.8 multiply_convert_fusion
  65.6 0.8 convolution_bitcast_fusion
  66.4 0.4 convolution_bitcast_fusion.1
  66.9 0.7 fusion.4
  67.5 0.4 copy.106
  69.7 0.5 fusion.15
  70.2 0.4 fusion.18
  70.7 0.4 fusion.49
  71.1 0.4 fusion.48
  71.5 0.5 select_convert_fusion
  72.1 2.5 %collective-permute-start.1 = (bf16[512,1024]{0,1:T(8,128)(2,1)S(1)}, bf16[512,1024]{0,1:T(8,128)(2,1)S(1)}, u32[]{:S(2)}, u32[]{:S(2)}) collective-permute-start(bf16[512,1024]{0,1:T(8,128)(2,1)S(1)} %select_convert_fusion), channel_id=1, source_target_pairs={{0,32},{32,0},{1,33},{33,1},{2,34},{34,2},{3,35},{35,3},{4,36},{36... | collective-permute-start | bytes 3145736 | tf_op jit(solution)/shard_map/ppermute | solution.py:148
  74.6 2.1 %collective-permute-done.1 = bf16[512,1024]{0,1:T(8,128)(2,1)S(1)} collective-permute-done((bf16[512,1024]{0,1:T(8,128)(2,1)S(1)}, bf16[512,1024]{0,1:T(8,128)(2,1)S(1)}, u32[]{:S(2)}, u32[]{:S(2)}) %collective-permute-start.1) | collective-permute-done | bytes 1048608 | tf_op jit(solution)/shard_map/ppermute | solution.py:148
  76.9 18.0 %all_to_all.26 = bf16[4,128,1024]{1,2,0:T(8,128)(2,1)} all-to-all(bf16[4,128,1024]{1,2,0:T(8,128)(2,1)S(1)} %copy_bitcast_fusion.1), channel_id=1, replica_groups=mesh['y'=8,'core'=2,'x'=4,'z'=8] {'x'}, dimensions={0} | all-to-all | bytes 2097152 | tf_op jit(solution)/shard_map/all_to_all | solution.py:124
  94.9 1.6 %reduce_sum.113 = bf16[128,1024]{0,1:T(8,128)(2,1)S(1)} reduce(bf16[4,128,1024]{1,2,0:T(8,128)(2,1)} %all_to_all.26, bf16[]{:T(256)} %constant.40.clone.1), dimensions={0}, to_apply=%region_8.9 | reduce | flops 393216 | bytes 1310722 | tf_op jit(solution)/shard_map/reduce_sum | solution.py:125
  96.6 0.8 copy.112
  97.4 3.4 %all-to-all-start.3 = ((bf16[8,16,1024]{2,1,0:T(8,128)(2,1)}), bf16[8,16,1024]{2,1,0:T(8,128)(2,1)S(1)}, u32[]{:S(2)}, u32[]{:S(2)}) async-start(bf16[8,16,1024]{2,1,0:T(8,128)(2,1)} %bitcast.153), calls=%async_computation.3 | async-start | bytes 524288 | tf_op jit(solution)/shard_map/all_to_all | solution.py:124
  100.8 2.5 %fusion.20 = f32[512,512]{1,0:T(8,128)} fusion(bf16[64,8,4,128]{3,2,1,0:T(4,128)(2,1)S(1)} %bitcast.151, bf16[512,1024]{0,1:T(8,128)(2,1)} %copy-done.11), kind=kOutput, calls=%fused_computation.51 | convolution fusion | flops 268435456 | bytes 2097152 | tf_op jit(solution)/shard_map/dot_general | solution.py:16
  103.3 1.4 %fusion.40 = f32[512,512]{1,0:T(8,128)} fusion(bf16[512,512]{0,1:T(8,128)(2,1)S(1)} %bitcast.145, bf16[512,1024]{0,1:T(8,128)(2,1)S(1)} %copy-done.2), kind=kOutput, calls=%fused_computation.91 | convolution fusion | flops 268435456 | bytes 2097152 | tf_op jit(solution)/shard_map/dot_general | solution.py:16
  104.8 6.1 %all-to-all-done.3 = bf16[8,16,1024]{2,1,0:T(8,128)(2,1)S(1)} async-done(((bf16[8,16,1024]{2,1,0:T(8,128)(2,1)}), bf16[8,16,1024]{2,1,0:T(8,128)(2,1)S(1)}, u32[]{:S(2)}, u32[]{:S(2)}) %all-to-all-start.3) | async-done | bytes 262176 | tf_op jit(solution)/shard_map/all_to_all | solution.py:124
  110.9 0.7 broadcast_in_dim.61
  111.6 6.8 %all-to-all-start.4 = ((bf16[8,16,1024]{2,1,0:T(8,128)(2,1)}), bf16[8,16,1024]{2,1,0:T(8,128)(2,1)S(1)}, u32[]{:S(2)}, u32[]{:S(2)}) async-start(bf16[8,16,1024]{2,1,0:T(8,128)(2,1)} %broadcast_in_dim.61), calls=%async_computation.4 | async-start | bytes 524288 | tf_op jit(solution)/shard_map/all_to_all | solution.py:120
  118.5 3.0 %multiply_reduce_fusion.1 = (f32[512]{0:T(512)S(1)}, f32[512,512]{1,0:T(8,128)}) fusion(bf16[2,8,32,512]{3,2,1,0:T(8,128)(2,1)S(1)} %copy-done, f32[512]{0:T(512)S(1)} %rsqrt.29, f32[512,512]{1,0:T(8,128)} %fusion.20, f32[512,512]{1,0:T(8,128)} %fusion.40, bf16[512,512]{0,1:T(8,128)(2,1)S(1)} %bitcast.147, bf16[512,1024]{0,1:T(8,128)(2,1)S(1)} %copy-done.2), kind=kOutput, calls=%fused_computation.34 | convolution fusion | flops 270007808 | bytes 4722688 | tf_op jit(solution)/shard_map/dot_general | solution.py:16
  121.5 6.3 %all-to-all-done.4 = bf16[8,16,1024]{2,1,0:T(8,128)(2,1)S(1)} async-done(((bf16[8,16,1024]{2,1,0:T(8,128)(2,1)}), bf16[8,16,1024]{2,1,0:T(8,128)(2,1)S(1)}, u32[]{:S(2)}, u32[]{:S(2)}) %all-to-all-start.4) | async-done | bytes 262176 | tf_op jit(solution)/shard_map/all_to_all | solution.py:120
  127.9 6.0 %collective-permute-start.2 = (f32[16,1024]{1,0:T(8,128)S(1)}, f32[16,1024]{1,0:T(8,128)S(1)}, u32[]{:S(2)}, u32[]{:S(2)}) collective-permute-start(f32[16,1024]{1,0:T(8,128)S(1)} %convert_reduce_fusion), channel_id=1, source_target_pairs={{0,32},{32,0},{1,33},{33,1},{2,34},{34,2},{3,35},{35,3},{4,36},{36... | collective-permute-start | bytes 196616 | tf_op jit(solution)/shard_map/ppermute | solution.py:156
  133.9 2.3 %add_convert_fusion.1 = bf16[512,512]{1,0:T(8,128)(2,1)} fusion(f32[512,512]{1,0:T(8,128)} %get-tuple-element.24, bf16[2,8,32,512]{3,2,1,0:T(8,128)(2,1)S(1)} %copy-done, f32[512]{0:T(512)S(1)} %broadcast_multiply_fusion.2, f32[512]{0:T(512)S(1)} %rsqrt.29, bf16[2,8,32,512]{3,2,1,0:T(8,128)(2,1)S(1)} %copy-done.4), kind=kLoop, calls=%fused_computation.33 | loop fusion | flops 2097152 | bytes 2625536 | tf_op jit(solution)/shard_map/convert_element_type | solution.py:97
  136.2 0.6 fusion.47
  136.9 0.6 fusion.46
  (63 shorter events, 4.3 us)
Async XLA Ops:
  22.5 5.4 %copy-start = (bf16[2,8,32,512]{3,2,1,0:T(8,128)(2,1)S(1)}, bf16[2,8,32,512]{3,2,1,0:T(8,128)(2,1)}, u32[]{:S(2)}) copy-start(bf16[2,8,32,512]{3,2,1,0:T(8,128)(2,1)} %param.7) | copy-start | bytes 1572868
  22.7 5.5 %copy-start.17 = (s32[1,2]{1,0:T(1,128)S(1)}, s32[1,2]{1,0:T(1,128)}, u32[]{:S(2)}) copy-start(s32[1,2]{1,0:T(1,128)} %param.9) | copy-start | bytes 28
  23.8 22.3 %copy-start.16 = (bf16[2,8,32,512]{3,2,1,0:T(8,128)(2,1)S(1)}, bf16[2,8,32,512]{3,2,1,0:T(8,128)(2,1)}, u32[]{:S(2)}) copy-start(bf16[2,8,32,512]{3,2,1,0:T(8,128)(2,1)} %param.8) | copy-start | bytes 1572868
  23.8 16.2 %all-to-all-start.1 = ((bf16[4,128,1024]{1,2,0:T(8,128)(2,1)}), bf16[4,128,1024]{1,2,0:T(8,128)(2,1)S(1)}, u32[]{:S(2)}, u32[]{:S(2)}) async-start(bf16[4,128,1024]{1,2,0:T(8,128)(2,1)} %broadcast_in_dim.58), calls=%async_computation.1 | async-start | bytes 2097152 | tf_op jit(solution)/shard_map/all_to_all | solution.py:120
  40.1 8.1 %collective-permute-start = (bf16[512,1024]{0,1:T(8,128)(2,1)S(1)}, bf16[512,1024]{0,1:T(8,128)(2,1)S(1)}, u32[]{:S(2)}, u32[]{:S(2)}) collective-permute-start(bf16[512,1024]{0,1:T(8,128)(2,1)S(1)} %copy_bitcast_fusion), channel_id=1, source_target_pairs={{0,32},{32,0},{1,33},{33,1},{2,34},{34,2},{3,35},{35,3},{4,36},{36... | collective-permute-start | bytes 3145736 | tf_op jit(solution)/shard_map/ppermute | solution.py:139
  46.2 2.4 %copy-start.3 = (bf16[2,8,32,512]{3,2,1,0:T(8,128)(2,1)}, bf16[2,8,32,512]{3,2,1,0:T(8,128)(2,1)S(1)}, u32[]{:S(2)}) copy-start(bf16[2,8,32,512]{3,2,1,0:T(8,128)(2,1)S(1)} %broadcast_select_fusion.2) | copy-start | bytes 1572868
  48.7 1.0 copy-start.11
  48.7 5.2 %copy-start.1 = (bf16[512,1024]{0,1:T(8,128)(2,1)}, bf16[512,1024]{0,1:T(8,128)(2,1)S(1)}, u32[]{:S(2)}) copy-start(bf16[512,1024]{0,1:T(8,128)(2,1)S(1)} %get-tuple-element.5) | copy-start | bytes 3145732
  54.5 1.2 copy-start.12
  54.5 1.3 copy-start.15
  62.0 1.0 copy-start.13
  63.0 1.0 copy-start.14
  68.0 2.2 %copy-start.9 = (bf16[4,128,8,64]{1,0,3,2:T(4,128)(2,1)}, bf16[4,128,8,64]{1,0,3,2:T(4,128)(2,1)S(1)}, u32[]{:S(2)}) copy-start(bf16[4,128,8,64]{1,0,3,2:T(4,128)(2,1)S(1)} %copy.106) | copy-start | bytes 1572868
  68.4 2.2 %copy-start.5 = (bf16[512,8,64]{0,2,1:T(8,128)(2,1)}, bf16[512,8,64]{0,2,1:T(8,128)(2,1)S(1)}, u32[]{:S(2)}) copy-start(bf16[512,8,64]{0,2,1:T(8,128)(2,1)S(1)} %fusion.8) | copy-start | bytes 1572868
  68.7 1.0 copy-start.4
  68.9 2.2 %copy-start.7 = (bf16[512,8,64]{0,2,1:T(8,128)(2,1)}, bf16[512,8,64]{0,2,1:T(8,128)(2,1)S(1)}, u32[]{:S(2)}) copy-start(bf16[512,8,64]{0,2,1:T(8,128)(2,1)S(1)} %fusion.11) | copy-start | bytes 1572868
  72.1 4.6 %collective-permute-start.1 = (bf16[512,1024]{0,1:T(8,128)(2,1)S(1)}, bf16[512,1024]{0,1:T(8,128)(2,1)S(1)}, u32[]{:S(2)}, u32[]{:S(2)}) collective-permute-start(bf16[512,1024]{0,1:T(8,128)(2,1)S(1)} %select_convert_fusion), channel_id=1, source_target_pairs={{0,32},{32,0},{1,33},{33,1},{2,34},{34,2},{3,35},{35,3},{4,36},{36... | collective-permute-start | bytes 3145736 | tf_op jit(solution)/shard_map/ppermute | solution.py:148
  94.9 5.9 %copy-start.10 = (bf16[4,128,8,64]{1,0,3,2:T(4,128)(2,1)S(1)}, bf16[4,128,8,64]{1,0,3,2:T(4,128)(2,1)}, u32[]{:S(2)}) copy-start(bf16[4,128,8,64]{1,0,3,2:T(4,128)(2,1)} %copy-done.9) | copy-start | bytes 1572868
  94.9 8.4 %copy-start.2 = (bf16[512,1024]{0,1:T(8,128)(2,1)S(1)}, bf16[512,1024]{0,1:T(8,128)(2,1)}, u32[]{:S(2)}) copy-start(bf16[512,1024]{0,1:T(8,128)(2,1)} %copy-done.1) | copy-start | bytes 3145732
  94.9 8.4 %copy-start.6 = (bf16[512,8,64]{0,2,1:T(8,128)(2,1)S(1)}, bf16[512,8,64]{0,2,1:T(8,128)(2,1)}, u32[]{:S(2)}) copy-start(bf16[512,8,64]{0,2,1:T(8,128)(2,1)} %copy-done.5) | copy-start | bytes 1572868
  97.4 13.5 %all-to-all-start.3 = ((bf16[8,16,1024]{2,1,0:T(8,128)(2,1)}), bf16[8,16,1024]{2,1,0:T(8,128)(2,1)S(1)}, u32[]{:S(2)}, u32[]{:S(2)}) async-start(bf16[8,16,1024]{2,1,0:T(8,128)(2,1)} %bitcast.153), calls=%async_computation.3 | async-start | bytes 524288 | tf_op jit(solution)/shard_map/all_to_all | solution.py:124
  103.3 15.1 %copy-start.8 = (bf16[512,8,64]{0,2,1:T(8,128)(2,1)S(1)}, bf16[512,8,64]{0,2,1:T(8,128)(2,1)}, u32[]{:S(2)}) copy-start(bf16[512,8,64]{0,2,1:T(8,128)(2,1)} %copy-done.7) | copy-start | bytes 1572868
  111.6 16.2 %all-to-all-start.4 = ((bf16[8,16,1024]{2,1,0:T(8,128)(2,1)}), bf16[8,16,1024]{2,1,0:T(8,128)(2,1)S(1)}, u32[]{:S(2)}, u32[]{:S(2)}) async-start(bf16[8,16,1024]{2,1,0:T(8,128)(2,1)} %broadcast_in_dim.61), calls=%async_computation.4 | async-start | bytes 524288 | tf_op jit(solution)/shard_map/all_to_all | solution.py:120
  127.9 8.3 %collective-permute-start.2 = (f32[16,1024]{1,0:T(8,128)S(1)}, f32[16,1024]{1,0:T(8,128)S(1)}, u32[]{:S(2)}, u32[]{:S(2)}) collective-permute-start(f32[16,1024]{1,0:T(8,128)S(1)} %convert_reduce_fusion), channel_id=1, source_target_pairs={{0,32},{32,0},{1,33},{33,1},{2,34},{34,2},{3,35},{35,3},{4,36},{36... | collective-permute-start | bytes 196616 | tf_op jit(solution)/shard_map/ppermute | solution.py:156

commit v2 on v1

--- a/solution.py
+++ b/solution.py
@@ -134,8 +134,7 @@
         )
     )
     half = lax.dynamic_index_in_dim(both, core, 0, keepdims=False)
-    half = spread(half, "z").reshape(-1, 2 * width)
-    half = spread(half, "x").reshape(-1, 2 * width)
+    half = spread(half, ("x", "z")).reshape(-1, 2 * width)
     other = lax.ppermute(half, "core", swap_pairs)
     first = jnp.where(core == 0, half, other)
     second = jnp.where(core == 0, other, half)
@@ -148,11 +147,9 @@
     arrived = lax.ppermute(theirs.astype(jnp.bfloat16), "core", swap_pairs)
     total = (mine + arrived.astype(jnp.float32)).astype(jnp.bfloat16)
     depth, width = total.shape
-    x_count, z_count = lax.axis_size("x"), lax.axis_size("z")
-    total = shared_sum(total.reshape(x_count, depth // x_count, width), "x").astype(jnp.bfloat16)
-    rows = depth // (x_count * z_count)
-    total = shared_sum(total.reshape(z_count, rows, width), "z").astype(jnp.bfloat16)
-    total = jnp.sum(spread(total, "y").astype(jnp.float32), axis=0)
+    peers = lax.axis_size(("x", "z"))
+    total = shared_sum(total.reshape(peers, depth // peers, width), ("x", "z"))
+    total = jnp.sum(spread(total.astype(jnp.bfloat16), "y").astype(jnp.float32), axis=0)
     other = lax.ppermute(total, "core", swap_pairs)
     return (jnp.where(core == 0, total, other), jnp.where(core == 0, other, total))
 

time: 138 us -> 143 us (1.036)
  blocking collectives: 39 us -> 0 us
  waiting for transfers between devices: 27.2 us -> 54.9 us
  starting transfers between devices: 28.7 us -> 42.7 us
    all_to_all x2 -> x0, blocking collectives: 39 us -> none  [the longest x1 21 us: spread(): return lax.all_to_all(copies, axis, split_axis=0, concat_axis=0, tiled=True)]
    all_to_all x1, waiting for transfers between devices: 6.1 us -> 21.2 us  [shared_sum(): lax.all_to_all(blocks, axis, split_axis=0, concat_axis=0, tiled=True)]
    all_to_all x2, waiting for transfers between devices: 18.1 us -> 30.7 us  [spread(): return lax.all_to_all(copies, axis, split_axis=0, concat_axis=0, tiled=True)]
    all_to_all x2, starting transfers between devices: 11 us -> 20.7 us  [spread(): return lax.all_to_all(copies, axis, split_axis=0, concat_axis=0, tiled=True)]
    all_to_all x1, starting transfers between devices: 3.41 us -> 5.05 us  [shared_sum(): lax.all_to_all(blocks, axis, split_axis=0, concat_axis=0, tiled=True)]
    ppermute x1, starting transfers between devices: 5.98 us -> 7.59 us  [reduce_terms(): other = lax.ppermute(total, 'core', swap_pairs)]
where the time goes in v2:
time: 143 us; the launch traced here: 142 us
  waiting for transfers between devices  54.9 us (38%)
  starting transfers between devices  42.7 us (30%)
  local copies, waits for them, and re-layouts  16.5 us (12%)
  matrix products  16.4 us (11%)
  other arithmetic  10.4 us (7%)
    all_to_all x2, waiting for transfers between devices, spread(): return lax.all_to_all(copies, axis, split_axis=0, concat_axis=0, tiled=True)  30.7 us
    all_to_all x1, waiting for transfers between devices, shared_sum(): lax.all_to_all(blocks, axis, split_axis=0, concat_axis=0, tiled=True)  21.2 us
    all_to_all x2, starting transfers between devices, spread(): return lax.all_to_all(copies, axis, split_axis=0, concat_axis=0, tiled=True)  20.7 us
    dot_general x4, matrix products, dot_rows(): lax.dot_general(first_op, second_op, (((1,), (1,)), ((), ())), preferred_...  8.18 us
    ppermute x1, starting transfers between devices, reduce_terms(): other = lax.ppermute(total, 'core', swap_pairs)  7.59 us
    ppermute x1, starting transfers between devices, gather_weights(): other = lax.ppermute(half, 'core', swap_pairs)  6.88 us
    all_to_all x1, starting transfers between devices, shared_sum(): lax.all_to_all(blocks, axis, split_axis=0, concat_axis=0, tiled=True)  5.05 us
    reshape x2, local copies, waits for them, and re-layouts, layer_backward(): values_full.astype(jnp.bfloat16)  4.86 us
  transfers between devices with their start and end apart: 6, of which 5 were waited for; matrix products, arithmetic and copies ran while one was open for 8% of the time, Pallas kernels for 0%

profile of v2, /device:TPU:1, one launch (start us, length us, event | category | flops | bytes accessed | tf_op | source)
XLA Modules:
  0.0 141.9 jit_solution(2268821196563613713)
XLA Ops:
  0.7 0.8 maximum_bitcast_fusion
  1.5 1.1 broadcast_in_dim.29
  2.6 13.8 %all-to-all-start = ((bf16[32,16,1024]{2,1,0:T(8,128)(2,1)}), bf16[32,16,1024]{2,1,0:T(8,128)(2,1)S(1)}, u32[]{:S(2)}, u32[]{:S(2)}) async-start(bf16[32,16,1024]{2,1,0:T(8,128)(2,1)} %broadcast_in_dim.29), calls=%async_computation | async-start | bytes 2097152 | tf_op jit(solution)/shard_map/all_to_all | solution.py:120
  16.8 24.3 %all-to-all-done = bf16[32,16,1024]{2,1,0:T(8,128)(2,1)S(1)} async-done(((bf16[32,16,1024]{2,1,0:T(8,128)(2,1)}), bf16[32,16,1024]{2,1,0:T(8,128)(2,1)S(1)}, u32[]{:S(2)}, u32[]{:S(2)}) %all-to-all-start) | async-done | bytes 1048608 | tf_op jit(solution)/shard_map/all_to_all | solution.py:120
  41.1 0.5 copy.49
  41.6 6.9 %collective-permute-start = (bf16[512,1024]{0,1:T(8,128)(2,1)S(1)}, bf16[512,1024]{0,1:T(8,128)(2,1)S(1)}, u32[]{:S(2)}, u32[]{:S(2)}) collective-permute-start(bf16[512,1024]{0,1:T(8,128)(2,1)S(1)} %copy.49), channel_id=1, source_target_pairs={{0,32},{32,0},{1,33},{33,1},{2,34},{34,2},{3,35},{35,3},{4,36},{36... | collective-permute-start | bytes 3145736 | tf_op jit(solution)/shard_map/ppermute | solution.py:138
  48.8 1.0 fusion.11
  49.9 0.9 collective-permute-done
  50.8 1.4 broadcast_select_fusion.1
  52.2 0.9 copy-done.12
  53.1 1.2 convolution_convert_fusion.1
  54.3 1.6 %reshape.191 = bf16[4,128,8,64]{3,2,1,0:T(8,128)(2,1)S(1)} reshape(bf16[512,512]{1,0:T(8,128)(2,1)} %convolution_convert_fusion.1) | data formatting | bytes 1048576 | tf_op jit(solution)/shard_map/reshape | solution.py:66
  56.0 1.4 copy.55
  57.5 0.5 multiply_reduce_fusion.3
  58.0 0.5 multiply_reduce_fusion.2
  58.5 0.7 copy-done.13
  59.3 1.3 convolution_convert_fusion
  60.6 2.4 %reshape.192 = bf16[4,128,8,64]{3,2,1,0:T(8,128)(2,1)} reshape(bf16[512,512]{1,0:T(8,128)(2,1)} %convolution_convert_fusion) | data formatting | bytes 1048576 | tf_op jit(solution)/shard_map/reshape | solution.py:53
  62.9 2.5 %copy.56 = bf16[4,128,8,64]{1,3,2,0:T(8,128)(2,1)} copy(bf16[4,128,8,64]{3,2,1,0:T(8,128)(2,1)} %reshape.192) | data formatting | bytes 1048576 | tf_op jit(solution)/shard_map/reshape | solution.py:53
  65.4 0.7 fusion.1
  66.5 0.8 fusion.3
  67.5 0.8 multiply_reduce_fusion
  68.3 0.7 multiply_convert_fusion
  69.0 0.8 convolution_bitcast_fusion
  69.9 0.4 convolution_bitcast_fusion.1
  70.3 0.7 fusion.4
  73.1 0.5 fusion.14
  73.6 0.4 fusion.17
  74.1 0.4 fusion.48
  74.5 0.4 fusion.47
  75.0 0.5 select_convert_fusion
  75.5 2.5 %collective-permute-start.1 = (bf16[512,1024]{0,1:T(8,128)(2,1)S(1)}, bf16[512,1024]{0,1:T(8,128)(2,1)S(1)}, u32[]{:S(2)}, u32[]{:S(2)}) collective-permute-start(bf16[512,1024]{0,1:T(8,128)(2,1)S(1)} %select_convert_fusion), channel_id=1, source_target_pairs={{0,32},{32,0},{1,33},{33,1},{2,34},{34,2},{3,35},{35,3},{4,36},{36... | collective-permute-start | bytes 3145736 | tf_op jit(solution)/shard_map/ppermute | solution.py:147
  78.0 2.1 %collective-permute-done.1 = bf16[512,1024]{0,1:T(8,128)(2,1)S(1)} collective-permute-done((bf16[512,1024]{0,1:T(8,128)(2,1)S(1)}, bf16[512,1024]{0,1:T(8,128)(2,1)S(1)}, u32[]{:S(2)}, u32[]{:S(2)}) %collective-permute-start.1) | collective-permute-done | bytes 1048608 | tf_op jit(solution)/shard_map/ppermute | solution.py:147
  80.1 0.6 add_convert_fusion
  80.7 1.3 copy.69
  82.0 5.1 %all-to-all-start.1 = ((bf16[32,16,1024]{2,1,0:T(8,128)(2,1)}), bf16[32,16,1024]{2,1,0:T(8,128)(2,1)}, u32[]{:S(2)}, u32[]{:S(2)}) async-start(bf16[32,16,1024]{2,1,0:T(8,128)(2,1)} %bitcast.133), calls=%async_computation.1 | async-start | bytes 2097152 | tf_op jit(solution)/shard_map/all_to_all | solution.py:124
  87.1 2.5 %fusion.19 = f32[512,512]{1,0:T(8,128)} fusion(bf16[64,8,4,128]{3,2,1,0:T(4,128)(2,1)S(1)} %bitcast.137, bf16[512,1024]{0,1:T(8,128)(2,1)} %copy-done.12), kind=kOutput, calls=%fused_computation.48 | convolution fusion | flops 268435456 | bytes 2097152 | tf_op jit(solution)/shard_map/dot_general | solution.py:16
  89.6 1.4 %fusion.39 = f32[512,512]{1,0:T(8,128)} fusion(bf16[512,512]{0,1:T(8,128)(2,1)S(1)} %bitcast.129, bf16[512,1024]{0,1:T(8,128)(2,1)S(1)} %copy-done.2), kind=kOutput, calls=%fused_computation.88 | convolution fusion | flops 268435456 | bytes 2097152 | tf_op jit(solution)/shard_map/dot_general | solution.py:16
  91.0 21.2 %all-to-all-done.1 = bf16[32,16,1024]{2,1,0:T(8,128)(2,1)} async-done(((bf16[32,16,1024]{2,1,0:T(8,128)(2,1)}), bf16[32,16,1024]{2,1,0:T(8,128)(2,1)}, u32[]{:S(2)}, u32[]{:S(2)}) %all-to-all-start.1) | async-done | bytes 1048608 | tf_op jit(solution)/shard_map/all_to_all | solution.py:124
  112.3 1.4 reduce_sum.101
  113.6 0.7 broadcast_in_dim.52
  114.4 6.8 %all-to-all-start.2 = ((bf16[8,16,1024]{2,1,0:T(8,128)(2,1)}), bf16[8,16,1024]{2,1,0:T(8,128)(2,1)S(1)}, u32[]{:S(2)}, u32[]{:S(2)}) async-start(bf16[8,16,1024]{2,1,0:T(8,128)(2,1)} %broadcast_in_dim.52), calls=%async_computation.2 | async-start | bytes 524288 | tf_op jit(solution)/shard_map/all_to_all | solution.py:120
  121.2 3.0 %multiply_reduce_fusion.1 = (f32[512]{0:T(512)S(1)}, f32[512,512]{1,0:T(8,128)}) fusion(bf16[2,8,32,512]{3,2,1,0:T(8,128)(2,1)S(1)} %copy-done, f32[512]{0:T(512)S(1)} %rsqrt.29, f32[512,512]{1,0:T(8,128)} %fusion.19, f32[512,512]{1,0:T(8,128)} %fusion.39, bf16[512,512]{0,1:T(8,128)(2,1)S(1)} %bitcast.131, bf16[512,1024]{0,1:T(8,128)(2,1)S(1)} %copy-done.2), kind=kOutput, calls=%fused_computation.31 | convolution fusion | flops 270007808 | bytes 4722688 | tf_op jit(solution)/shard_map/dot_general | solution.py:16
  124.2 6.4 %all-to-all-done.2 = bf16[8,16,1024]{2,1,0:T(8,128)(2,1)S(1)} async-done(((bf16[8,16,1024]{2,1,0:T(8,128)(2,1)}), bf16[8,16,1024]{2,1,0:T(8,128)(2,1)S(1)}, u32[]{:S(2)}, u32[]{:S(2)}) %all-to-all-start.2) | async-done | bytes 262176 | tf_op jit(solution)/shard_map/all_to_all | solution.py:120
  130.7 7.6 %collective-permute-start.2 = (f32[16,1024]{1,0:T(8,128)S(1)}, f32[16,1024]{1,0:T(8,128)S(1)}, u32[]{:S(2)}, u32[]{:S(2)}) collective-permute-start(f32[16,1024]{1,0:T(8,128)S(1)} %convert_reduce_fusion), channel_id=1, source_target_pairs={{0,32},{32,0},{1,33},{33,1},{2,34},{34,2},{3,35},{35,3},{4,36},{36... | collective-permute-start | bytes 196616 | tf_op jit(solution)/shard_map/ppermute | solution.py:153
  138.3 2.3 %add_convert_fusion.1 = bf16[512,512]{1,0:T(8,128)(2,1)} fusion(f32[512,512]{1,0:T(8,128)} %get-tuple-element.24, bf16[2,8,32,512]{3,2,1,0:T(8,128)(2,1)S(1)} %copy-done, f32[512]{0:T(512)S(1)} %broadcast_multiply_fusion.2, f32[512]{0:T(512)S(1)} %rsqrt.29, bf16[2,8,32,512]{3,2,1,0:T(8,128)(2,1)S(1)} %copy-done.4), kind=kLoop, calls=%fused_computation.30 | loop fusion | flops 2097152 | bytes 2625536 | tf_op jit(solution)/shard_map/convert_element_type | solution.py:97
  140.6 0.6 fusion.46
  141.3 0.6 fusion.45
  (60 shorter events, 3.7 us)
Async XLA Ops:
  0.6 15.8 %copy-start = (bf16[2,8,32,512]{3,2,1,0:T(8,128)(2,1)S(1)}, bf16[2,8,32,512]{3,2,1,0:T(8,128)(2,1)}, u32[]{:S(2)}) copy-start(bf16[2,8,32,512]{3,2,1,0:T(8,128)(2,1)} %param.7) | copy-start | bytes 1572868
  0.6 16.1 %copy-start.18 = (s32[1,2]{1,0:T(1,128)S(1)}, s32[1,2]{1,0:T(1,128)}, u32[]{:S(2)}) copy-start(s32[1,2]{1,0:T(1,128)} %param.9) | copy-start | bytes 28
  2.6 46.0 %copy-start.17 = (bf16[2,8,32,512]{3,2,1,0:T(8,128)(2,1)S(1)}, bf16[2,8,32,512]{3,2,1,0:T(8,128)(2,1)}, u32[]{:S(2)}) copy-start(bf16[2,8,32,512]{3,2,1,0:T(8,128)(2,1)} %param.8) | copy-start | bytes 1572868
  2.6 38.5 %all-to-all-start = ((bf16[32,16,1024]{2,1,0:T(8,128)(2,1)}), bf16[32,16,1024]{2,1,0:T(8,128)(2,1)S(1)}, u32[]{:S(2)}, u32[]{:S(2)}) async-start(bf16[32,16,1024]{2,1,0:T(8,128)(2,1)} %broadcast_in_dim.29), calls=%async_computation | async-start | bytes 2097152 | tf_op jit(solution)/shard_map/all_to_all | solution.py:120
  41.6 8.3 %copy-start.9 = (bf16[512,1024]{0,1:T(8,128)(2,1)}, bf16[512,1024]{0,1:T(8,128)(2,1)S(1)}, u32[]{:S(2)}) copy-start(bf16[512,1024]{0,1:T(8,128)(2,1)S(1)} %copy.49) | copy-start | bytes 3145732
  41.6 9.2 %collective-permute-start = (bf16[512,1024]{0,1:T(8,128)(2,1)S(1)}, bf16[512,1024]{0,1:T(8,128)(2,1)S(1)}, u32[]{:S(2)}, u32[]{:S(2)}) collective-permute-start(bf16[512,1024]{0,1:T(8,128)(2,1)S(1)} %copy.49), channel_id=1, source_target_pairs={{0,32},{32,0},{1,33},{33,1},{2,34},{34,2},{3,35},{35,3},{4,36},{36... | collective-permute-start | bytes 3145736 | tf_op jit(solution)/shard_map/ppermute | solution.py:138
  48.7 3.4 %copy-start.3 = (bf16[2,8,32,512]{3,2,1,0:T(8,128)(2,1)}, bf16[2,8,32,512]{3,2,1,0:T(8,128)(2,1)S(1)}, u32[]{:S(2)}) copy-start(bf16[2,8,32,512]{3,2,1,0:T(8,128)(2,1)S(1)} %broadcast_select_fusion.2) | copy-start | bytes 1572868
  52.2 1.0 copy-start.12
  52.2 5.2 %copy-start.1 = (bf16[512,1024]{0,1:T(8,128)(2,1)}, bf16[512,1024]{0,1:T(8,128)(2,1)S(1)}, u32[]{:S(2)}) copy-start(bf16[512,1024]{0,1:T(8,128)(2,1)S(1)} %get-tuple-element.5) | copy-start | bytes 3145732
  57.9 1.2 copy-start.13
  58.0 1.3 copy-start.16
  65.4 1.0 copy-start.14
  66.5 1.0 copy-start.15
  71.4 2.2 %copy-start.10 = (bf16[4,128,8,64]{1,0,3,2:T(4,128)(2,1)}, bf16[4,128,8,64]{1,0,3,2:T(4,128)(2,1)S(1)}, u32[]{:S(2)}) copy-start(bf16[4,128,8,64]{1,0,3,2:T(4,128)(2,1)S(1)} %copy.65) | copy-start | bytes 1572868
  71.8 2.2 %copy-start.5 = (bf16[512,8,64]{0,2,1:T(8,128)(2,1)}, bf16[512,8,64]{0,2,1:T(8,128)(2,1)S(1)}, u32[]{:S(2)}) copy-start(bf16[512,8,64]{0,2,1:T(8,128)(2,1)S(1)} %fusion.7) | copy-start | bytes 1572868
  72.1 1.0 copy-start.4
  72.3 2.2 %copy-start.7 = (bf16[512,8,64]{0,2,1:T(8,128)(2,1)}, bf16[512,8,64]{0,2,1:T(8,128)(2,1)S(1)}, u32[]{:S(2)}) copy-start(bf16[512,8,64]{0,2,1:T(8,128)(2,1)S(1)} %fusion.10) | copy-start | bytes 1572868
  75.5 4.6 %collective-permute-start.1 = (bf16[512,1024]{0,1:T(8,128)(2,1)S(1)}, bf16[512,1024]{0,1:T(8,128)(2,1)S(1)}, u32[]{:S(2)}, u32[]{:S(2)}) collective-permute-start(bf16[512,1024]{0,1:T(8,128)(2,1)S(1)} %select_convert_fusion), channel_id=1, source_target_pairs={{0,32},{32,0},{1,33},{33,1},{2,34},{34,2},{3,35},{35,3},{4,36},{36... | collective-permute-start | bytes 3145736 | tf_op jit(solution)/shard_map/ppermute | solution.py:147
  80.7 6.4 %copy-start.11 = (bf16[4,128,8,64]{1,0,3,2:T(4,128)(2,1)S(1)}, bf16[4,128,8,64]{1,0,3,2:T(4,128)(2,1)}, u32[]{:S(2)}) copy-start(bf16[4,128,8,64]{1,0,3,2:T(4,128)(2,1)} %copy-done.10) | copy-start | bytes 1572868
  82.0 7.6 %copy-start.2 = (bf16[512,1024]{0,1:T(8,128)(2,1)S(1)}, bf16[512,1024]{0,1:T(8,128)(2,1)}, u32[]{:S(2)}) copy-start(bf16[512,1024]{0,1:T(8,128)(2,1)} %copy-done.1) | copy-start | bytes 3145732
  82.0 7.6 %copy-start.6 = (bf16[512,8,64]{0,2,1:T(8,128)(2,1)S(1)}, bf16[512,8,64]{0,2,1:T(8,128)(2,1)}, u32[]{:S(2)}) copy-start(bf16[512,8,64]{0,2,1:T(8,128)(2,1)} %copy-done.5) | copy-start | bytes 1572868
  82.0 30.2 %all-to-all-start.1 = ((bf16[32,16,1024]{2,1,0:T(8,128)(2,1)}), bf16[32,16,1024]{2,1,0:T(8,128)(2,1)}, u32[]{:S(2)}, u32[]{:S(2)}) async-start(bf16[32,16,1024]{2,1,0:T(8,128)(2,1)} %bitcast.133), calls=%async_computation.1 | async-start | bytes 2097152 | tf_op jit(solution)/shard_map/all_to_all | solution.py:124
  89.6 31.6 %copy-start.8 = (bf16[512,8,64]{0,2,1:T(8,128)(2,1)S(1)}, bf16[512,8,64]{0,2,1:T(8,128)(2,1)}, u32[]{:S(2)}) copy-start(bf16[512,8,64]{0,2,1:T(8,128)(2,1)} %copy-done.7) | copy-start | bytes 1572868
  114.4 16.3 %all-to-all-start.2 = ((bf16[8,16,1024]{2,1,0:T(8,128)(2,1)}), bf16[8,16,1024]{2,1,0:T(8,128)(2,1)S(1)}, u32[]{:S(2)}, u32[]{:S(2)}) async-start(bf16[8,16,1024]{2,1,0:T(8,128)(2,1)} %broadcast_in_dim.52), calls=%async_computation.2 | async-start | bytes 524288 | tf_op jit(solution)/shard_map/all_to_all | solution.py:120
  130.7 9.9 %collective-permute-start.2 = (f32[16,1024]{1,0:T(8,128)S(1)}, f32[16,1024]{1,0:T(8,128)S(1)}, u32[]{:S(2)}, u32[]{:S(2)}) collective-permute-start(f32[16,1024]{1,0:T(8,128)S(1)} %convert_reduce_fusion), channel_id=1, source_target_pairs={{0,32},{32,0},{1,33},{33,1},{2,34},{34,2},{3,35},{35,3},{4,36},{36... | collective-permute-start | bytes 196616 | tf_op jit(solution)/shard_map/ppermute | solution.py:153

commit v3 on v2

v3 whole, which is shorter than its diff:
```python
import math
import jax
import jax.numpy as jnp
from jax import lax
from jax.experimental import pallas as pl
from jax.experimental.pallas import tpu as pltpu
from jax.sharding import PartitionSpec as P

HEADS = 8
HEAD = 64
ROW = 32
SPAN = 128
STEP = 256
gain = 6.0 / HEAD
tiny_eps = 1e-06
f32, bf16 = jnp.float32, jnp.bfloat16


def dot_nn(a, b):
    return lax.dot_general(a, b, (((1,), (0,)), ((), ())), preferred_element_type=f32)


def dot_nt(a, b):
    return lax.dot_general(a, b, (((1,), (1,)), ((), ())), preferred_element_type=f32)


def dot_tn(a, b):
    return lax.dot_general(a, b, (((0,), (0,)), ((), ())), preferred_element_type=f32)


def head_ones(width):
    row = lax.broadcasted_iota(jnp.int32, (width, width), 0) // HEAD
    col = lax.broadcasted_iota(jnp.int32, (width, width), 1) // HEAD
    return jnp.where(row == col, 1.0, 0.0).astype(bf16)


def head_means(values, ones):
    return dot_nn(values.astype(bf16), ones) * (1.0 / HEAD)


def stacked(block):
    first = lax.broadcasted_iota(jnp.int32, block.shape, 1) < HEAD
    zero = jnp.zeros((), block.dtype)
    return jnp.concatenate((jnp.where(first, block, zero), jnp.where(first, zero, block)), axis=0)


def unstacked(block):
    span = block.shape[0] // 2
    first = lax.broadcasted_iota(jnp.int32, (span, block.shape[1]), 1) < HEAD
    return jnp.where(first, block[:span], block[span:])


def per_head(values, scale_of):
    return jnp.concatenate(
        (scale_of(values[:, :SPAN]), scale_of(values[:, SPAN:])), axis=1
    )


def forward_kernel(normed_ref, grads_ref, wqkv_ref, raw_ref, half_ref, probs_ref, dwo_ref, acc_ref):
    step = pl.program_id(0)
    width = dwo_ref.shape[0]
    ones = head_ones(width)
    qkv = dot_nn(normed_ref[...], wqkv_ref[...])
    query, key = qkv[:, :width], qkv[:, width : 2 * width]
    raw_ref[...] = qkv[:, : 2 * width]
    q_half = (query * lax.rsqrt(head_means(query * query, ones) + tiny_eps)).astype(bf16)
    k_half = (key * lax.rsqrt(head_means(key * key, ones) + tiny_eps)).astype(bf16)
    v_half = qkv[:, 2 * width :].astype(bf16)
    half_ref[:, :width] = q_half
    half_ref[:, width : 2 * width] = k_half
    half_ref[:, 2 * width :] = v_half
    row_of = lax.broadcasted_iota(jnp.int32, (SPAN, 2 * SPAN), 0) // ROW
    col_of = lax.broadcasted_iota(jnp.int32, (SPAN, 2 * SPAN), 1) % SPAN // ROW
    same_row = row_of == col_of
    spans = []
    for low in range(0, STEP, SPAN):
        pairs = []
        for left in range(0, width, 2 * HEAD):
            rows, cols = slice(low, low + SPAN), slice(left, left + 2 * HEAD)
            k_two, v_two = stacked(k_half[rows, cols]), stacked(v_half[rows, cols])
            scores = dot_nt(q_half[rows, cols], k_two)
            exps = jnp.where(same_row, jnp.exp(scores * gain), 0.0)
            probs = per_head(exps, lambda e: e * (1.0 / jnp.sum(e, axis=1, keepdims=True)))
            probs_ref[rows, 2 * left : 2 * left + 2 * SPAN] = probs
            pairs.append(dot_nn(probs.astype(bf16), v_two).astype(bf16))
        spans.append(jnp.concatenate(pairs, axis=1))
    attended = jnp.concatenate(spans, axis=0)
    term = dot_tn(attended, grads_ref[...])

    @pl.when(step == 0)
    def _():
        acc_ref[...] = term

    @pl.when(step > 0)
    def _():
        acc_ref[...] += term

    @pl.when(step == pl.num_programs(0) - 1)
    def _():
        dwo_ref[...] = acc_ref[...].astype(bf16)


def backward_kernel(
    normed_ref, grads_ref, raw_ref, half_ref, probs_ref, wo_ref, dqkv_ref, dw_ref, acc_ref
):
    step = pl.program_id(0)
    width = wo_ref.shape[0]
    ones = head_ones(width)
    grad_att = dot_nt(grads_ref[...], wo_ref[...]).astype(bf16)
    spans = []
    for low in range(0, STEP, SPAN):
        d_query, d_key, d_value = [], [], []
        for left in range(0, width, 2 * HEAD):
            rows, cols = slice(low, low + SPAN), slice(left, left + 2 * HEAD)
            q_pair = half_ref[rows, left : left + 2 * HEAD]
            k_two = stacked(half_ref[rows, width + left : width + left + 2 * HEAD])
            v_two = stacked(half_ref[rows, 2 * width + left : 2 * width + left + 2 * HEAD])
            g_pair = grad_att[rows, cols]
            probs = probs_ref[rows, 2 * left : 2 * left + 2 * SPAN]
            grad_probs = dot_nt(g_pair, v_two)
            d_value.append(unstacked(dot_tn(probs.astype(bf16), g_pair)))
            weighted = probs * grad_probs
            d_scores = jnp.concatenate(
                [
                    weighted[:, half]
                    - probs[:, half] * jnp.sum(weighted[:, half], axis=1, keepdims=True)
                    for half in (slice(0, SPAN), slice(SPAN, 2 * SPAN))
                ],
                axis=1,
            )
            d_scores = (d_scores * gain).astype(bf16)
            d_query.append(dot_nn(d_scores, k_two))
            d_key.append(unstacked(dot_tn(d_scores, q_pair)))
        spans.append([jnp.concatenate(part, axis=1) for part in (d_query, d_key, d_value)])
    d_query, d_key, d_value = (jnp.concatenate(part, axis=0) for part in zip(*spans))

    def through_norm(raw, grad):
        scale = lax.rsqrt(head_means(raw * raw, ones) + tiny_eps)
        unit = raw * scale
        return (scale * (grad - unit * head_means(unit * grad, ones))).astype(bf16)

    dqkv = jnp.concatenate(
        (
            through_norm(raw_ref[:, :width], d_query),
            through_norm(raw_ref[:, width:], d_key),
            d_value.astype(bf16),
        ),
        axis=1,
    )
    dqkv_ref[...] = dqkv
    term = dot_tn(normed_ref[...], dqkv)

    @pl.when(step == 0)
    def _():
        acc_ref[...] = term

    @pl.when(step > 0)
    def _():
        acc_ref[...] += term

    @pl.when(step == pl.num_programs(0) - 1)
    def _():
        dw_ref[...] = acc_ref[...].astype(bf16)


def token_spec(width):
    return pl.BlockSpec((STEP, width), lambda i: (i, 0))


def whole_spec(shape):
    return pl.BlockSpec(shape, lambda i: (0, 0))


def forward(normed, grads, wqkv):
    tokens, depth = normed.shape
    width = wqkv.shape[1] // 3
    return pl.pallas_call(
        forward_kernel,
        grid=(tokens // STEP,),
        in_specs=[token_spec(depth), token_spec(depth), whole_spec(wqkv.shape)],
        out_specs=[
            token_spec(2 * width),
            token_spec(3 * width),
            token_spec(2 * width),
            whole_spec((width, depth)),
        ],
        out_shape=[
            jax.ShapeDtypeStruct((tokens, 2 * width), f32),
            jax.ShapeDtypeStruct((tokens, 3 * width), bf16),
            jax.ShapeDtypeStruct((tokens, 2 * width), f32),
            jax.ShapeDtypeStruct((width, depth), bf16),
        ],
        scratch_shapes=[pltpu.VMEM((width, depth), f32)],
        compiler_params=pltpu.CompilerParams(vmem_limit_bytes=32 * 1024 * 1024),
        cost_estimate=pl.CostEstimate(
            flops=3 * tokens * depth * width * 3, bytes_accessed=8 << 20, transcendentals=0
        ),
        name="attention_forward",
    )(normed, grads, wqkv)


def backward(normed, grads, raw, half, probs, wo):
    tokens, depth = normed.shape
    width = wo.shape[0]
    return pl.pallas_call(
        backward_kernel,
        grid=(tokens // STEP,),
        in_specs=[
            token_spec(depth),
            token_spec(depth),
            token_spec(2 * width),
            token_spec(3 * width),
            token_spec(2 * width),
            whole_spec(wo.shape),
        ],
        out_specs=[token_spec(3 * width), whole_spec((depth, 3 * width))],
        out_shape=[
            jax.ShapeDtypeStruct((tokens, 3 * width), bf16),
            jax.ShapeDtypeStruct((depth, 3 * width), bf16),
        ],
        scratch_shapes=[pltpu.VMEM((depth, 3 * width), f32)],
        compiler_params=pltpu.CompilerParams(vmem_limit_bytes=32 * 1024 * 1024),
        cost_estimate=pl.CostEstimate(
            flops=6 * tokens * depth * width * 3, bytes_accessed=8 << 20, transcendentals=0
        ),
        name="attention_backward",
    )(normed, grads, raw, half, probs, wo)


MESH_AXES = ("y", "core", "x", "z")
PEERS = ("x", "z")


def swapped(block):
    return lax.ppermute(block, "core", [(0, 1), (1, 0)])


def spread(block, axis):
    copies = jnp.broadcast_to(block[None], (lax.axis_size(axis),) + block.shape)
    return lax.all_to_all(copies, axis, split_axis=0, concat_axis=0, tiled=True)


def shared_sum(blocks, axis):
    arrived = lax.all_to_all(blocks, axis, split_axis=0, concat_axis=0, tiled=True)
    return jnp.sum(arrived.astype(f32), axis=0)


def local(trace_rows, upstream, counts, w_query, w_key, w_value, w_out):
    core = lax.axis_index("core")
    is_first = core == 0
    view_count, most_rows, row_length, depth = trace_rows.shape
    tokens = view_count * most_rows * row_length
    half_width = w_query.shape[1] // 2
    own = core * half_width

    def ordered(mine, theirs, axis):
        return jnp.concatenate(
            (jnp.where(is_first, mine, theirs), jnp.where(is_first, theirs, mine)), axis=axis
        )

    def half_of(block, axis, of_other=False):
        low = half_width - own if of_other else own
        return lax.dynamic_slice_in_dim(block, low, half_width, axis)

    shards = jnp.concatenate(
        [half_of(weight, 1) for weight in (w_query, w_key, w_value, w_out)], axis=1
    )
    gathered = spread(shards, PEERS).reshape(-1, 4 * half_width)
    w_qkv, w_out_cols = gathered[:, : 3 * half_width], gathered[:, 3 * half_width :]
    w_out_rows = ordered(
        half_of(w_out_cols, 0), swapped(half_of(w_out_cols, 0, of_other=True)), 1
    )

    is_live = lax.iota(jnp.int32, most_rows)[None, :] < counts.reshape(view_count)[:, None]
    masked = jnp.where(is_live[:, :, None, None], upstream, jnp.zeros((), upstream.dtype))
    rows, grads = trace_rows.reshape(tokens, depth), masked.reshape(tokens, depth)
    both_rows = jnp.concatenate((rows, swapped(rows)), axis=0).astype(f32)
    both_grads = jnp.concatenate((grads, swapped(grads)), axis=0)
    inv_rms = lax.rsqrt(jnp.mean(both_rows * both_rows, axis=-1, keepdims=True) + tiny_eps)
    normed = (both_rows * inv_rms).astype(bf16)

    raw, half, probs, d_out_rows = forward(normed, both_grads, w_qkv)
    d_out_cols = ordered(
        half_of(d_out_rows, 1), swapped(half_of(d_out_rows, 1, of_other=True)), 0
    )
    d_qkv, d_weights = backward(normed, both_grads, raw, half, probs, w_out_rows)

    terms = jnp.concatenate((d_weights, d_out_cols), axis=1)
    peers = lax.axis_size(PEERS)
    total = shared_sum(terms.reshape(peers, depth // peers, 4 * half_width), PEERS)
    total = jnp.sum(spread(total.astype(bf16), "y").astype(f32), axis=0)
    devices = math.prod(lax.axis_size(name) for name in MESH_AXES)
    total = total * (1.0 / math.sqrt(devices * tokens // 2))
    other_total = swapped(total)
    weight_grads = [
        ordered(total[:, low : low + half_width], other_total[:, low : low + half_width], 1)
        for low in range(0, 4 * half_width, half_width)
    ]

    grad_norm = dot_nt(d_qkv, w_qkv)
    grad_norm = grad_norm[:tokens] + swapped(grad_norm[tokens:].astype(bf16)).astype(f32)
    inv_rms, scaled = inv_rms[:tokens], both_rows[:tokens] * inv_rms[:tokens]
    done = grads.astype(f32) + inv_rms * (
        grad_norm - scaled * jnp.mean(scaled * grad_norm, axis=-1, keepdims=True)
    )
    return (done.astype(bf16).reshape(trace_rows.shape), *weight_grads)


def solution(mesh):
    fine_mesh = jax.sharding.Mesh(mesh.devices.reshape(8, 2, 4, 8), MESH_AXES)
    every, peer = P(MESH_AXES), P(PEERS, None)
    in_specs = (every, every, P(("y", "core"), PEERS), peer, peer, peer, peer)
    out_specs = (every, peer, peer, peer, peer)
    return jax.shard_map(
        local, mesh=fine_mesh, in_specs=in_specs, out_specs=out_specs, check_vma=False
    )
```

time: 143 us -> 144 us (level)
  matrix products: 16.4 us -> 2.14 us
  Pallas kernels: 0 us -> 13.5 us
  waiting for transfers between devices: 54.9 us -> 45.9 us
  starting transfers between devices: 42.7 us -> 49.1 us
  local copies, waits for them, and re-layouts: 16.5 us -> 19.6 us
    dot_general x17 -> x1, matrix products: 16.4 us -> 2.14 us  [dot_nt(): lax.dot_general(a, b, (((1,), (1,)), ((), ())), preferred_element_type=f32)]
    pallas_call x0 -> x2, Pallas kernels: none -> 13.5 us  [the longest x1 8.66 us: backward(): pl.pallas_call(backward_kernel, grid=(tokens // STEP,), in_specs=[token_s...]
    unnamed x38 -> x36, local copies, waits for them, and re-layouts: 2.75 us -> 11.3 us
    reshape x5 -> x0, local copies, waits for them, and re-layouts: 8.42 us -> none  [the longest x2 4.86 us: layer_backward(): values_full.astype(jnp.bfloat16)]
    all_to_all x2, waiting for transfers between devices: 30.7 us -> 24.1 us  [spread(): return lax.all_to_all(copies, axis, split_axis=0, concat_axis=0, tiled=True)]
    ppermute x3 -> x6, starting transfers between devices: 16.9 us -> 23.4 us  [swapped(): return lax.ppermute(block, 'core', [(0, 1), (1, 0)])]
    concatenate x0 -> x8, other arithmetic: none -> 3.81 us  [the longest x5 2.49 us: ordered(): jnp.concatenate((jnp.where(is_first, mine, theirs), jnp.where(is_first, t...]
    dynamic_slice x0 -> x6, local copies, waits for them, and re-layouts: none -> 3.41 us  [half_of(): return lax.dynamic_slice_in_dim(block, low, half_width, axis)]
  transfers between devices with their start and end apart: 6 -> 9, of which waited for: 5 -> 5; matrix products, arithmetic and copies ran while one was open for 8% -> 8% of each run, Pallas kernels for 0% -> 0%
where the time goes in v3:
time: 144 us; the launch traced here: 143 us
  starting transfers between devices  49.1 us (34%)
  waiting for transfers between devices  45.9 us (32%)
  local copies, waits for them, and re-layouts  19.6 us (14%)
  Pallas kernels  13.5 us (9%)
  other arithmetic  11.6 us (8%)
  matrix products  2.14 us (1%)
    all_to_all x2, waiting for transfers between devices, spread(): return lax.all_to_all(copies, axis, split_axis=0, concat_axis=0, tiled=True)  24.1 us
    ppermute x6, starting transfers between devices, swapped(): return lax.ppermute(block, 'core', [(0, 1), (1, 0)])  23.4 us
    all_to_all x2, starting transfers between devices, spread(): return lax.all_to_all(copies, axis, split_axis=0, concat_axis=0, tiled=True)  20.7 us
    all_to_all x1, waiting for transfers between devices, shared_sum(): lax.all_to_all(blocks, axis, split_axis=0, concat_axis=0, tiled=True)  18.6 us
    unnamed x36, local copies, waits for them, and re-layouts  11.3 us
    pallas_call x1, Pallas kernels, backward(): pl.pallas_call(backward_kernel, grid=(tokens // STEP,), in_specs=[token_s...  8.66 us
    all_to_all x1, starting transfers between devices, shared_sum(): lax.all_to_all(blocks, axis, split_axis=0, concat_axis=0, tiled=True)  5.05 us
    pallas_call x1, Pallas kernels, forward(): pl.pallas_call(forward_kernel, grid=(tokens // STEP,), in_specs=[token_sp...  4.8 us
  transfers between devices with their start and end apart: 9, of which 5 were waited for; matrix products, arithmetic and copies ran while one was open for 8% of the time, Pallas kernels for 0%

profile of v3, /device:TPU:1, one launch (start us, length us, event | category | flops | bytes accessed | tf_op | source)
XLA Modules:
  0.0 142.8 jit_solution(13222599596098981702)
XLA Ops:
  0.7 0.7 copy-done
  1.4 0.7 constant_dynamic-slice_fusion.3
  2.1 0.7 constant_dynamic-slice_fusion.4
  2.8 0.7 constant_dynamic-slice_fusion.5
  3.5 1.1 broadcast_in_dim.18
  4.6 13.8 %all-to-all-start = ((bf16[32,16,1024]{2,1,0:T(8,128)(2,1)}), bf16[32,16,1024]{2,1,0:T(8,128)(2,1)}, u32[]{:S(2)}, u32[]{:S(2)}) async-start(bf16[32,16,1024]{2,1,0:T(8,128)(2,1)} %broadcast_in_dim.18), calls=%async_computation | async-start | bytes 2097152 | tf_op jit(solution)/shard_map/all_to_all | solution.py:240
  18.5 2.9 %collective-permute-start = (bf16[512,512]{1,0:T(8,128)(2,1)S(1)}, bf16[512,512]{1,0:T(8,128)(2,1)S(1)}, u32[]{:S(2)}, u32[]{:S(2)}) collective-permute-start(bf16[512,512]{1,0:T(8,128)(2,1)S(1)} %bitcast.8), channel_id=1, source_target_pairs={{0,32},{32,0},{1,33},{33,1},{2,34},{34,2},{3,35},{35,3},{4,36},{36... | collective-permute-start | bytes 1572872 | tf_op jit(solution)/shard_map/ppermute | solution.py:235
  21.5 1.9 %collective-permute-start.1 = (bf16[512,512]{1,0:T(8,128)(2,1)S(1)}, bf16[512,512]{1,0:T(8,128)(2,1)S(1)}, u32[]{:S(2)}, u32[]{:S(2)}) collective-permute-start(bf16[512,512]{1,0:T(8,128)(2,1)S(1)} %bitcast.12), channel_id=1, source_target_pairs={{0,32},{32,0},{1,33},{33,1},{2,34},{34,2},{3,35},{35,3},{4,36},{36... | collective-permute-start | bytes 1572872 | tf_op jit(solution)/shard_map/ppermute | solution.py:235
  23.5 0.3 multiply_reduce_fusion
  23.7 1.6 %collective-permute-done.1 = bf16[512,512]{1,0:T(8,128)(2,1)S(1)} collective-permute-done((bf16[512,512]{1,0:T(8,128)(2,1)S(1)}, bf16[512,512]{1,0:T(8,128)(2,1)S(1)}, u32[]{:S(2)}, u32[]{:S(2)}) %collective-permute-start.1) | collective-permute-done | bytes 524320 | tf_op jit(solution)/shard_map/ppermute | solution.py:235
  25.4 0.6 copy-done.15
  26.0 0.3 multiply_convert_fusion.normed_ref
  26.3 16.7 %all-to-all-done = bf16[32,16,1024]{2,1,0:T(8,128)(2,1)} async-done(((bf16[32,16,1024]{2,1,0:T(8,128)(2,1)}), bf16[32,16,1024]{2,1,0:T(8,128)(2,1)}, u32[]{:S(2)}, u32[]{:S(2)}) %all-to-all-start) | async-done | bytes 1048608 | tf_op jit(solution)/shard_map/all_to_all | solution.py:240
  43.0 1.2 slice.59.wqkv_ref
  44.2 1.0 slice.60
  45.2 4.8 %attention_forward.1 = (f32[1024,512]{1,0:T(8,128)S(1)}, bf16[1024,768]{1,0:T(8,128)(2,1)S(1)}, f32[1024,512]{1,0:T(8,128)S(1)}, bf16[256,512]{1,0:T(8,128)(2,1)S(1)}) custom-call(bf16[1024,512]{1,0:T(8,128)(2,1)S(1)} %multiply_convert_fusion.normed_ref, bf16[1024,512]{1,0:T(8,128)(2,1)S(1)} %pad_maximum_fusion.grads_ref, bf16[512,768]{1,0:T(8,128)(2,1)S(1)} %slice.59.wqkv_ref), custom_call_target="tpu_custom_call" | custom-call | flops 1207959552 | bytes 8388608 | tf_op jit(solution)/shard_map/attention_forward/pallas_call | solution.py:177
  50.0 1.3 copy-done.3
  51.4 1.3 copy-done.5
  52.7 1.2 copy-done.7
  53.8 0.7 constant_dynamic-slice_fusion
  54.5 6.9 %collective-permute-start.4 = (bf16[256,256]{1,0:T(8,128)(2,1)}, bf16[256,256]{1,0:T(8,128)(2,1)S(1)}, u32[]{:S(2)}, u32[]{:S(2)}) collective-permute-start(bf16[256,256]{1,0:T(8,128)(2,1)} %constant_dynamic-slice_fusion), channel_id=1, source_target_pairs={{0,32},{32,0},{1,33},{33,1},{2,34},{34,2},{3,35},{35,3},{4,36},{36... | collective-permute-start | bytes 393224 | tf_op jit(solution)/shard_map/ppermute | solution.py:235
  61.4 0.7 constant_dynamic-slice_fusion.1
  62.0 1.9 %collective-permute-start.2 = (bf16[256,256]{1,0:T(8,128)(2,1)}, bf16[256,256]{1,0:T(8,128)(2,1)}, u32[]{:S(2)}, u32[]{:S(2)}) collective-permute-start(bf16[256,256]{1,0:T(8,128)(2,1)} %constant_dynamic-slice_fusion.1), channel_id=1, source_target_pairs={{0,32},{32,0},{1,33},{33,1},{2,34},{34,2},{3,35},{35,3},{4,36},{36... | collective-permute-start | bytes 393224 | tf_op jit(solution)/shard_map/ppermute | solution.py:235
  64.0 1.6 %collective-permute-done.2 = bf16[256,256]{1,0:T(8,128)(2,1)} collective-permute-done((bf16[256,256]{1,0:T(8,128)(2,1)}, bf16[256,256]{1,0:T(8,128)(2,1)}, u32[]{:S(2)}, u32[]{:S(2)}) %collective-permute-start.2) | collective-permute-done | bytes 131104 | tf_op jit(solution)/shard_map/ppermute | solution.py:235
  65.6 1.1 broadcast_select_fusion.2
  66.7 1.6 %copy-done.4 = f32[1024,512]{1,0:T(8,128)S(1)} copy-done((f32[1024,512]{1,0:T(8,128)S(1)}, f32[1024,512]{1,0:T(8,128)}, u32[]{:S(2)}) %copy-start.4) | copy-done | bytes 2097176
  68.3 1.6 %copy-done.6 = f32[1024,512]{1,0:T(8,128)S(1)} copy-done((f32[1024,512]{1,0:T(8,128)S(1)}, f32[1024,512]{1,0:T(8,128)}, u32[]{:S(2)}) %copy-start.6) | copy-done | bytes 2097176
  69.9 1.4 copy-done.8
  71.3 8.7 %attention_backward.1 = (bf16[1024,768]{1,0:T(8,128)(2,1)S(1)}, bf16[512,768]{1,0:T(8,128)(2,1)S(1)}) custom-call(bf16[1024,512]{1,0:T(8,128)(2,1)S(1)} %multiply_convert_fusion.normed_ref, bf16[1024,512]{1,0:T(8,128)(2,1)S(1)} %pad_maximum_fusion.grads_ref, f32[1024,512]{1,0:T(8,128)S(1)} %copy-done.4, bf16[1024,768]{1,0:T(8,128)(2,1)S(1)} %copy-done.8, ...), custom_call_target="tpu_custom_call" | custom-call | flops 2415919104 | bytes 8388608 | tf_op jit(solution)/shard_map/attention_backward/pallas_call | solution.py:205
  80.0 1.2 maximum_maximum_fusion
  81.5 5.1 %all-to-all-start.1 = ((bf16[32,16,1024]{2,1,0:T(8,128)(2,1)}), bf16[32,16,1024]{2,1,0:T(8,128)(2,1)}, u32[]{:S(2)}, u32[]{:S(2)}) async-start(bf16[32,16,1024]{2,1,0:T(8,128)(2,1)} %bitcast.14), calls=%async_computation.1 | async-start | bytes 2097152 | tf_op jit(solution)/shard_map/all_to_all | solution.py:244
  86.6 2.1 %fusion = f32[1024,512]{1,0:T(8,128)S(1)} fusion(bf16[1024,768]{1,0:T(8,128)(2,1)S(1)} %copy-done.2, bf16[512,1024]{1,0:T(8,128)(2,1)} %bitcast.3), kind=kOutput, calls=%fused_computation.40 | convolution fusion | flops 805306368 | bytes 4456448 | tf_op jit(solution)/shard_map/dot_general | solution.py:24
  88.7 1.3 copy-done.12
  90.0 0.9 slice.101
  90.9 2.3 %collective-permute-start.3 = (bf16[512,512]{1,0:T(8,128)(2,1)}, bf16[512,512]{1,0:T(8,128)(2,1)}, u32[]{:S(2)}, u32[]{:S(2)}) collective-permute-start(bf16[512,512]{1,0:T(8,128)(2,1)} %slice.101), channel_id=1, source_target_pairs={{0,32},{32,0},{1,33},{33,1},{2,34},{34,2},{3,35},{35,3},{4,36},{36... | collective-permute-start | bytes 1572872 | tf_op jit(solution)/shard_map/ppermute | solution.py:235
  93.2 18.6 %all-to-all-done.1 = bf16[32,16,1024]{2,1,0:T(8,128)(2,1)} async-done(((bf16[32,16,1024]{2,1,0:T(8,128)(2,1)}), bf16[32,16,1024]{2,1,0:T(8,128)(2,1)}, u32[]{:S(2)}, u32[]{:S(2)}) %all-to-all-start.1) | async-done | bytes 1048608 | tf_op jit(solution)/shard_map/all_to_all | solution.py:244
  111.8 1.4 reduce_sum.41
  113.2 0.7 broadcast_in_dim.19
  113.9 6.8 %all-to-all-start.2 = ((bf16[8,16,1024]{2,1,0:T(8,128)(2,1)}), bf16[8,16,1024]{2,1,0:T(8,128)(2,1)S(1)}, u32[]{:S(2)}, u32[]{:S(2)}) async-start(bf16[8,16,1024]{2,1,0:T(8,128)(2,1)} %broadcast_in_dim.19), calls=%async_computation.2 | async-start | bytes 524288 | tf_op jit(solution)/shard_map/all_to_all | solution.py:240
  120.8 0.3 maximum_convert_fusion
  121.1 1.7 %multiply_reduce_fusion.1 = f32[512]{0:T(512)S(1)} fusion(f32[1024,512]{1,0:T(8,128)S(1)} %maximum_convert_fusion, bf16[512,512]{1,0:T(8,128)(2,1)} %collective-permute-done.3, f32[1024,512]{1,0:T(8,128)} %copy-done.12, f32[512]{0:T(512)S(1)} %slice.45), kind=kLoop, calls=%fused_computation.9 | loop fusion | flops 1310208 | bytes 2625536 | tf_op jit(solution)/shard_map/reduce_sum | solution.py:304
  122.8 7.4 %all-to-all-done.2 = bf16[8,16,1024]{2,1,0:T(8,128)(2,1)S(1)} async-done(((bf16[8,16,1024]{2,1,0:T(8,128)(2,1)}), bf16[8,16,1024]{2,1,0:T(8,128)(2,1)S(1)}, u32[]{:S(2)}, u32[]{:S(2)}) %all-to-all-start.2) | async-done | bytes 262176 | tf_op jit(solution)/shard_map/all_to_all | solution.py:240
  130.2 7.5 %collective-permute-start.5 = (f32[16,1024]{1,0:T(8,128)S(1)}, f32[16,1024]{1,0:T(8,128)S(1)}, u32[]{:S(2)}, u32[]{:S(2)}) collective-permute-start(f32[16,1024]{1,0:T(8,128)S(1)} %broadcast_multiply_fusion), channel_id=1, source_target_pairs={{0,32},{32,0},{1,33},{33,1},{2,34},{34,2},{3,35},{35,3},{4,36},{36... | collective-permute-start | bytes 196616 | tf_op jit(solution)/shard_map/ppermute | solution.py:235
  137.8 2.5 %add_convert_fusion = bf16[512,512]{1,0:T(8,128)(2,1)} fusion(f32[1024,512]{1,0:T(8,128)S(1)} %maximum_convert_fusion, bf16[512,512]{1,0:T(8,128)(2,1)} %collective-permute-done.3, f32[1024,512]{1,0:T(8,128)} %copy-done.12, f32[512]{0:T(512)S(1)} %broadcast_multiply_fusion.1, f32[512]{0:T(512)S(1)} %slice.45, bf16[2,8,32,512]{3,2,1,0:T(8,128)(2,1)S(1)} %copy-done.11), kind=kLoop, calls=%fused_computation.8 | loop fusion | flops 2359296 | bytes 3674112 | tf_op jit(solution)/shard_map/convert_element_type | solution.py:306
  140.3 0.6 pad_maximum_fusion.6
  140.9 0.6 pad_maximum_fusion.5
  141.6 0.6 pad_maximum_fusion.4
  142.2 0.6 pad_maximum_fusion.3
  (43 shorter events, 0.7 us)
Async XLA Ops:
  0.6 0.7 copy-start
  0.6 17.8 %copy-start.9 = (bf16[2,8,32,512]{3,2,1,0:T(8,128)(2,1)S(1)}, bf16[2,8,32,512]{3,2,1,0:T(8,128)(2,1)}, u32[]{:S(2)}) copy-start(bf16[2,8,32,512]{3,2,1,0:T(8,128)(2,1)} %param.7) | copy-start | bytes 1572868
  0.7 20.7 %copy-start.17 = (s32[1,2]{1,0:T(1,128)S(1)}, s32[1,2]{1,0:T(1,128)}, u32[]{:S(2)}) copy-start(s32[1,2]{1,0:T(1,128)} %param.9) | copy-start | bytes 28
  0.7 20.7 %copy-start.14 = (bf16[2,8,32,512]{3,2,1,0:T(8,128)(2,1)S(1)}, bf16[2,8,32,512]{3,2,1,0:T(8,128)(2,1)}, u32[]{:S(2)}) copy-start(bf16[2,8,32,512]{3,2,1,0:T(8,128)(2,1)} %param.8) | copy-start | bytes 1572868
  4.6 38.5 %all-to-all-start = ((bf16[32,16,1024]{2,1,0:T(8,128)(2,1)}), bf16[32,16,1024]{2,1,0:T(8,128)(2,1)}, u32[]{:S(2)}, u32[]{:S(2)}) async-start(bf16[32,16,1024]{2,1,0:T(8,128)(2,1)} %broadcast_in_dim.18), calls=%async_computation | async-start | bytes 2097152 | tf_op jit(solution)/shard_map/all_to_all | solution.py:240
  18.5 5.0 %collective-permute-start = (bf16[512,512]{1,0:T(8,128)(2,1)S(1)}, bf16[512,512]{1,0:T(8,128)(2,1)S(1)}, u32[]{:S(2)}, u32[]{:S(2)}) collective-permute-start(bf16[512,512]{1,0:T(8,128)(2,1)S(1)} %bitcast.8), channel_id=1, source_target_pairs={{0,32},{32,0},{1,33},{33,1},{2,34},{34,2},{3,35},{35,3},{4,36},{36... | collective-permute-start | bytes 1572872 | tf_op jit(solution)/shard_map/ppermute | solution.py:235
  21.5 3.9 %copy-start.10 = (bf16[2,8,32,512]{3,2,1,0:T(8,128)(2,1)}, bf16[2,8,32,512]{3,2,1,0:T(8,128)(2,1)S(1)}, u32[]{:S(2)}) copy-start(bf16[2,8,32,512]{3,2,1,0:T(8,128)(2,1)S(1)} %broadcast_select_fusion) | copy-start | bytes 1572868
  21.5 3.8 %collective-permute-start.1 = (bf16[512,512]{1,0:T(8,128)(2,1)S(1)}, bf16[512,512]{1,0:T(8,128)(2,1)S(1)}, u32[]{:S(2)}, u32[]{:S(2)}) collective-permute-start(bf16[512,512]{1,0:T(8,128)(2,1)S(1)} %bitcast.12), channel_id=1, source_target_pairs={{0,32},{32,0},{1,33},{33,1},{2,34},{34,2},{3,35},{35,3},{4,36},{36... | collective-permute-start | bytes 1572872 | tf_op jit(solution)/shard_map/ppermute | solution.py:235
  25.4 0.6 copy-start.15
  45.2 16.2 %copy-start.13 = (bf16[512,256]{1,0:T(8,128)(2,1)}, bf16[512,256]{1,0:T(8,128)(2,1)S(1)}, u32[]{:S(2)}) copy-start(bf16[512,256]{1,0:T(8,128)(2,1)S(1)} %slice.60) | copy-start | bytes 786436
  50.0 1.3 copy-start.3
  51.4 1.3 copy-start.5
  52.7 1.2 copy-start.7
  54.5 9.5 %collective-permute-start.4 = (bf16[256,256]{1,0:T(8,128)(2,1)}, bf16[256,256]{1,0:T(8,128)(2,1)S(1)}, u32[]{:S(2)}, u32[]{:S(2)}) collective-permute-start(bf16[256,256]{1,0:T(8,128)(2,1)} %constant_dynamic-slice_fusion), channel_id=1, source_target_pairs={{0,32},{32,0},{1,33},{33,1},{2,34},{34,2},{3,35},{35,3},{4,36},{36... | collective-permute-start | bytes 393224 | tf_op jit(solution)/shard_map/ppermute | solution.py:235
  62.0 3.6 %collective-permute-start.2 = (bf16[256,256]{1,0:T(8,128)(2,1)}, bf16[256,256]{1,0:T(8,128)(2,1)}, u32[]{:S(2)}, u32[]{:S(2)}) collective-permute-start(bf16[256,256]{1,0:T(8,128)(2,1)} %constant_dynamic-slice_fusion.1), channel_id=1, source_target_pairs={{0,32},{32,0},{1,33},{33,1},{2,34},{34,2},{3,35},{35,3},{4,36},{36... | collective-permute-start | bytes 393224 | tf_op jit(solution)/shard_map/ppermute | solution.py:235
  66.7 1.6 %copy-start.4 = (f32[1024,512]{1,0:T(8,128)S(1)}, f32[1024,512]{1,0:T(8,128)}, u32[]{:S(2)}) copy-start(f32[1024,512]{1,0:T(8,128)} %copy-done.3) | copy-start | bytes 6291460
  68.3 1.6 %copy-start.6 = (f32[1024,512]{1,0:T(8,128)S(1)}, f32[1024,512]{1,0:T(8,128)}, u32[]{:S(2)}) copy-start(f32[1024,512]{1,0:T(8,128)} %copy-done.5) | copy-start | bytes 6291460
  69.9 1.4 copy-start.8
  80.0 1.5 %copy-start.1 = (bf16[1024,768]{1,0:T(8,128)(2,1)}, bf16[1024,768]{1,0:T(8,128)(2,1)S(1)}, u32[]{:S(2)}) copy-start(bf16[1024,768]{1,0:T(8,128)(2,1)S(1)} %get-tuple-element.14) | copy-start | bytes 4718596
  81.5 5.1 %copy-start.2 = (bf16[1024,768]{1,0:T(8,128)(2,1)S(1)}, bf16[1024,768]{1,0:T(8,128)(2,1)}, u32[]{:S(2)}) copy-start(bf16[1024,768]{1,0:T(8,128)(2,1)} %copy-done.1) | copy-start | bytes 4718596
  81.5 30.3 %all-to-all-start.1 = ((bf16[32,16,1024]{2,1,0:T(8,128)(2,1)}), bf16[32,16,1024]{2,1,0:T(8,128)(2,1)}, u32[]{:S(2)}, u32[]{:S(2)}) async-start(bf16[32,16,1024]{2,1,0:T(8,128)(2,1)} %bitcast.14), calls=%async_computation.1 | async-start | bytes 2097152 | tf_op jit(solution)/shard_map/all_to_all | solution.py:244
  88.7 1.3 copy-start.12
  90.9 30.2 %collective-permute-start.3 = (bf16[512,512]{1,0:T(8,128)(2,1)}, bf16[512,512]{1,0:T(8,128)(2,1)}, u32[]{:S(2)}, u32[]{:S(2)}) collective-permute-start(bf16[512,512]{1,0:T(8,128)(2,1)} %slice.101), channel_id=1, source_target_pairs={{0,32},{32,0},{1,33},{33,1},{2,34},{34,2},{3,35},{35,3},{4,36},{36... | collective-permute-start | bytes 1572872 | tf_op jit(solution)/shard_map/ppermute | solution.py:235
  113.2 7.9 %copy-start.16 = (f32[1024]{0:T(1024)S(1)}, f32[1024]{0:T(1024)}, u32[]{:S(2)}) copy-start(f32[1024]{0:T(1024)} %copy-done.15) | copy-start | bytes 12292
  113.9 16.3 %all-to-all-start.2 = ((bf16[8,16,1024]{2,1,0:T(8,128)(2,1)}), bf16[8,16,1024]{2,1,0:T(8,128)(2,1)S(1)}, u32[]{:S(2)}, u32[]{:S(2)}) async-start(bf16[8,16,1024]{2,1,0:T(8,128)(2,1)} %broadcast_in_dim.19), calls=%async_computation.2 | async-start | bytes 524288 | tf_op jit(solution)/shard_map/all_to_all | solution.py:240
  121.0 16.7 %copy-start.11 = (bf16[2,8,32,512]{3,2,1,0:T(8,128)(2,1)S(1)}, bf16[2,8,32,512]{3,2,1,0:T(8,128)(2,1)}, u32[]{:S(2)}) copy-start(bf16[2,8,32,512]{3,2,1,0:T(8,128)(2,1)} %copy-done.10) | copy-start | bytes 1572868
  130.2 10.1 %collective-permute-start.5 = (f32[16,1024]{1,0:T(8,128)S(1)}, f32[16,1024]{1,0:T(8,128)S(1)}, u32[]{:S(2)}, u32[]{:S(2)}) collective-permute-start(f32[16,1024]{1,0:T(8,128)S(1)} %broadcast_multiply_fusion), channel_id=1, source_target_pairs={{0,32},{32,0},{1,33},{33,1},{2,34},{34,2},{3,35},{35,3},{4,36},{36... | collective-permute-start | bytes 196616 | tf_op jit(solution)/shard_map/ppermute | solution.py:235

commit v4 on v2

v4 whole, which is shorter than its diff:
```python
import math
import jax
import jax.numpy as jnp
from jax import lax
from jax.experimental import pallas as pl
from jax.experimental.pallas import tpu as pltpu
from jax.sharding import PartitionSpec as P

HEAD = 64
ROW = 32
SPAN = 128
gain = 6.0 / HEAD
tiny_eps = 1e-06
f32, bf16 = jnp.float32, jnp.bfloat16


def dot_nn(a, b):
    return lax.dot_general(a, b, (((1,), (0,)), ((), ())), preferred_element_type=f32)


def dot_nt(a, b):
    return lax.dot_general(a, b, (((1,), (1,)), ((), ())), preferred_element_type=f32)


def dot_tn(a, b):
    return lax.dot_general(a, b, (((0,), (0,)), ((), ())), preferred_element_type=f32)


def head_ones(width):
    row = lax.broadcasted_iota(jnp.int32, (width, width), 0) // HEAD
    col = lax.broadcasted_iota(jnp.int32, (width, width), 1) // HEAD
    return jnp.where(row == col, 1.0, 0.0).astype(bf16)


def head_means(values, ones):
    return dot_nn(values.astype(bf16), ones) * (1.0 / HEAD)


def stacked(block):
    first = lax.broadcasted_iota(jnp.int32, block.shape, 1) < HEAD
    zero = jnp.zeros((), block.dtype)
    return jnp.concatenate((jnp.where(first, block, zero), jnp.where(first, zero, block)), axis=0)


def unstacked(block):
    span = block.shape[0] // 2
    first = lax.broadcasted_iota(jnp.int32, (span, block.shape[1]), 1) < HEAD
    return jnp.where(first, block[:span], block[span:])


def attention(q_half, k_half, v_half, grad_att, same_row):
    k_two, v_two = stacked(k_half), stacked(v_half)
    exps = jnp.where(same_row, jnp.exp(dot_nt(q_half, k_two) * gain), 0.0)
    grad_probs = dot_nt(grad_att, v_two)
    probs, d_scores = [], []
    for half in (slice(0, SPAN), slice(SPAN, 2 * SPAN)):
        part = exps[:, half] * (1.0 / jnp.sum(exps[:, half], axis=1, keepdims=True))
        weighted = part * grad_probs[:, half]
        total = jnp.sum(weighted, axis=1, keepdims=True)
        probs.append(part.astype(bf16))
        d_scores.append(((weighted - part * total) * gain).astype(bf16))
    probs, d_scores = jnp.concatenate(probs, axis=1), jnp.concatenate(d_scores, axis=1)
    return (
        dot_nn(probs, v_two).astype(bf16),
        dot_nn(d_scores, k_two),
        unstacked(dot_tn(d_scores, q_half)),
        unstacked(dot_tn(probs, grad_att)).astype(bf16),
    )


def layer_kernel(
    core_ref, counts_ref, rows_ref, up_ref, mine_ref, theirs_ref,
    d_mine_ref, d_theirs_ref, out_mine_ref, out_theirs_ref,
    normed_ref, masked_ref, att_ref,
):
    step = pl.program_id(0)
    tokens = rows_ref.shape[0]
    width = mine_ref.shape[1] // 4
    own = pl.multiple_of(core_ref[0] * width, width)
    other = pl.multiple_of(width - own, width)
    here = pl.ds(pl.multiple_of(step * tokens, tokens), tokens)
    ones = head_ones(width)

    rows = rows_ref[...].astype(f32)
    inv_rms = lax.rsqrt(jnp.mean(rows * rows, axis=1, keepdims=True) + tiny_eps)
    normed = (rows * inv_rms).astype(bf16)
    normed_ref[here, :] = normed
    slot = lax.broadcasted_iota(jnp.int32, up_ref.shape, 0) // ROW
    masked_ref[here, :] = jnp.where(slot < counts_ref[step], up_ref[...], jnp.zeros((), bf16))

    row_of = lax.broadcasted_iota(jnp.int32, (SPAN, 2 * SPAN), 0) // ROW
    col_of = lax.broadcasted_iota(jnp.int32, (SPAN, 2 * SPAN), 1) % SPAN // ROW
    same_row = row_of == col_of

    for weight_ref, d_ref, heads, place in (
        (theirs_ref, d_theirs_ref, other, 1),
        (mine_ref, d_mine_ref, own, 0),
    ):
        qkv = dot_nn(normed, weight_ref[:, : 3 * width])
        query, key = qkv[:, :width], qkv[:, width : 2 * width]
        q_scale = lax.rsqrt(head_means(query * query, ones) + tiny_eps)
        k_scale = lax.rsqrt(head_means(key * key, ones) + tiny_eps)
        q_unit, k_unit = query * q_scale, key * k_scale
        q_half, k_half = q_unit.astype(bf16), k_unit.astype(bf16)
        v_half = qkv[:, 2 * width :].astype(bf16)
        grad_att = (
            dot_nt(masked_ref[here, pl.ds(own, width)], mine_ref[pl.ds(heads, width), 3 * width :])
            + dot_nt(
                masked_ref[here, pl.ds(other, width)], theirs_ref[pl.ds(heads, width), 3 * width :]
            )
        ).astype(bf16)
        spans = []
        for low in range(0, tokens, SPAN):
            pairs = []
            for left in range(0, width, 2 * HEAD):
                at = (slice(low, low + SPAN), slice(left, left + 2 * HEAD))
                pairs.append(
                    attention(q_half[at], k_half[at], v_half[at], grad_att[at], same_row)
                )
            spans.append([jnp.concatenate(part, axis=1) for part in zip(*pairs)])
        attended, d_query, d_key, d_value = (
            jnp.concatenate(part, axis=0) for part in zip(*spans)
        )
        att_ref[here, place * width : (place + 1) * width] = attended
        d_ref[here, :width] = (
            q_scale * (d_query - q_unit * head_means(q_unit * d_query, ones))
        ).astype(bf16)
        d_ref[here, width : 2 * width] = (
            k_scale * (d_key - k_unit * head_means(k_unit * d_key, ones))
        ).astype(bf16)
        d_ref[here, 2 * width :] = d_value

    @pl.when(step == pl.num_programs(0) - 1)
    def _():
        for d_ref, out_ref, cols in (
            (d_theirs_ref, out_theirs_ref, other),
            (d_mine_ref, out_mine_ref, own),
        ):
            out_ref[:, : 3 * width] = dot_tn(normed_ref[...], d_ref[...]).astype(bf16)
            grads = masked_ref[:, pl.ds(cols, width)]
            for heads, place in ((own, 0), (other, 1)):
                part = att_ref[:, place * width : (place + 1) * width]
                out_ref[pl.ds(heads, width), 3 * width :] = dot_tn(part, grads).astype(bf16)


def layer(core, counts, rows, up, mine, theirs):
    tokens, depth = rows.shape
    views = counts.shape[0]
    width = mine.shape[1] // 4
    smem = pl.BlockSpec(memory_space=pltpu.SMEM)
    part = pl.BlockSpec((tokens // views, depth), lambda i: (i, 0))

    def whole(shape):
        return pl.BlockSpec(shape, lambda i: (0, 0))

    outs = [(tokens, 3 * width)] * 2 + [(depth, 4 * width)] * 2
    return pl.pallas_call(
        layer_kernel,
        grid=(views,),
        in_specs=[smem, smem, part, part, whole(mine.shape), whole(theirs.shape)],
        out_specs=[whole(shape) for shape in outs],
        out_shape=[jax.ShapeDtypeStruct(shape, bf16) for shape in outs],
        scratch_shapes=[pltpu.VMEM((tokens, depth), bf16)] * 3,
        compiler_params=pltpu.CompilerParams(vmem_limit_bytes=40 * 1024 * 1024),
        cost_estimate=pl.CostEstimate(
            flops=20 * tokens * depth * depth, bytes_accessed=6 << 20, transcendentals=0
        ),
        name="attention_layer",
    )(core, counts, rows, up, mine, theirs)


MESH_AXES = ("y", "core", "x", "z")
PEERS = ("x", "z")


def swapped(block):
    return lax.ppermute(block, "core", [(0, 1), (1, 0)])


def sent(blocks, axis):
    return lax.all_to_all(blocks, axis, split_axis=0, concat_axis=0, tiled=True)


def shared_sum(terms, axis):
    count = lax.axis_size(axis)
    blocks = terms.reshape(count, terms.shape[0] // count, terms.shape[1])
    return jnp.sum(sent(blocks, axis).astype(f32), axis=0).astype(bf16)


def copies_kernel(core_ref, *refs):
    *weight_refs, out_ref = refs
    width = weight_refs[0].shape[1] // 2
    own = pl.multiple_of(core_ref[0] * width, width)
    for index, weight_ref in enumerate(weight_refs):
        block = weight_ref[:, pl.ds(own, width)]
        out_ref[:, :, index * width : (index + 1) * width] = jnp.broadcast_to(
            block[None], (out_ref.shape[0],) + block.shape
        )


def weight_copies(core, weights, count):
    rows, width = weights[0].shape
    parts = 4
    out = (count, rows, 2 * width)
    return pl.pallas_call(
        copies_kernel,
        grid=(parts,),
        in_specs=[pl.BlockSpec(memory_space=pltpu.SMEM)]
        + [pl.BlockSpec((rows, width), lambda i: (0, 0))] * 4,
        out_specs=pl.BlockSpec((count // parts,) + out[1:], lambda i: (i, 0, 0)),
        out_shape=jax.ShapeDtypeStruct(out, bf16),
        name="weight_copies",
    )(core, *weights)


def split_kernel(core_ref, mine_ref, theirs_ref, *out_refs):
    width = mine_ref.shape[1] // 4
    own = pl.multiple_of(core_ref[0] * width, width)
    other = pl.multiple_of(width - own, width)
    for index, out_ref in enumerate(out_refs):
        cols = slice(index * width, (index + 1) * width)
        out_ref[:, pl.ds(own, width)] = mine_ref[:, cols]
        out_ref[:, pl.ds(other, width)] = theirs_ref[:, cols]


def split_weights(core, mine, theirs):
    rows, width = mine.shape
    vmem = pl.BlockSpec(memory_space=pltpu.VMEM)
    return pl.pallas_call(
        split_kernel,
        in_specs=[pl.BlockSpec(memory_space=pltpu.SMEM), vmem, vmem],
        out_specs=[vmem] * 4,
        out_shape=[jax.ShapeDtypeStruct((rows, width // 2), f32)] * 4,
        name="split_weights",
    )(core, mine, theirs)


def local(trace_rows, upstream, counts, w_query, w_key, w_value, w_out):
    core = lax.axis_index("core").reshape(1)
    view_count, most_rows, row_length, depth = trace_rows.shape
    tokens = view_count * most_rows * row_length
    view_counts = counts.reshape(view_count)

    copies = weight_copies(core, (w_query, w_key, w_value, w_out), lax.axis_size(PEERS))
    mine = sent(copies, PEERS).reshape(depth, -1)
    theirs = swapped(mine)

    rows, up = trace_rows.reshape(tokens, depth), upstream.reshape(tokens, depth)
    d_mine, d_theirs, out_mine, out_theirs = layer(core, view_counts, rows, up, mine, theirs)

    terms = out_mine.astype(f32) + swapped(out_theirs).astype(f32)
    total = shared_sum(shared_sum(terms.astype(bf16), "x"), "z")
    spread = jnp.broadcast_to(total[None], (lax.axis_size("y"),) + total.shape)
    total = jnp.sum(sent(spread, "y").astype(f32), axis=0)
    devices = math.prod(lax.axis_size(name) for name in MESH_AXES)
    total = total * (1.0 / math.sqrt(devices * tokens // 2))
    weight_grads = split_weights(core, total, swapped(total))

    used = d_mine.shape[1]
    grad_norm = dot_nt(d_mine, mine[:, :used]) + dot_nt(d_theirs, theirs[:, :used])
    rows = rows.astype(f32)
    inv_rms = lax.rsqrt(jnp.mean(rows * rows, axis=-1, keepdims=True) + tiny_eps)
    scaled = rows * inv_rms
    is_live = lax.iota(jnp.int32, most_rows)[None, :] < view_counts[:, None]
    is_live = jnp.repeat(is_live.reshape(-1), row_length)[:, None]
    masked = jnp.where(is_live, up, jnp.zeros((), up.dtype)).astype(f32)
    done = masked + inv_rms * (
        grad_norm - scaled * jnp.mean(scaled * grad_norm, axis=-1, keepdims=True)
    )
    return (done.astype(bf16).reshape(trace_rows.shape), *weight_grads)


def solution(mesh):
    fine_mesh = jax.sharding.Mesh(mesh.devices.reshape(8, 2, 4, 8), MESH_AXES)
    every, peer = P(MESH_AXES), P(PEERS, None)
    in_specs = (every, every, P(("y", "core"), PEERS), peer, peer, peer, peer)
    out_specs = (every, peer, peer, peer, peer)
    return jax.shard_map(
        local, mesh=fine_mesh, in_specs=in_specs, out_specs=out_specs, check_vma=False
    )
```

time: 143 us -> 131 us (0.916)
  blocking collectives: 0 us -> 38.5 us
  waiting for transfers between devices: 54.9 us -> 32.7 us
  Pallas kernels: 0 us -> 15.3 us
  local copies, waits for them, and re-layouts: 16.5 us -> 1.71 us
  starting transfers between devices: 42.7 us -> 29.6 us
  matrix products: 16.4 us -> 5.68 us
  other arithmetic: 10.4 us -> 6.32 us
    all_to_all x0 -> x1, blocking collectives: none -> 38.5 us  [sent(): return lax.all_to_all(blocks, axis, split_axis=0, concat_axis=0, tiled=True)]
    all_to_all x3, waiting for transfers between devices: 51.9 us -> 28.2 us  [sent(): return lax.all_to_all(blocks, axis, split_axis=0, concat_axis=0, tiled=True)]
    pallas_call x0 -> x3, Pallas kernels: none -> 15.3 us  [the longest x1 11.5 us: layer(): pl.pallas_call(layer_kernel, grid=(views,), in_specs=[smem, smem, part, p...]
    all_to_all x3, starting transfers between devices: 25.7 us -> 14.5 us  [sent(): return lax.all_to_all(blocks, axis, split_axis=0, concat_axis=0, tiled=True)]
    dot_general x17 -> x2, matrix products: 16.4 us -> 5.68 us  [dot_nt(): lax.dot_general(a, b, (((1,), (1,)), ((), ())), preferred_element_type=f32)]
    reshape x5 -> x0, local copies, waits for them, and re-layouts: 8.42 us -> none  [the longest x2 4.86 us: layer_backward(): values_full.astype(jnp.bfloat16)]
    convert_element_type x3 -> x0, local copies, waits for them, and re-layouts: 2.15 us -> none  [the longest x1 1.32 us: reduce_terms(): total = (mine + arrived.astype(jnp.float32)).astype(jnp.bfloat16)]
    unnamed x38 -> x14, local copies, waits for them, and re-layouts: 2.75 us -> 0.65 us
  transfers between devices with their start and end apart: 6 -> 6, of which waited for: 5 -> 5; matrix products, arithmetic and copies ran while one was open for 8% -> 7% of each run, Pallas kernels for 0% -> 0%
where the time goes in v4:
time: 131 us
  blocking collectives  38.5 us (29%)
  waiting for transfers between devices  32.7 us (25%)
  starting transfers between devices  29.6 us (23%)
  Pallas kernels  15.3 us (12%)
  other arithmetic  6.32 us (5%)
  matrix products  5.68 us (4%)
  local copies, waits for them, and re-layouts  1.71 us (1%)
    all_to_all x1, blocking collectives, sent(): return lax.all_to_all(blocks, axis, split_axis=0, concat_axis=0, tiled=True)  38.5 us
    all_to_all x3, waiting for transfers between devices, sent(): return lax.all_to_all(blocks, axis, split_axis=0, concat_axis=0, tiled=True)  28.2 us
    ppermute x3, starting transfers between devices, swapped(): return lax.ppermute(block, 'core', [(0, 1), (1, 0)])  15.1 us
    all_to_all x3, starting transfers between devices, sent(): return lax.all_to_all(blocks, axis, split_axis=0, concat_axis=0, tiled=True)  14.5 us
    pallas_call x1, Pallas kernels, layer(): pl.pallas_call(layer_kernel, grid=(views,), in_specs=[smem, smem, part, p...  11.5 us
    dot_general x2, matrix products, dot_nt(): lax.dot_general(a, b, (((1,), (1,)), ((), ())), preferred_element_type=f32)  5.68 us
    ppermute x3, waiting for transfers between devices, swapped(): return lax.ppermute(block, 'core', [(0, 1), (1, 0)])  4.53 us
  transfers between devices with their start and end apart: 6, of which 5 were waited for; matrix products, arithmetic and copies ran while one was open for 7% of the time, Pallas kernels for 0%

profile of v4, /device:TPU:1, one launch (start us, length us, event | category | flops | bytes accessed | tf_op | source)
XLA Modules:
  0.0 130.6 jit_solution(6101890585150097904)
XLA Ops:
  0.6 2.3 %weight_copies.1 = bf16[32,16,1024]{2,1,0:T(8,128)(2,1)} custom-call(s32[1]{0:T(128)} %bitcast.2.core_ref, bf16[16,512]{1,0:T(8,128)(2,1)} %refs_0_.1, bf16[16,512]{1,0:T(8,128)(2,1)} %refs_1_.1, bf16[16,512]{1,0:T(8,128)(2,1)} %refs_2_.1, bf16[16,512]{1,0:T(8,128)(2,1)} %refs_3_.1), custom_call_target="tpu_custom_call" | custom-call | tf_op jit(solution)/shard_map/weight_copies/pallas_call | solution.py:205
  3.0 0.0 copy-start
  3.0 0.0 copy-start.2
  3.0 0.0 copy-start.4
  3.0 38.5 %all_to_all.20 = bf16[32,16,1024]{2,1,0:T(8,128)(2,1)S(1)} all-to-all(bf16[32,16,1024]{2,1,0:T(8,128)(2,1)} %weight_copies.1), channel_id=1, replica_groups=mesh['y'=8,'core'=2,'x'=4,'z'=8] {'x','z'}, dimensions={0} | all-to-all | bytes 2097152 | tf_op jit(solution)/shard_map/all_to_all | solution.py:181
  41.5 6.9 %collective-permute-start = (bf16[512,1024]{1,0:T(8,128)(2,1)S(1)}, bf16[512,1024]{1,0:T(8,128)(2,1)S(1)}, u32[]{:S(2)}, u32[]{:S(2)}) collective-permute-start(bf16[512,1024]{1,0:T(8,128)(2,1)S(1)} %bitcast.14), channel_id=1, source_target_pairs={{0,32},{32,0},{1,33},{33,1},{2,34},{34,2},{3,35},{35,3},{4,36},{36... | collective-permute-start | bytes 3145736 | tf_op jit(solution)/shard_map/ppermute | solution.py:177
  48.4 2.3 %collective-permute-done.theirs_ref = bf16[512,1024]{1,0:T(8,128)(2,1)S(1)} collective-permute-done((bf16[512,1024]{1,0:T(8,128)(2,1)S(1)}, bf16[512,1024]{1,0:T(8,128)(2,1)S(1)}, u32[]{:S(2)}, u32[]{:S(2)}) %collective-permute-start) | collective-permute-done | bytes 1048608 | tf_op jit(solution)/shard_map/ppermute | solution.py:177
  50.6 0.0 copy-start.1
  50.6 0.0 copy-done
  50.6 0.0 copy-done.2
  50.6 0.0 copy-done.4
  50.6 11.5 %attention_layer.1 = (bf16[512,768]{1,0:T(8,128)(2,1)S(1)}, bf16[512,768]{1,0:T(8,128)(2,1)S(1)}, bf16[512,1024]{1,0:T(8,128)(2,1)S(1)}, bf16[512,1024]{1,0:T(8,128)(2,1)S(1)}) custom-call(s32[1]{0:T(128)} %bitcast.2.core_ref, s32[2]{0:T(128)S(1)} %bitcast.18, bf16[512,512]{1,0:T(8,128)(2,1)S(1)} %bitcast.13, bf16[512,512]{1,0:T(8,128)(2,1)S(1)} %bitcast.17, ...), custom_call_target="tpu_custom_call" | custom-call | flops 2684354560 | bytes 6291456 | tf_op jit(solution)/shard_map/attention_layer/pallas_call | solution.py:157
  62.1 0.0 copy-done.1
  62.1 2.3 %collective-permute-start.1 = (bf16[512,1024]{1,0:T(8,128)(2,1)S(1)}, bf16[512,1024]{1,0:T(8,128)(2,1)S(1)}, u32[]{:S(2)}, u32[]{:S(2)}) collective-permute-start(bf16[512,1024]{1,0:T(8,128)(2,1)S(1)} %get-tuple-element.16), channel_id=1, source_target_pairs={{0,32},{32,0},{1,33},{33,1},{2,34},{34,2},{3,35},{35,3},{4,36},{36... | collective-permute-start | bytes 3145736 | tf_op jit(solution)/shard_map/ppermute | solution.py:177
  64.4 2.3 %collective-permute-done.1 = bf16[512,1024]{1,0:T(8,128)(2,1)S(1)} collective-permute-done((bf16[512,1024]{1,0:T(8,128)(2,1)S(1)}, bf16[512,1024]{1,0:T(8,128)(2,1)S(1)}, u32[]{:S(2)}, u32[]{:S(2)}) %collective-permute-start.1) | collective-permute-done | bytes 1048608 | tf_op jit(solution)/shard_map/ppermute | solution.py:177
  66.7 1.4 %add_convert_fusion = bf16[512,1024]{1,0:T(8,128)(2,1)} fusion(bf16[512,1024]{1,0:T(8,128)(2,1)S(1)} %collective-permute-done.1, bf16[512,1024]{1,0:T(8,128)(2,1)S(1)} %get-tuple-element.15), kind=kLoop, calls=%fused_computation | loop fusion | flops 2097152 | bytes 3145728 | tf_op jit(solution)/shard_map/convert_element_type | solution.py:252
  68.1 4.2 %all-to-all-start.1 = ((bf16[4,128,1024]{2,1,0:T(8,128)(2,1)}), bf16[4,128,1024]{2,1,0:T(8,128)(2,1)}, u32[]{:S(2)}, u32[]{:S(2)}) async-start(bf16[4,128,1024]{2,1,0:T(8,128)(2,1)} %bitcast.20), calls=%async_computation.1 | async-start | bytes 2097152 | tf_op jit(solution)/shard_map/all_to_all | solution.py:181
  72.3 0.2 multiply_reduce_fusion.1
  72.5 0.1 rsqrt.12
  72.6 14.6 %all-to-all-done.1 = bf16[4,128,1024]{2,1,0:T(8,128)(2,1)} async-done(((bf16[4,128,1024]{2,1,0:T(8,128)(2,1)}), bf16[4,128,1024]{2,1,0:T(8,128)(2,1)}, u32[]{:S(2)}, u32[]{:S(2)}) %all-to-all-start.1) | async-done | bytes 1048608 | tf_op jit(solution)/shard_map/all_to_all | solution.py:181
  87.2 2.2 %reduce_sum.53 = bf16[128,1024]{1,0:T(8,128)(2,1)} reduce(bf16[4,128,1024]{2,1,0:T(8,128)(2,1)} %all-to-all-done.1, bf16[]{:T(256)} %constant.6.clone.1), dimensions={0}, to_apply=%region_2.0 | reduce | flops 393216 | bytes 1310722 | tf_op jit(solution)/shard_map/reduce_sum | solution.py:187
  89.4 3.4 %all-to-all-start.2 = ((bf16[8,16,1024]{2,1,0:T(8,128)(2,1)}), bf16[8,16,1024]{2,1,0:T(8,128)(2,1)S(1)}, u32[]{:S(2)}, u32[]{:S(2)}) async-start(bf16[8,16,1024]{2,1,0:T(8,128)(2,1)} %bitcast.7), calls=%async_computation.2 | async-start | bytes 524288 | tf_op jit(solution)/shard_map/all_to_all | solution.py:181
  92.8 0.1 iota_compare_fusion
  92.9 0.1 lt.23
  93.0 0.1 broadcast_in_dim.26
  93.1 0.1 broadcast_in_dim.27
  93.2 2.7 %fusion = f32[512,512]{1,0:T(8,128)} fusion(bf16[512,768]{1,0:T(8,128)(2,1)S(1)} %get-tuple-element.14, bf16[512,1024]{1,0:T(8,128)(2,1)} %copy-done.1), kind=kOutput, calls=%fused_computation.6 | convolution fusion | flops 402653184 | bytes 2621440 | tf_op jit(solution)/shard_map/dot_general | solution.py:22
  95.9 7.1 %all-to-all-done.2 = bf16[8,16,1024]{2,1,0:T(8,128)(2,1)S(1)} async-done(((bf16[8,16,1024]{2,1,0:T(8,128)(2,1)}), bf16[8,16,1024]{2,1,0:T(8,128)(2,1)S(1)}, u32[]{:S(2)}, u32[]{:S(2)}) %all-to-all-start.2) | async-done | bytes 262176 | tf_op jit(solution)/shard_map/all_to_all | solution.py:181
  103.1 0.7 broadcast_in_dim.30
  103.8 6.8 %all-to-all-start.3 = ((bf16[8,16,1024]{2,1,0:T(8,128)(2,1)}), bf16[8,16,1024]{2,1,0:T(8,128)(2,1)S(1)}, u32[]{:S(2)}, u32[]{:S(2)}) async-start(bf16[8,16,1024]{2,1,0:T(8,128)(2,1)} %broadcast_in_dim.30), calls=%async_computation.3 | async-start | bytes 524288 | tf_op jit(solution)/shard_map/all_to_all | solution.py:181
  110.6 0.0 copy-start.3
  110.6 2.9 %multiply_reduce_fusion = (f32[512]{0:T(512)S(1)}, f32[512,512]{1,0:T(8,128)}) fusion(f32[512]{0:T(512)S(1)} %rsqrt.12, bf16[2,8,32,512]{3,2,1,0:T(8,128)(2,1)S(1)} %copy-done, f32[512,512]{1,0:T(8,128)} %fusion, bf16[512,768]{1,0:T(8,128)(2,1)S(1)} %get-tuple-element.13, bf16[512,1024]{1,0:T(8,128)(2,1)S(1)} %bitcast.16), kind=kOutput, calls=%fused_computation.3 | convolution fusion | flops 403963392 | bytes 4198400 | tf_op jit(solution)/shard_map/dot_general | solution.py:22
  113.5 6.4 %all-to-all-done.3 = bf16[8,16,1024]{2,1,0:T(8,128)(2,1)S(1)} async-done(((bf16[8,16,1024]{2,1,0:T(8,128)(2,1)}), bf16[8,16,1024]{2,1,0:T(8,128)(2,1)S(1)}, u32[]{:S(2)}, u32[]{:S(2)}) %all-to-all-start.3) | async-done | bytes 262176 | tf_op jit(solution)/shard_map/all_to_all | solution.py:181
  120.0 0.0 copy-start.5
  120.0 6.0 %collective-permute-start.2 = (f32[16,1024]{1,0:T(8,128)S(1)}, f32[16,1024]{1,0:T(8,128)S(1)}, u32[]{:S(2)}, u32[]{:S(2)}) collective-permute-start(f32[16,1024]{1,0:T(8,128)S(1)} %broadcast_multiply_fusion.mine_ref), channel_id=1, source_target_pairs={{0,32},{32,0},{1,33},{33,1},{2,34},{34,2},{3,35},{35,3},{4,36},{36... | collective-permute-start | bytes 196616 | tf_op jit(solution)/shard_map/ppermute | solution.py:177
  126.0 0.0 copy-done.3
  126.0 2.4 %add_convert_fusion.1 = bf16[512,512]{1,0:T(8,128)(2,1)} fusion(f32[512,512]{1,0:T(8,128)} %get-tuple-element.22, f32[512]{0:T(512)S(1)} %broadcast_multiply_fusion.1, f32[512]{0:T(512)S(1)} %rsqrt.12, pred[512]{0:T(512)(128)(4,1)S(1)} %broadcast_in_dim.27, bf16[2,8,32,512]{3,2,1,0:T(8,128)(2,1)S(1)} %copy-done, bf16[2,8,32,512]{3,2,1,0:T(8,128)(2,1)S(1)} %copy-done.3), kind=kLoop, calls=%fused_computation.2 | loop fusion | flops 2359296 | bytes 2626048 | tf_op jit(solution)/shard_map/convert_element_type | solution.py:270
  128.4 0.0 copy-done.5
  128.4 0.0 collective-permute-done.2.theirs_ref
  128.4 0.0 copy-start.6
  128.4 0.6 copy-done.6
  129.0 1.5 %split_weights.1 = (f32[16,512]{1,0:T(8,128)}, f32[16,512]{1,0:T(8,128)}, f32[16,512]{1,0:T(8,128)}, f32[16,512]{1,0:T(8,128)}) custom-call(s32[1]{0:T(128)} %bitcast.2.core_ref, f32[16,1024]{1,0:T(8,128)} %copy-done.5, f32[16,1024]{1,0:T(8,128)} %copy-done.6), custom_call_target="tpu_custom_call" | custom-call | tf_op jit(solution)/shard_map/split_weights/pallas_call | solution.py:229
  (5 shorter events, 0.1 us)
Async XLA Ops:
  3.0 47.6 %copy-start = (bf16[2,8,32,512]{3,2,1,0:T(8,128)(2,1)S(1)}, bf16[2,8,32,512]{3,2,1,0:T(8,128)(2,1)}, u32[]{:S(2)}) copy-start(bf16[2,8,32,512]{3,2,1,0:T(8,128)(2,1)} %param.7) | copy-start | bytes 1572868
  3.0 47.6 %copy-start.2 = (bf16[2,8,32,512]{3,2,1,0:T(8,128)(2,1)S(1)}, bf16[2,8,32,512]{3,2,1,0:T(8,128)(2,1)}, u32[]{:S(2)}) copy-start(bf16[2,8,32,512]{3,2,1,0:T(8,128)(2,1)} %param.8) | copy-start | bytes 1572868
  3.0 47.6 %copy-start.4 = (s32[1,2]{1,0:T(1,128)S(1)}, s32[1,2]{1,0:T(1,128)}, u32[]{:S(2)}) copy-start(s32[1,2]{1,0:T(1,128)} %param.9) | copy-start | bytes 28
  41.5 9.1 %collective-permute-start = (bf16[512,1024]{1,0:T(8,128)(2,1)S(1)}, bf16[512,1024]{1,0:T(8,128)(2,1)S(1)}, u32[]{:S(2)}, u32[]{:S(2)}) collective-permute-start(bf16[512,1024]{1,0:T(8,128)(2,1)S(1)} %bitcast.14), channel_id=1, source_target_pairs={{0,32},{32,0},{1,33},{33,1},{2,34},{34,2},{3,35},{35,3},{4,36},{36... | collective-permute-start | bytes 3145736 | tf_op jit(solution)/shard_map/ppermute | solution.py:177
  50.6 11.5 %copy-start.1 = (bf16[512,1024]{1,0:T(8,128)(2,1)}, bf16[512,1024]{1,0:T(8,128)(2,1)S(1)}, u32[]{:S(2)}) copy-start(bf16[512,1024]{1,0:T(8,128)(2,1)S(1)} %collective-permute-done.theirs_ref) | copy-start | bytes 3145732
  62.1 4.6 %collective-permute-start.1 = (bf16[512,1024]{1,0:T(8,128)(2,1)S(1)}, bf16[512,1024]{1,0:T(8,128)(2,1)S(1)}, u32[]{:S(2)}, u32[]{:S(2)}) collective-permute-start(bf16[512,1024]{1,0:T(8,128)(2,1)S(1)} %get-tuple-element.16), channel_id=1, source_target_pairs={{0,32},{32,0},{1,33},{33,1},{2,34},{34,2},{3,35},{35,3},{4,36},{36... | collective-permute-start | bytes 3145736 | tf_op jit(solution)/shard_map/ppermute | solution.py:177
  68.1 19.2 %all-to-all-start.1 = ((bf16[4,128,1024]{2,1,0:T(8,128)(2,1)}), bf16[4,128,1024]{2,1,0:T(8,128)(2,1)}, u32[]{:S(2)}, u32[]{:S(2)}) async-start(bf16[4,128,1024]{2,1,0:T(8,128)(2,1)} %bitcast.20), calls=%async_computation.1 | async-start | bytes 2097152 | tf_op jit(solution)/shard_map/all_to_all | solution.py:181
  89.4 13.6 %all-to-all-start.2 = ((bf16[8,16,1024]{2,1,0:T(8,128)(2,1)}), bf16[8,16,1024]{2,1,0:T(8,128)(2,1)S(1)}, u32[]{:S(2)}, u32[]{:S(2)}) async-start(bf16[8,16,1024]{2,1,0:T(8,128)(2,1)} %bitcast.7), calls=%async_computation.2 | async-start | bytes 524288 | tf_op jit(solution)/shard_map/all_to_all | solution.py:181
  103.8 16.2 %all-to-all-start.3 = ((bf16[8,16,1024]{2,1,0:T(8,128)(2,1)}), bf16[8,16,1024]{2,1,0:T(8,128)(2,1)S(1)}, u32[]{:S(2)}, u32[]{:S(2)}) async-start(bf16[8,16,1024]{2,1,0:T(8,128)(2,1)} %broadcast_in_dim.30), calls=%async_computation.3 | async-start | bytes 524288 | tf_op jit(solution)/shard_map/all_to_all | solution.py:181
  110.6 15.4 %copy-start.3 = (bf16[2,8,32,512]{3,2,1,0:T(8,128)(2,1)S(1)}, bf16[2,8,32,512]{3,2,1,0:T(8,128)(2,1)}, u32[]{:S(2)}) copy-start(bf16[2,8,32,512]{3,2,1,0:T(8,128)(2,1)} %param.8) | copy-start | bytes 1572868
  120.0 8.4 %copy-start.5 = (f32[16,1024]{1,0:T(8,128)}, f32[16,1024]{1,0:T(8,128)S(1)}, u32[]{:S(2)}) copy-start(f32[16,1024]{1,0:T(8,128)S(1)} %broadcast_multiply_fusion.mine_ref) | copy-start | bytes 196612
  120.0 8.4 %collective-permute-start.2 = (f32[16,1024]{1,0:T(8,128)S(1)}, f32[16,1024]{1,0:T(8,128)S(1)}, u32[]{:S(2)}, u32[]{:S(2)}) collective-permute-start(f32[16,1024]{1,0:T(8,128)S(1)} %broadcast_multiply_fusion.mine_ref), channel_id=1, source_target_pairs={{0,32},{32,0},{1,33},{33,1},{2,34},{34,2},{3,35},{35,3},{4,36},{36... | collective-permute-start | bytes 196616 | tf_op jit(solution)/shard_map/ppermute | solution.py:177
  128.4 0.6 copy-start.6

commit v5 on v4

--- a/solution.py
+++ b/solution.py
@@ -1,3 +1,4 @@
+import functools
 import math
 import jax
 import jax.numpy as jnp
@@ -69,14 +70,15 @@
 
 
 def layer_kernel(
-    core_ref, counts_ref, rows_ref, up_ref, mine_ref, theirs_ref,
+    place_ref, counts_ref, rows_ref, up_ref, mine_ref, theirs_ref,
     d_mine_ref, d_theirs_ref, out_mine_ref, out_theirs_ref,
     normed_ref, masked_ref, att_ref,
 ):
     step = pl.program_id(0)
     tokens = rows_ref.shape[0]
-    width = mine_ref.shape[1] // 4
-    own = pl.multiple_of(core_ref[0] * width, width)
+    depth = rows_ref.shape[1]
+    width = depth // 2
+    own = pl.multiple_of(place_ref[0] * width, width)
     other = pl.multiple_of(width - own, width)
     here = pl.ds(pl.multiple_of(step * tokens, tokens), tokens)
     ones = head_ones(width)
@@ -96,17 +98,17 @@
         (theirs_ref, d_theirs_ref, other, 1),
         (mine_ref, d_mine_ref, own, 0),
     ):
-        qkv = dot_nn(normed, weight_ref[:, : 3 * width])
-        query, key = qkv[:, :width], qkv[:, width : 2 * width]
+        query_key = dot_nn(normed, weight_ref[:depth])
+        query, key = query_key[:, :width], query_key[:, width:]
         q_scale = lax.rsqrt(head_means(query * query, ones) + tiny_eps)
         k_scale = lax.rsqrt(head_means(key * key, ones) + tiny_eps)
         q_unit, k_unit = query * q_scale, key * k_scale
         q_half, k_half = q_unit.astype(bf16), k_unit.astype(bf16)
-        v_half = qkv[:, 2 * width :].astype(bf16)
+        v_half = dot_nn(normed, weight_ref[depth:, :width]).astype(bf16)
         grad_att = (
-            dot_nt(masked_ref[here, pl.ds(own, width)], mine_ref[pl.ds(heads, width), 3 * width :])
+            dot_nt(masked_ref[here, pl.ds(own, width)], mine_ref[pl.ds(depth + heads, width), width:])
             + dot_nt(
-                masked_ref[here, pl.ds(other, width)], theirs_ref[pl.ds(heads, width), 3 * width :]
+                masked_ref[here, pl.ds(other, width)], theirs_ref[pl.ds(depth + heads, width), width:]
             )
         ).astype(bf16)
         spans = []
@@ -136,24 +138,26 @@
             (d_theirs_ref, out_theirs_ref, other),
             (d_mine_ref, out_mine_ref, own),
         ):
-            out_ref[:, : 3 * width] = dot_tn(normed_ref[...], d_ref[...]).astype(bf16)
+            terms = dot_tn(normed_ref[...], d_ref[...]).astype(bf16)
+            out_ref[:depth, :] = terms[:, :depth]
+            out_ref[depth:, :width] = terms[:, depth:]
             grads = masked_ref[:, pl.ds(cols, width)]
             for heads, place in ((own, 0), (other, 1)):
                 part = att_ref[:, place * width : (place + 1) * width]
-                out_ref[pl.ds(heads, width), 3 * width :] = dot_tn(part, grads).astype(bf16)
-
-
-def layer(core, counts, rows, up, mine, theirs):
+                out_ref[pl.ds(depth + heads, width), width:] = dot_tn(part, grads).astype(bf16)
+
+
+def layer(place, counts, rows, up, mine, theirs):
     tokens, depth = rows.shape
     views = counts.shape[0]
-    width = mine.shape[1] // 4
+    width = depth // 2
     smem = pl.BlockSpec(memory_space=pltpu.SMEM)
     part = pl.BlockSpec((tokens // views, depth), lambda i: (i, 0))
 
     def whole(shape):
         return pl.BlockSpec(shape, lambda i: (0, 0))
 
-    outs = [(tokens, 3 * width)] * 2 + [(depth, 4 * width)] * 2
+    outs = [(tokens, 3 * width)] * 2 + [(2 * depth, depth)] * 2
     return pl.pallas_call(
         layer_kernel,
         grid=(views,),
@@ -166,11 +170,12 @@
             flops=20 * tokens * depth * depth, bytes_accessed=6 << 20, transcendentals=0
         ),
         name="attention_layer",
-    )(core, counts, rows, up, mine, theirs)
-
-
-MESH_AXES = ("y", "core", "x", "z")
-PEERS = ("x", "z")
+    )(place, counts, rows, up, mine, theirs)
+
+
+MESH_AXES = ("yh", "yl", "core", "x", "z")
+ALL_Y = ("yh", "yl")
+NEAR = ("yl", "x")
 
 
 def swapped(block):
@@ -181,83 +186,110 @@
     return lax.all_to_all(blocks, axis, split_axis=0, concat_axis=0, tiled=True)
 
 
-def shared_sum(terms, axis):
-    count = lax.axis_size(axis)
-    blocks = terms.reshape(count, terms.shape[0] // count, terms.shape[1])
-    return jnp.sum(sent(blocks, axis).astype(f32), axis=0).astype(bf16)
-
-
-def copies_kernel(core_ref, *refs):
+def blocks_of(terms, count):
+    return terms.reshape(count, terms.shape[0] // count, terms.shape[1])
+
+
+def copies_kernel(place_ref, *refs):
     *weight_refs, out_ref = refs
     width = weight_refs[0].shape[1] // 2
-    own = pl.multiple_of(core_ref[0] * width, width)
-    for index, weight_ref in enumerate(weight_refs):
-        block = weight_ref[:, pl.ds(own, width)]
-        out_ref[:, :, index * width : (index + 1) * width] = jnp.broadcast_to(
-            block[None], (out_ref.shape[0],) + block.shape
-        )
-
-
-def weight_copies(core, weights, count):
-    rows, width = weights[0].shape
-    parts = 4
-    out = (count, rows, 2 * width)
+    own = pl.multiple_of(place_ref[0] * width, width)
+    for yl in range(2):
+
+        @pl.when(place_ref[1] == yl)
+        def _():
+            for index, weight_ref in enumerate(weight_refs[2 * yl : 2 * yl + 2]):
+                block = weight_ref[:, pl.ds(own, width)]
+                out_ref[:, :, index * width : (index + 1) * width] = jnp.broadcast_to(
+                    block[None], (out_ref.shape[0],) + block.shape
+                )
+
+
+def weight_copies(place, weights, count):
+    vmem = pl.BlockSpec(memory_space=pltpu.VMEM)
     return pl.pallas_call(
         copies_kernel,
+        in_specs=[pl.BlockSpec(memory_space=pltpu.SMEM)] + [vmem] * 4,
+        out_specs=vmem,
+        out_shape=jax.ShapeDtypeStruct((count,) + weights[0].shape, bf16),
+        name="weight_copies",
+    )(place, *weights)
+
+
+def sum_kernel(blocks_ref, out_ref):
+    total = jnp.sum(blocks_ref[...].astype(f32), axis=0).astype(bf16)
+    out_ref[...] = jnp.broadcast_to(total, out_ref.shape)
+
+
+def block_sum(blocks, parts, copies=None):
+    count, rows, width = blocks.shape
+    out = (rows // parts, width) if copies is None else (copies, rows // parts, width)
+    lead = (0,) * (len(out) - 2)
+    return pl.pallas_call(
+        sum_kernel,
         grid=(parts,),
-        in_specs=[pl.BlockSpec(memory_space=pltpu.SMEM)]
-        + [pl.BlockSpec((rows, width), lambda i: (0, 0))] * 4,
-        out_specs=pl.BlockSpec((count // parts,) + out[1:], lambda i: (i, 0, 0)),
-        out_shape=jax.ShapeDtypeStruct(out, bf16),
-        name="weight_copies",
-    )(core, *weights)
-
-
-def split_kernel(core_ref, mine_ref, theirs_ref, *out_refs):
-    width = mine_ref.shape[1] // 4
-    own = pl.multiple_of(core_ref[0] * width, width)
-    other = pl.multiple_of(width - own, width)
-    for index, out_ref in enumerate(out_refs):
-        cols = slice(index * width, (index + 1) * width)
-        out_ref[:, pl.ds(own, width)] = mine_ref[:, cols]
-        out_ref[:, pl.ds(other, width)] = theirs_ref[:, cols]
-
-
-def split_weights(core, mine, theirs):
-    rows, width = mine.shape
+        in_specs=[pl.BlockSpec((count, rows // parts, width), lambda i: (0, i, 0))],
+        out_specs=pl.BlockSpec(out, lambda i: lead + (i, 0)),
+        out_shape=jax.ShapeDtypeStruct(out[:-2] + (rows, width), bf16),
+        name="block_sum",
+    )(blocks)
+
+
+def final_kernel(scale, blocks_ref, *out_refs):
+    count, _, width = blocks_ref.shape
+    half = width // 2
+    for yl in range(2):
+        for core in range(2):
+            total = blocks_ref[2 * yl + core].astype(f32)
+            for yh in range(1, count // 4):
+                total = total + blocks_ref[4 * yh + 2 * yl + core].astype(f32)
+            total = total * scale
+            cols = slice(core * half, (core + 1) * half)
+            out_refs[2 * yl][:, cols] = total[:, :half]
+            out_refs[2 * yl + 1][:, cols] = total[:, half:]
+
+
+def final_sum(blocks, scale):
+    _, rows, width = blocks.shape
     vmem = pl.BlockSpec(memory_space=pltpu.VMEM)
     return pl.pallas_call(
-        split_kernel,
-        in_specs=[pl.BlockSpec(memory_space=pltpu.SMEM), vmem, vmem],
+        functools.partial(final_kernel, scale),
+        in_specs=[vmem],
         out_specs=[vmem] * 4,
-        out_shape=[jax.ShapeDtypeStruct((rows, width // 2), f32)] * 4,
-        name="split_weights",
-    )(core, mine, theirs)
+        out_shape=[jax.ShapeDtypeStruct((rows, width), f32)] * 4,
+        name="final_sum",
+    )(blocks)
 
 
 def local(trace_rows, upstream, counts, w_query, w_key, w_value, w_out):
-    core = lax.axis_index("core").reshape(1)
+    place = jnp.stack((lax.axis_index("core"), lax.axis_index("yl")))
     view_count, most_rows, row_length, depth = trace_rows.shape
     tokens = view_count * most_rows * row_length
     view_counts = counts.reshape(view_count)
 
-    copies = weight_copies(core, (w_query, w_key, w_value, w_out), lax.axis_size(PEERS))
-    mine = sent(copies, PEERS).reshape(depth, -1)
+    copies = weight_copies(place, (w_query, w_key, w_value, w_out), lax.axis_size("z"))
+    lines = sent(copies, "z").reshape(-1, depth)
+    lines = jnp.broadcast_to(lines[None], (lax.axis_size(NEAR),) + lines.shape)
+    mine = sent(lines, NEAR).reshape(-1, depth)
     theirs = swapped(mine)
 
     rows, up = trace_rows.reshape(tokens, depth), upstream.reshape(tokens, depth)
-    d_mine, d_theirs, out_mine, out_theirs = layer(core, view_counts, rows, up, mine, theirs)
-
-    terms = out_mine.astype(f32) + swapped(out_theirs).astype(f32)
-    total = shared_sum(shared_sum(terms.astype(bf16), "x"), "z")
-    spread = jnp.broadcast_to(total[None], (lax.axis_size("y"),) + total.shape)
-    total = jnp.sum(sent(spread, "y").astype(f32), axis=0)
+    d_mine, d_theirs, out_mine, out_theirs = layer(place, view_counts, rows, up, mine, theirs)
+
+    terms = (out_mine.astype(f32) + swapped(out_theirs).astype(f32)).astype(bf16)
+    total = block_sum(sent(blocks_of(terms, lax.axis_size(NEAR)), NEAR), 4)
+    total = sent(blocks_of(total, lax.axis_size("z")), "z")
+    total = block_sum(total, 1, lax.axis_size(ALL_Y + ("core",)))
     devices = math.prod(lax.axis_size(name) for name in MESH_AXES)
-    total = total * (1.0 / math.sqrt(devices * tokens // 2))
-    weight_grads = split_weights(core, total, swapped(total))
-
-    used = d_mine.shape[1]
-    grad_norm = dot_nt(d_mine, mine[:, :used]) + dot_nt(d_theirs, theirs[:, :used])
+    weight_grads = final_sum(
+        sent(total, ALL_Y + ("core",)), 1.0 / math.sqrt(devices * tokens // 2)
+    )
+
+    grad_norm = sum(
+        dot_nt(d[:, :depth], weights[:depth])
+        + dot_nt(d[:, depth:], weights[depth:, : depth // 2])
+        for d, weights in ((d_mine, mine), (d_theirs, theirs))
+    )
     rows = rows.astype(f32)
     inv_rms = lax.rsqrt(jnp.mean(rows * rows, axis=-1, keepdims=True) + tiny_eps)
     scaled = rows * inv_rms
@@ -271,9 +303,9 @@
 
 
 def solution(mesh):
-    fine_mesh = jax.sharding.Mesh(mesh.devices.reshape(8, 2, 4, 8), MESH_AXES)
-    every, peer = P(MESH_AXES), P(PEERS, None)
-    in_specs = (every, every, P(("y", "core"), PEERS), peer, peer, peer, peer)
+    fine_mesh = jax.sharding.Mesh(mesh.devices.reshape(4, 2, 2, 4, 8), MESH_AXES)
+    every, peer = P(MESH_AXES), P(("x", "z"), None)
+    in_specs = (every, every, P(("yh", "yl", "core"), ("x", "z")), peer, peer, peer, peer)
     out_specs = (every, peer, peer, peer, peer)
     return jax.shard_map(
         local, mesh=fine_mesh, in_specs=in_specs, out_specs=out_specs, check_vma=False

time: 131 us -> 124 us (0.947)
  starting transfers between devices: 29.6 us -> 24.4 us
  Pallas kernels: 15.3 us -> 19.4 us
  other arithmetic: 6.32 us -> 3.3 us
  blocking collectives: 38.5 us -> 36.1 us
  waiting for transfers between devices: 32.7 us -> 31.1 us
    ppermute x3 -> x2, starting transfers between devices: 15.1 us -> 8.27 us  [swapped(): return lax.ppermute(block, 'core', [(0, 1), (1, 0)])]
    pallas_call x2 -> x4, Pallas kernels: 3.87 us -> 7.92 us  [the longest x2 4.83 us: block_sum(): pl.pallas_call(sum_kernel, grid=(parts,), in_specs=[pl.BlockSpec((count,...]
    all_to_all x1 -> x2, blocking collectives: 38.5 us -> 36.1 us  [sent(): return lax.all_to_all(blocks, axis, split_axis=0, concat_axis=0, tiled=True)]
    reduce_sum x3 -> x0, other arithmetic: 2.27 us -> none  [the longest x2 2.23 us: shared_sum(): return jnp.sum(sent(blocks, axis).astype(f32), axis=0).astype(bf16)]
    all_to_all x3, starting transfers between devices: 14.5 us -> 16.1 us  [sent(): return lax.all_to_all(blocks, axis, split_axis=0, concat_axis=0, tiled=True)]
    all_to_all x3, waiting for transfers between devices: 28.2 us -> 26.6 us  [sent(): return lax.all_to_all(blocks, axis, split_axis=0, concat_axis=0, tiled=True)]
    dot_general x2 -> x4, matrix products: 5.68 us -> 5.1 us  [dot_nt(): lax.dot_general(a, b, (((1,), (1,)), ((), ())), preferred_element_type=f32)]
    ppermute x3 -> x2, waiting for transfers between devices: 4.53 us -> 4.53 us  [swapped(): return lax.ppermute(block, 'core', [(0, 1), (1, 0)])]
  transfers between devices with their start and end apart: 6 -> 5, of which waited for: 5 -> 5; matrix products, arithmetic and copies ran while one was open for 7% -> 6% of each run, Pallas kernels for 0% -> 0%
where the time goes in v5:
time: 124 us; the launch traced here: 123 us
  blocking collectives  36.1 us (29%)
  waiting for transfers between devices  31.1 us (25%)
  starting transfers between devices  24.4 us (20%)
  Pallas kernels  19.4 us (16%)
  matrix products  5.1 us (4%)
  other arithmetic  3.3 us (3%)
  local copies, waits for them, and re-layouts  2.64 us (2%)
    all_to_all x2, blocking collectives, sent(): return lax.all_to_all(blocks, axis, split_axis=0, concat_axis=0, tiled=True)  36.1 us
    all_to_all x3, waiting for transfers between devices, sent(): return lax.all_to_all(blocks, axis, split_axis=0, concat_axis=0, tiled=True)  26.6 us
    all_to_all x3, starting transfers between devices, sent(): return lax.all_to_all(blocks, axis, split_axis=0, concat_axis=0, tiled=True)  16.1 us
    pallas_call x1, Pallas kernels, layer(): pl.pallas_call(layer_kernel, grid=(views,), in_specs=[smem, smem, part, p...  11.4 us
    ppermute x2, starting transfers between devices, swapped(): return lax.ppermute(block, 'core', [(0, 1), (1, 0)])  8.27 us
    dot_general x4, matrix products, dot_nt(): lax.dot_general(a, b, (((1,), (1,)), ((), ())), preferred_element_type=f32)  5.1 us
    pallas_call x2, Pallas kernels, block_sum(): pl.pallas_call(sum_kernel, grid=(parts,), in_specs=[pl.BlockSpec((count,...  4.83 us
    ppermute x2, waiting for transfers between devices, swapped(): return lax.ppermute(block, 'core', [(0, 1), (1, 0)])  4.53 us
  transfers between devices with their start and end apart: 5, of which 5 were waited for; matrix products, arithmetic and copies ran while one was open for 6% of the time, Pallas kernels for 0%

profile of v5, /device:TPU:1, one launch (start us, length us, event | category | flops | bytes accessed | tf_op | source)
XLA Modules:
  0.0 122.8 jit_solution(11734778891283855005)
XLA Ops:
  0.6 0.6 pad_add_fusion.place_ref
  1.2 1.5 %weight_copies.1 = bf16[8,16,512]{2,1,0:T(8,128)(2,1)} custom-call(s32[2]{0:T(128)} %pad_add_fusion.place_ref, bf16[16,512]{1,0:T(8,128)(2,1)} %refs_0_.1, bf16[16,512]{1,0:T(8,128)(2,1)} %refs_1_.1, bf16[16,512]{1,0:T(8,128)(2,1)} %refs_2_.1, bf16[16,512]{1,0:T(8,128)(2,1)} %refs_3_.1), custom_call_target="tpu_custom_call" | custom-call | tf_op jit(solution)/shard_map/weight_copies/pallas_call | solution.py:210
  2.7 18.6 %all_to_all.25 = bf16[8,16,512]{2,1,0:T(8,128)(2,1)S(1)} all-to-all(bf16[8,16,512]{2,1,0:T(8,128)(2,1)} %weight_copies.1), channel_id=1, replica_groups=mesh['yh'=4,'yl'=2,'core'=2,'x'=4,'z'=8] {'z'}, dimensions={0} | all-to-all | bytes 262144 | tf_op jit(solution)/shard_map/all_to_all | solution.py:186
  21.3 0.1 broadcast_in_dim.32
  21.4 0.0 copy-start
  21.4 0.0 copy-start.3
  21.4 0.0 copy-start.5
  21.5 0.0 copy-start.6
  21.5 17.5 %all_to_all.26 = bf16[8,128,512]{2,1,0:T(8,128)(2,1)S(1)} all-to-all(bf16[8,128,512]{2,1,0:T(8,128)(2,1)S(1)} %broadcast_in_dim.32), channel_id=1, replica_groups=mesh['yh'=4,'yl'=2,'core'=2,'x'=4,'z'=8] {'yl','x'}, dimensions={0} | all-to-all | bytes 2097152 | tf_op jit(solution)/shard_map/all_to_all | solution.py:186
  39.0 6.0 %collective-permute-start = (bf16[1024,512]{1,0:T(8,128)(2,1)S(1)}, bf16[1024,512]{1,0:T(8,128)(2,1)S(1)}, u32[]{:S(2)}, u32[]{:S(2)}) collective-permute-start(bf16[1024,512]{1,0:T(8,128)(2,1)S(1)} %bitcast.16), channel_id=1, source_target_pairs={{0,32},{32,0},{1,33},{33,1},{2,34},{34,2},{3,35},{35,3},{4,36},{36... | collective-permute-start | bytes 3145736 | tf_op jit(solution)/shard_map/ppermute | solution.py:182
  44.9 2.3 %collective-permute-done.theirs_ref = bf16[1024,512]{1,0:T(8,128)(2,1)S(1)} collective-permute-done((bf16[1024,512]{1,0:T(8,128)(2,1)S(1)}, bf16[1024,512]{1,0:T(8,128)(2,1)S(1)}, u32[]{:S(2)}, u32[]{:S(2)}) %collective-permute-start) | collective-permute-done | bytes 1048608 | tf_op jit(solution)/shard_map/ppermute | solution.py:182
  47.2 0.0 copy-start.1
  47.2 0.0 copy-done
  47.2 0.0 copy-done.3
  47.2 0.0 copy-done.5
  47.2 0.0 copy-done.6
  47.2 11.4 %attention_layer.1 = (bf16[512,768]{1,0:T(8,128)(2,1)S(1)}, bf16[512,768]{1,0:T(8,128)(2,1)S(1)}, bf16[1024,512]{1,0:T(8,128)(2,1)S(1)}, bf16[1024,512]{1,0:T(8,128)(2,1)S(1)}) custom-call(s32[2]{0:T(128)S(1)} %copy-done.5, s32[2]{0:T(128)S(1)} %bitcast.20, bf16[512,512]{1,0:T(8,128)(2,1)S(1)} %bitcast.15, bf16[512,512]{1,0:T(8,128)(2,1)S(1)} %bitcast.19, ...), custom_call_target="tpu_custom_call" | custom-call | flops 2684354560 | bytes 6291456 | tf_op jit(solution)/shard_map/attention_layer/pallas_call | solution.py:161
  58.7 0.0 copy-done.1
  58.7 2.3 %collective-permute-start.1 = (bf16[1024,512]{1,0:T(8,128)(2,1)S(1)}, bf16[1024,512]{1,0:T(8,128)(2,1)S(1)}, u32[]{:S(2)}, u32[]{:S(2)}) collective-permute-start(bf16[1024,512]{1,0:T(8,128)(2,1)S(1)} %get-tuple-element.16), channel_id=1, source_target_pairs={{0,32},{32,0},{1,33},{33,1},{2,34},{34,2},{3,35},{35,3},{4,36},{36... | collective-permute-start | bytes 3145736 | tf_op jit(solution)/shard_map/ppermute | solution.py:182
  61.0 2.3 %collective-permute-done.1 = bf16[1024,512]{1,0:T(8,128)(2,1)S(1)} collective-permute-done((bf16[1024,512]{1,0:T(8,128)(2,1)S(1)}, bf16[1024,512]{1,0:T(8,128)(2,1)S(1)}, u32[]{:S(2)}, u32[]{:S(2)}) %collective-permute-start.1) | collective-permute-done | bytes 1048608 | tf_op jit(solution)/shard_map/ppermute | solution.py:182
  63.3 1.3 %add_convert_fusion = bf16[1024,512]{1,0:T(8,128)(2,1)} fusion(bf16[1024,512]{1,0:T(8,128)(2,1)S(1)} %collective-permute-done.1, bf16[1024,512]{1,0:T(8,128)(2,1)S(1)} %get-tuple-element.15), kind=kLoop, calls=%fused_computation | loop fusion | flops 2097152 | bytes 3145728 | tf_op jit(solution)/shard_map/convert_element_type | solution.py:279
  64.5 4.2 %all-to-all-start.2 = ((bf16[8,128,512]{2,1,0:T(8,128)(2,1)}), bf16[8,128,512]{2,1,0:T(8,128)(2,1)}, u32[]{:S(2)}, u32[]{:S(2)}) async-start(bf16[8,128,512]{2,1,0:T(8,128)(2,1)} %bitcast.22), calls=%async_computation.2 | async-start | bytes 2097152 | tf_op jit(solution)/shard_map/all_to_all | solution.py:186
  68.8 0.2 multiply_reduce_fusion.1
  69.0 0.1 rsqrt.12
  69.1 0.1 iota_compare_fusion
  69.1 0.1 lt.23
  69.2 0.1 broadcast_in_dim.27
  69.3 0.1 broadcast_in_dim.28
  69.4 0.8 slice.36
  70.2 1.3 %fusion.6 = f32[512,512]{1,0:T(8,128)} fusion(bf16[1024,512]{1,0:T(8,128)(2,1)S(1)} %bitcast.18, bf16[512,768]{1,0:T(8,128)(2,1)S(1)} %get-tuple-element.13), kind=kOutput, calls=%fused_computation.13 | convolution fusion | flops 134217728 | bytes 1572864 | tf_op jit(solution)/shard_map/dot_general | solution.py:23
  71.5 0.0 copy-done.2
  71.5 0.3 fusion.4
  71.9 1.5 %convolution_add_fusion = f32[512,512]{1,0:T(8,128)} fusion(f32[512,512]{1,0:T(8,128)S(1)} %fusion.4, bf16[1024,512]{1,0:T(8,128)(2,1)S(1)} %copy-done.2, bf16[512,768]{1,0:T(8,128)(2,1)S(1)} %get-tuple-element.14), kind=kOutput, calls=%fused_computation.1 | convolution fusion | flops 268697600 | bytes 3145728 | tf_op jit(solution)/shard_map/dot_general | solution.py:23
  73.3 10.4 %all-to-all-done.2.blocks_ref = bf16[8,128,512]{2,1,0:T(8,128)(2,1)} async-done(((bf16[8,128,512]{2,1,0:T(8,128)(2,1)}), bf16[8,128,512]{2,1,0:T(8,128)(2,1)}, u32[]{:S(2)}, u32[]{:S(2)}) %all-to-all-start.2) | async-done | bytes 1048608 | tf_op jit(solution)/shard_map/all_to_all | solution.py:186
  83.8 3.2 %block_sum.2 = bf16[128,512]{1,0:T(8,128)(2,1)} custom-call(bf16[8,128,512]{2,1,0:T(8,128)(2,1)} %all-to-all-done.2.blocks_ref), custom_call_target="tpu_custom_call" | custom-call | tf_op jit(solution)/shard_map/block_sum/pallas_call | solution.py:228
  87.0 3.4 %all-to-all-start.3 = ((bf16[8,16,512]{2,1,0:T(8,128)(2,1)}), bf16[8,16,512]{2,1,0:T(8,128)(2,1)S(1)}, u32[]{:S(2)}, u32[]{:S(2)}) async-start(bf16[8,16,512]{2,1,0:T(8,128)(2,1)} %bitcast.24), calls=%async_computation.3 | async-start | bytes 262144 | tf_op jit(solution)/shard_map/all_to_all | solution.py:186
  90.3 0.0 copy-done.7
  90.4 2.0 %multiply_reduce_fusion = (f32[512]{0:T(512)S(1)}, f32[512,512]{1,0:T(8,128)S(1)}) fusion(f32[512]{0:T(512)S(1)} %rsqrt.12, bf16[2,8,32,512]{3,2,1,0:T(8,128)(2,1)S(1)} %copy-done, f32[512,512]{1,0:T(8,128)S(1)} %copy-done.7, f32[512,512]{1,0:T(8,128)} %fusion.6, bf16[512,512]{1,0:T(8,128)(2,1)} %bitcast.23, bf16[512,768]{1,0:T(8,128)(2,1)S(1)} %get-tuple-element.13), kind=kOutput, calls=%fused_computation.5 | convolution fusion | flops 270007808 | bytes 4722688 | tf_op jit(solution)/shard_map/dot_general | solution.py:23
  92.4 0.0 copy-start.4
  92.4 5.7 %all-to-all-done.3.blocks_ref = bf16[8,16,512]{2,1,0:T(8,128)(2,1)S(1)} async-done(((bf16[8,16,512]{2,1,0:T(8,128)(2,1)}), bf16[8,16,512]{2,1,0:T(8,128)(2,1)S(1)}, u32[]{:S(2)}, u32[]{:S(2)}) %all-to-all-start.3) | async-done | bytes 131104 | tf_op jit(solution)/shard_map/all_to_all | solution.py:186
  98.0 0.7 copy-done.9
  98.7 1.6 %block_sum.3 = bf16[16,16,512]{2,1,0:T(8,128)(2,1)} custom-call(bf16[8,16,512]{2,1,0:T(8,128)(2,1)} %copy-done.9), custom_call_target="tpu_custom_call" | custom-call | tf_op jit(solution)/shard_map/block_sum/pallas_call | solution.py:228
  100.3 8.5 %all-to-all-start.4 = ((bf16[16,16,512]{2,1,0:T(8,128)(2,1)}), bf16[16,16,512]{2,1,0:T(8,128)(2,1)S(1)}, u32[]{:S(2)}, u32[]{:S(2)}) async-start(bf16[16,16,512]{2,1,0:T(8,128)(2,1)} %block_sum.3), calls=%async_computation.4 | async-start | bytes 524288 | tf_op jit(solution)/shard_map/all_to_all | solution.py:186
  108.8 0.0 copy-done.4
  108.8 1.2 add_convert_fusion.1
  110.0 10.5 %all-to-all-done.4.blocks_ref = bf16[16,16,512]{2,1,0:T(8,128)(2,1)S(1)} async-done(((bf16[16,16,512]{2,1,0:T(8,128)(2,1)}), bf16[16,16,512]{2,1,0:T(8,128)(2,1)S(1)}, u32[]{:S(2)}, u32[]{:S(2)}) %all-to-all-start.4) | async-done | bytes 262176 | tf_op jit(solution)/shard_map/all_to_all | solution.py:186
  120.5 0.7 copy-done.8
  121.2 1.6 %final_sum.1 = (f32[16,512]{1,0:T(8,128)}, f32[16,512]{1,0:T(8,128)}, f32[16,512]{1,0:T(8,128)}, f32[16,512]{1,0:T(8,128)}) custom-call(bf16[16,16,512]{2,1,0:T(8,128)(2,1)} %copy-done.8), custom_call_target="tpu_custom_call" | custom-call | tf_op jit(solution)/shard_map/final_sum/pallas_call | solution.py:255
  (6 shorter events, 0.0 us)
Async XLA Ops:
  21.4 25.8 %copy-start = (bf16[2,8,32,512]{3,2,1,0:T(8,128)(2,1)S(1)}, bf16[2,8,32,512]{3,2,1,0:T(8,128)(2,1)}, u32[]{:S(2)}) copy-start(bf16[2,8,32,512]{3,2,1,0:T(8,128)(2,1)} %param.7) | copy-start | bytes 1572868
  21.4 25.8 %copy-start.3 = (bf16[2,8,32,512]{3,2,1,0:T(8,128)(2,1)S(1)}, bf16[2,8,32,512]{3,2,1,0:T(8,128)(2,1)}, u32[]{:S(2)}) copy-start(bf16[2,8,32,512]{3,2,1,0:T(8,128)(2,1)} %param.8) | copy-start | bytes 1572868
  21.4 25.8 %copy-start.5 = (s32[2]{0:T(128)S(1)}, s32[2]{0:T(128)}, u32[]{:S(2)}) copy-start(s32[2]{0:T(128)} %pad_add_fusion.place_ref) | copy-start | bytes 28
  21.5 25.8 %copy-start.6 = (s32[1,2]{1,0:T(1,128)S(1)}, s32[1,2]{1,0:T(1,128)}, u32[]{:S(2)}) copy-start(s32[1,2]{1,0:T(1,128)} %param.9) | copy-start | bytes 28
  39.0 8.2 %collective-permute-start = (bf16[1024,512]{1,0:T(8,128)(2,1)S(1)}, bf16[1024,512]{1,0:T(8,128)(2,1)S(1)}, u32[]{:S(2)}, u32[]{:S(2)}) collective-permute-start(bf16[1024,512]{1,0:T(8,128)(2,1)S(1)} %bitcast.16), channel_id=1, source_target_pairs={{0,32},{32,0},{1,33},{33,1},{2,34},{34,2},{3,35},{35,3},{4,36},{36... | collective-permute-start | bytes 3145736 | tf_op jit(solution)/shard_map/ppermute | solution.py:182
  47.2 11.5 %copy-start.1 = (bf16[1024,512]{1,0:T(8,128)(2,1)}, bf16[1024,512]{1,0:T(8,128)(2,1)S(1)}, u32[]{:S(2)}) copy-start(bf16[1024,512]{1,0:T(8,128)(2,1)S(1)} %collective-permute-done.theirs_ref) | copy-start | bytes 3145732
  58.7 4.6 %collective-permute-start.1 = (bf16[1024,512]{1,0:T(8,128)(2,1)S(1)}, bf16[1024,512]{1,0:T(8,128)(2,1)S(1)}, u32[]{:S(2)}, u32[]{:S(2)}) collective-permute-start(bf16[1024,512]{1,0:T(8,128)(2,1)S(1)} %get-tuple-element.16), channel_id=1, source_target_pairs={{0,32},{32,0},{1,33},{33,1},{2,34},{34,2},{3,35},{35,3},{4,36},{36... | collective-permute-start | bytes 3145736 | tf_op jit(solution)/shard_map/ppermute | solution.py:182
  64.5 19.2 %all-to-all-start.2 = ((bf16[8,128,512]{2,1,0:T(8,128)(2,1)}), bf16[8,128,512]{2,1,0:T(8,128)(2,1)}, u32[]{:S(2)}, u32[]{:S(2)}) async-start(bf16[8,128,512]{2,1,0:T(8,128)(2,1)} %bitcast.22), calls=%async_computation.2 | async-start | bytes 2097152 | tf_op jit(solution)/shard_map/all_to_all | solution.py:186
  70.2 1.3 %copy-start.2 = (bf16[1024,512]{1,0:T(8,128)(2,1)S(1)}, bf16[1024,512]{1,0:T(8,128)(2,1)}, u32[]{:S(2)}) copy-start(bf16[1024,512]{1,0:T(8,128)(2,1)} %copy-done.1) | copy-start | bytes 3145732
  73.3 17.0 %copy-start.7 = (f32[512,512]{1,0:T(8,128)S(1)}, f32[512,512]{1,0:T(8,128)}, u32[]{:S(2)}) copy-start(f32[512,512]{1,0:T(8,128)} %convolution_add_fusion) | copy-start | bytes 3145732
  87.0 11.1 %all-to-all-start.3 = ((bf16[8,16,512]{2,1,0:T(8,128)(2,1)}), bf16[8,16,512]{2,1,0:T(8,128)(2,1)S(1)}, u32[]{:S(2)}, u32[]{:S(2)}) async-start(bf16[8,16,512]{2,1,0:T(8,128)(2,1)} %bitcast.24), calls=%async_computation.3 | async-start | bytes 262144 | tf_op jit(solution)/shard_map/all_to_all | solution.py:186
  92.4 16.5 %copy-start.4 = (bf16[2,8,32,512]{3,2,1,0:T(8,128)(2,1)S(1)}, bf16[2,8,32,512]{3,2,1,0:T(8,128)(2,1)}, u32[]{:S(2)}) copy-start(bf16[2,8,32,512]{3,2,1,0:T(8,128)(2,1)} %param.8) | copy-start | bytes 1572868
  98.0 0.7 copy-start.9
  100.3 20.2 %all-to-all-start.4 = ((bf16[16,16,512]{2,1,0:T(8,128)(2,1)}), bf16[16,16,512]{2,1,0:T(8,128)(2,1)S(1)}, u32[]{:S(2)}, u32[]{:S(2)}) async-start(bf16[16,16,512]{2,1,0:T(8,128)(2,1)} %block_sum.3), calls=%async_computation.4 | async-start | bytes 524288 | tf_op jit(solution)/shard_map/all_to_all | solution.py:186
  120.5 0.7 copy-start.8

commit v6 on v5

--- a/solution.py
+++ b/solution.py
@@ -51,21 +51,21 @@
 
 def attention(q_half, k_half, v_half, grad_att, same_row):
     k_two, v_two = stacked(k_half), stacked(v_half)
-    exps = jnp.where(same_row, jnp.exp(dot_nt(q_half, k_two) * gain), 0.0)
-    grad_probs = dot_nt(grad_att, v_two)
+    exps = jnp.where(same_row, jnp.exp(dot_nt(k_two, q_half) * gain), 0.0)
+    grad_probs = dot_nt(v_two, grad_att)
     probs, d_scores = [], []
     for half in (slice(0, SPAN), slice(SPAN, 2 * SPAN)):
-        part = exps[:, half] * (1.0 / jnp.sum(exps[:, half], axis=1, keepdims=True))
-        weighted = part * grad_probs[:, half]
-        total = jnp.sum(weighted, axis=1, keepdims=True)
+        part = exps[half] * (1.0 / jnp.sum(exps[half], axis=0, keepdims=True))
+        weighted = part * grad_probs[half]
+        total = jnp.sum(weighted, axis=0, keepdims=True)
         probs.append(part.astype(bf16))
         d_scores.append(((weighted - part * total) * gain).astype(bf16))
-    probs, d_scores = jnp.concatenate(probs, axis=1), jnp.concatenate(d_scores, axis=1)
+    probs, d_scores = jnp.concatenate(probs, axis=0), jnp.concatenate(d_scores, axis=0)
     return (
-        dot_nn(probs, v_two).astype(bf16),
-        dot_nn(d_scores, k_two),
-        unstacked(dot_tn(d_scores, q_half)),
-        unstacked(dot_tn(probs, grad_att)).astype(bf16),
+        dot_tn(probs, v_two).astype(bf16),
+        dot_tn(d_scores, k_two),
+        unstacked(dot_nn(d_scores, q_half)),
+        unstacked(dot_nn(probs, grad_att)).astype(bf16),
     )
 
 
@@ -90,8 +90,8 @@
     slot = lax.broadcasted_iota(jnp.int32, up_ref.shape, 0) // ROW
     masked_ref[here, :] = jnp.where(slot < counts_ref[step], up_ref[...], jnp.zeros((), bf16))
 
-    row_of = lax.broadcasted_iota(jnp.int32, (SPAN, 2 * SPAN), 0) // ROW
-    col_of = lax.broadcasted_iota(jnp.int32, (SPAN, 2 * SPAN), 1) % SPAN // ROW
+    row_of = lax.broadcasted_iota(jnp.int32, (2 * SPAN, SPAN), 0) % SPAN // ROW
+    col_of = lax.broadcasted_iota(jnp.int32, (2 * SPAN, SPAN), 1) // ROW
     same_row = row_of == col_of
 
     for weight_ref, d_ref, heads, place in (
@@ -190,47 +190,30 @@
     return terms.reshape(count, terms.shape[0] // count, terms.shape[1])
 
 
-def copies_kernel(place_ref, *refs):
-    *weight_refs, out_ref = refs
-    width = weight_refs[0].shape[1] // 2
-    own = pl.multiple_of(place_ref[0] * width, width)
-    for yl in range(2):
-
-        @pl.when(place_ref[1] == yl)
-        def _():
-            for index, weight_ref in enumerate(weight_refs[2 * yl : 2 * yl + 2]):
-                block = weight_ref[:, pl.ds(own, width)]
-                out_ref[:, :, index * width : (index + 1) * width] = jnp.broadcast_to(
-                    block[None], (out_ref.shape[0],) + block.shape
-                )
-
-
-def weight_copies(place, weights, count):
+def weight_copies(core, yl, weights, count):
+    width = weights[0].shape[1] // 2
+    halves = [jnp.where(core == 0, weight[:, :width], weight[:, width:]) for weight in weights]
+    block = jnp.concatenate(
+        [jnp.where(yl == 0, halves[index], halves[index + 2]) for index in range(2)], axis=1
+    )
+    return jnp.broadcast_to(block[None], (count,) + block.shape)
+
+
+small = pltpu.CompilerParams(vmem_limit_bytes=4 * 1024 * 1024)
+
+
+def sum_kernel(blocks_ref, out_ref):
+    out_ref[...] = jnp.sum(blocks_ref[...].astype(f32), axis=0).astype(bf16)
+
+
+def block_sum(blocks):
     vmem = pl.BlockSpec(memory_space=pltpu.VMEM)
     return pl.pallas_call(
-        copies_kernel,
-        in_specs=[pl.BlockSpec(memory_space=pltpu.SMEM)] + [vmem] * 4,
+        sum_kernel,
+        in_specs=[vmem],
         out_specs=vmem,
-        out_shape=jax.ShapeDtypeStruct((count,) + weights[0].shape, bf16),
-        name="weight_copies",
-    )(place, *weights)
-
-
-def sum_kernel(blocks_ref, out_ref):
-    total = jnp.sum(blocks_ref[...].astype(f32), axis=0).astype(bf16)
-    out_ref[...] = jnp.broadcast_to(total, out_ref.shape)
-
-
-def block_sum(blocks, parts, copies=None):
-    count, rows, width = blocks.shape
-    out = (rows // parts, width) if copies is None else (copies, rows // parts, width)
-    lead = (0,) * (len(out) - 2)
-    return pl.pallas_call(
-        sum_kernel,
-        grid=(parts,),
-        in_specs=[pl.BlockSpec((count, rows // parts, width), lambda i: (0, i, 0))],
-        out_specs=pl.BlockSpec(out, lambda i: lead + (i, 0)),
-        out_shape=jax.ShapeDtypeStruct(out[:-2] + (rows, width), bf16),
+        out_shape=jax.ShapeDtypeStruct(blocks.shape[1:], bf16),
+        compiler_params=small,
         name="block_sum",
     )(blocks)
 
@@ -257,29 +240,31 @@
         in_specs=[vmem],
         out_specs=[vmem] * 4,
         out_shape=[jax.ShapeDtypeStruct((rows, width), f32)] * 4,
+        compiler_params=small,
         name="final_sum",
     )(blocks)
 
 
 def local(trace_rows, upstream, counts, w_query, w_key, w_value, w_out):
-    place = jnp.stack((lax.axis_index("core"), lax.axis_index("yl")))
+    core, yl = lax.axis_index("core"), lax.axis_index("yl")
     view_count, most_rows, row_length, depth = trace_rows.shape
     tokens = view_count * most_rows * row_length
     view_counts = counts.reshape(view_count)
 
-    copies = weight_copies(place, (w_query, w_key, w_value, w_out), lax.axis_size("z"))
+    copies = weight_copies(core, yl, (w_query, w_key, w_value, w_out), lax.axis_size("z"))
     lines = sent(copies, "z").reshape(-1, depth)
     lines = jnp.broadcast_to(lines[None], (lax.axis_size(NEAR),) + lines.shape)
     mine = sent(lines, NEAR).reshape(-1, depth)
     theirs = swapped(mine)
 
     rows, up = trace_rows.reshape(tokens, depth), upstream.reshape(tokens, depth)
-    d_mine, d_theirs, out_mine, out_theirs = layer(place, view_counts, rows, up, mine, theirs)
+    d_mine, d_theirs, out_mine, out_theirs = layer(core.reshape(1), view_counts, rows, up, mine, theirs)
 
     terms = (out_mine.astype(f32) + swapped(out_theirs).astype(f32)).astype(bf16)
-    total = block_sum(sent(blocks_of(terms, lax.axis_size(NEAR)), NEAR), 4)
+    total = block_sum(sent(blocks_of(terms, lax.axis_size(NEAR)), NEAR))
     total = sent(blocks_of(total, lax.axis_size("z")), "z")
-    total = block_sum(total, 1, lax.axis_size(ALL_Y + ("core",)))
+    total = jnp.sum(total.astype(f32), axis=0).astype(bf16)
+    total = jnp.broadcast_to(total[None], (lax.axis_size(ALL_Y + ("core",)),) + total.shape)
     devices = math.prod(lax.axis_size(name) for name in MESH_AXES)
     weight_grads = final_sum(
         sent(total, ALL_Y + ("core",)), 1.0 / math.sqrt(devices * tokens // 2)

time: 124 us -> 114 us (0.919)
  Pallas kernels: 19.4 us -> 10.9 us
  waiting for transfers between devices: 31.1 us -> 29.7 us
  matrix products: 5.1 us -> 6.47 us
    pallas_call x3 -> x1, Pallas kernels: 6.32 us -> 0.79 us  [block_sum(): pl.pallas_call(sum_kernel, in_specs=[vmem], out_specs=vmem, out_shape=jax...]
    pallas_call x1, Pallas kernels: 11.4 us -> 9.47 us  [layer(): pl.pallas_call(layer_kernel, grid=(views,), in_specs=[smem, smem, part, p...]
    all_to_all x3, waiting for transfers between devices: 26.6 us -> 25.2 us  [sent(): return lax.all_to_all(blocks, axis, split_axis=0, concat_axis=0, tiled=True)]
    dot_general x4, matrix products: 5.1 us -> 6.47 us  [dot_nt(): lax.dot_general(a, b, (((1,), (1,)), ((), ())), preferred_element_type=f32)]
    unnamed x20 -> x16, local copies, waits for them, and re-layouts: 1.4 us -> 0.04 us
  transfers between devices with their start and end apart: 5 -> 5, of which waited for: 5 -> 5; matrix products, arithmetic and copies ran while one was open for 6% -> 8% of each run, Pallas kernels for 0% -> 0%
where the time goes in v6:
time: 114 us; the launch traced here: 113 us
  blocking collectives  35.9 us (31%)
  waiting for transfers between devices  29.7 us (26%)
  starting transfers between devices  23.7 us (21%)
  Pallas kernels  10.9 us (10%)
  matrix products  6.47 us (6%)
  other arithmetic  3.55 us (3%)
  local copies, waits for them, and re-layouts  2.03 us (2%)
    all_to_all x2, blocking collectives, sent(): return lax.all_to_all(blocks, axis, split_axis=0, concat_axis=0, tiled=True)  35.9 us
    all_to_all x3, waiting for transfers between devices, sent(): return lax.all_to_all(blocks, axis, split_axis=0, concat_axis=0, tiled=True)  25.2 us
    all_to_all x3, starting transfers between devices, sent(): return lax.all_to_all(blocks, axis, split_axis=0, concat_axis=0, tiled=True)  15.4 us
    pallas_call x1, Pallas kernels, layer(): pl.pallas_call(layer_kernel, grid=(views,), in_specs=[smem, smem, part, p...  9.47 us
    ppermute x2, starting transfers between devices, swapped(): return lax.ppermute(block, 'core', [(0, 1), (1, 0)])  8.24 us
    dot_general x4, matrix products, dot_nt(): lax.dot_general(a, b, (((1,), (1,)), ((), ())), preferred_element_type=f32)  6.47 us
    ppermute x2, waiting for transfers between devices, swapped(): return lax.ppermute(block, 'core', [(0, 1), (1, 0)])  4.53 us
  transfers between devices with their start and end apart: 5, of which 5 were waited for; matrix products, arithmetic and copies ran while one was open for 8% of the time, Pallas kernels for 0%

profile of v6, /device:TPU:1, one launch (start us, length us, event | category | flops | bytes accessed | tf_op | source)
XLA Modules:
  0.0 113.1 jit_solution(16808202611332159304)
XLA Ops:
  0.6 0.8 select_select_fusion
  1.5 18.4 %all_to_all.25 = bf16[8,16,512]{2,1,0:T(8,128)(2,1)S(1)} all-to-all(bf16[8,16,512]{2,1,0:T(8,128)(2,1)S(1)} %broadcast_in_dim.43), channel_id=1, replica_groups=mesh['yh'=4,'yl'=2,'core'=2,'x'=4,'z'=8] {'z'}, dimensions={0} | all-to-all | bytes 262144 | tf_op jit(solution)/shard_map/all_to_all | solution.py:186
  19.9 0.1 broadcast_in_dim.45
  20.0 0.0 copy-start
  20.0 0.0 copy-start.5
  20.0 0.0 copy-start.7
  20.0 17.5 %all_to_all.26 = bf16[8,128,512]{2,1,0:T(8,128)(2,1)S(1)} all-to-all(bf16[8,128,512]{2,1,0:T(8,128)(2,1)S(1)} %broadcast_in_dim.45), channel_id=1, replica_groups=mesh['yh'=4,'yl'=2,'core'=2,'x'=4,'z'=8] {'yl','x'}, dimensions={0} | all-to-all | bytes 2097152 | tf_op jit(solution)/shard_map/all_to_all | solution.py:186
  37.5 6.0 %collective-permute-start = (bf16[1024,512]{1,0:T(8,128)(2,1)S(1)}, bf16[1024,512]{1,0:T(8,128)(2,1)S(1)}, u32[]{:S(2)}, u32[]{:S(2)}) collective-permute-start(bf16[1024,512]{1,0:T(8,128)(2,1)S(1)} %bitcast.15), channel_id=1, source_target_pairs={{0,32},{32,0},{1,33},{33,1},{2,34},{34,2},{3,35},{35,3},{4,36},{36... | collective-permute-start | bytes 3145736 | tf_op jit(solution)/shard_map/ppermute | solution.py:182
  43.5 2.3 %collective-permute-done.theirs_ref = bf16[1024,512]{1,0:T(8,128)(2,1)S(1)} collective-permute-done((bf16[1024,512]{1,0:T(8,128)(2,1)S(1)}, bf16[1024,512]{1,0:T(8,128)(2,1)S(1)}, u32[]{:S(2)}, u32[]{:S(2)}) %collective-permute-start) | collective-permute-done | bytes 1048608 | tf_op jit(solution)/shard_map/ppermute | solution.py:182
  45.8 0.0 copy-start.3
  45.8 0.0 copy-done
  45.8 0.0 copy-done.5
  45.8 0.0 copy-done.7
  45.8 9.5 %attention_layer.1 = (bf16[512,768]{1,0:T(8,128)(2,1)S(1)}, bf16[512,768]{1,0:T(8,128)(2,1)S(1)}, bf16[1024,512]{1,0:T(8,128)(2,1)S(1)}, bf16[1024,512]{1,0:T(8,128)(2,1)S(1)}) custom-call(s32[1]{0:T(128)} %bitcast.2.place_ref, s32[2]{0:T(128)S(1)} %bitcast.19, bf16[512,512]{1,0:T(8,128)(2,1)S(1)} %bitcast.14, bf16[512,512]{1,0:T(8,128)(2,1)S(1)} %bitcast.18, ...), custom_call_target="tpu_custom_call" | custom-call | flops 2684354560 | bytes 6291456 | tf_op jit(solution)/shard_map/attention_layer/pallas_call | solution.py:161
  55.3 0.0 copy-done.3
  55.3 0.0 copy-start.1
  55.3 2.3 %collective-permute-start.1 = (bf16[1024,512]{1,0:T(8,128)(2,1)S(1)}, bf16[1024,512]{1,0:T(8,128)(2,1)S(1)}, u32[]{:S(2)}, u32[]{:S(2)}) collective-permute-start(bf16[1024,512]{1,0:T(8,128)(2,1)S(1)} %get-tuple-element.16), channel_id=1, source_target_pairs={{0,32},{32,0},{1,33},{33,1},{2,34},{34,2},{3,35},{35,3},{4,36},{36... | collective-permute-start | bytes 3145736 | tf_op jit(solution)/shard_map/ppermute | solution.py:182
  57.6 2.3 %collective-permute-done.1 = bf16[1024,512]{1,0:T(8,128)(2,1)S(1)} collective-permute-done((bf16[1024,512]{1,0:T(8,128)(2,1)S(1)}, bf16[1024,512]{1,0:T(8,128)(2,1)S(1)}, u32[]{:S(2)}, u32[]{:S(2)}) %collective-permute-start.1) | collective-permute-done | bytes 1048608 | tf_op jit(solution)/shard_map/ppermute | solution.py:182
  59.8 1.3 %add_convert_fusion = bf16[1024,512]{1,0:T(8,128)(2,1)} fusion(bf16[1024,512]{1,0:T(8,128)(2,1)S(1)} %collective-permute-done.1, bf16[1024,512]{1,0:T(8,128)(2,1)S(1)} %get-tuple-element.15), kind=kLoop, calls=%fused_computation | loop fusion | flops 2097152 | bytes 3145728 | tf_op jit(solution)/shard_map/convert_element_type | solution.py:263
  61.1 0.0 copy-done.1
  61.1 3.6 %all-to-all-start.2 = ((bf16[8,128,512]{2,1,0:T(8,128)(2,1)}), bf16[8,128,512]{2,1,0:T(8,128)(2,1)S(1)}, u32[]{:S(2)}, u32[]{:S(2)}) async-start(bf16[8,128,512]{2,1,0:T(8,128)(2,1)} %bitcast.21), calls=%async_computation.2 | async-start | bytes 2097152 | tf_op jit(solution)/shard_map/all_to_all | solution.py:186
  64.7 0.2 multiply_reduce_fusion.1
  64.9 0.1 rsqrt.12
  65.0 0.1 iota_compare_fusion
  65.0 0.1 lt.23
  65.1 0.1 broadcast_in_dim.39
  65.2 0.1 broadcast_in_dim.40
  65.3 0.8 slice.68
  66.1 0.0 copy-start.4
  66.1 2.3 %fusion.6 = f32[512,512]{1,0:T(8,128)} fusion(bf16[1024,512]{1,0:T(8,128)(2,1)S(1)} %bitcast.17, bf16[512,768]{1,0:T(8,128)(2,1)} %copy-done.1), kind=kOutput, calls=%fused_computation.13 | convolution fusion | flops 134217728 | bytes 1572864 | tf_op jit(solution)/shard_map/dot_general | solution.py:23
  68.4 0.0 copy-done.4
  68.4 0.3 fusion.4
  68.8 1.5 %convolution_add_fusion = f32[512,512]{1,0:T(8,128)} fusion(f32[512,512]{1,0:T(8,128)S(1)} %fusion.4, bf16[1024,512]{1,0:T(8,128)(2,1)S(1)} %copy-done.4, bf16[512,768]{1,0:T(8,128)(2,1)S(1)} %get-tuple-element.14), kind=kOutput, calls=%fused_computation.1 | convolution fusion | flops 268697600 | bytes 3145728 | tf_op jit(solution)/shard_map/dot_general | solution.py:23
  70.3 0.0 copy-start.2
  70.3 9.3 %all-to-all-done.2.blocks_ref = bf16[8,128,512]{2,1,0:T(8,128)(2,1)S(1)} async-done(((bf16[8,128,512]{2,1,0:T(8,128)(2,1)}), bf16[8,128,512]{2,1,0:T(8,128)(2,1)S(1)}, u32[]{:S(2)}, u32[]{:S(2)}) %all-to-all-start.2) | async-done | bytes 1048608 | tf_op jit(solution)/shard_map/all_to_all | solution.py:186
  79.6 0.8 block_sum.1
  80.4 3.4 %all-to-all-start.3 = ((bf16[8,16,512]{2,1,0:T(8,128)(2,1)}), bf16[8,16,512]{2,1,0:T(8,128)(2,1)S(1)}, u32[]{:S(2)}, u32[]{:S(2)}) async-start(bf16[8,16,512]{2,1,0:T(8,128)(2,1)} %bitcast.9), calls=%async_computation.3 | async-start | bytes 262144 | tf_op jit(solution)/shard_map/all_to_all | solution.py:186
  83.8 0.0 copy-done.2
  83.8 2.3 %multiply_reduce_fusion = (f32[512]{0:T(512)S(1)}, f32[512,512]{1,0:T(8,128)S(1)}) fusion(f32[512]{0:T(512)S(1)} %rsqrt.12, bf16[2,8,32,512]{3,2,1,0:T(8,128)(2,1)S(1)} %copy-done, f32[512,512]{1,0:T(8,128)} %convolution_add_fusion, f32[512,512]{1,0:T(8,128)} %fusion.6, bf16[512,512]{1,0:T(8,128)(2,1)} %bitcast.22, bf16[512,768]{1,0:T(8,128)(2,1)S(1)} %copy-done.2), kind=kOutput, calls=%fused_computation.5 | convolution fusion | flops 270007808 | bytes 4722688 | tf_op jit(solution)/shard_map/dot_general | solution.py:23
  86.1 0.0 copy-start.6
  86.1 5.3 %all-to-all-done.3 = bf16[8,16,512]{2,1,0:T(8,128)(2,1)S(1)} async-done(((bf16[8,16,512]{2,1,0:T(8,128)(2,1)}), bf16[8,16,512]{2,1,0:T(8,128)(2,1)S(1)}, u32[]{:S(2)}, u32[]{:S(2)}) %all-to-all-start.3) | async-done | bytes 131104 | tf_op jit(solution)/shard_map/all_to_all | solution.py:186
  91.5 0.7 broadcast_in_dim.46
  92.2 8.5 %all-to-all-start.4 = ((bf16[16,16,512]{2,1,0:T(8,128)(2,1)}), bf16[16,16,512]{2,1,0:T(8,128)(2,1)S(1)}, u32[]{:S(2)}, u32[]{:S(2)}) async-start(bf16[16,16,512]{2,1,0:T(8,128)(2,1)} %broadcast_in_dim.46), calls=%async_computation.4 | async-start | bytes 524288 | tf_op jit(solution)/shard_map/all_to_all | solution.py:186
  100.7 0.0 copy-done.6
  100.7 1.2 %add_convert_fusion.1 = bf16[512,512]{1,0:T(8,128)(2,1)} fusion(f32[512,512]{1,0:T(8,128)S(1)} %get-tuple-element.22, f32[512]{0:T(512)S(1)} %broadcast_multiply_fusion, f32[512]{0:T(512)S(1)} %rsqrt.12, pred[512]{0:T(512)(128)(4,1)S(1)} %broadcast_in_dim.40, bf16[2,8,32,512]{3,2,1,0:T(8,128)(2,1)S(1)} %copy-done, bf16[2,8,32,512]{3,2,1,0:T(8,128)(2,1)S(1)} %copy-done.6), kind=kLoop, calls=%fused_computation.4 | loop fusion | flops 2359296 | bytes 2626048 | tf_op jit(solution)/shard_map/convert_element_type | solution.py:287
  101.9 10.5 %all-to-all-done.4.blocks_ref = bf16[16,16,512]{2,1,0:T(8,128)(2,1)S(1)} async-done(((bf16[16,16,512]{2,1,0:T(8,128)(2,1)}), bf16[16,16,512]{2,1,0:T(8,128)(2,1)S(1)}, u32[]{:S(2)}, u32[]{:S(2)}) %all-to-all-start.4) | async-done | bytes 262176 | tf_op jit(solution)/shard_map/all_to_all | solution.py:186
  112.4 0.7 final_sum.1
  (5 shorter events, 0.0 us)
Async XLA Ops:
  20.0 25.8 %copy-start = (bf16[2,8,32,512]{3,2,1,0:T(8,128)(2,1)S(1)}, bf16[2,8,32,512]{3,2,1,0:T(8,128)(2,1)}, u32[]{:S(2)}) copy-start(bf16[2,8,32,512]{3,2,1,0:T(8,128)(2,1)} %param.7) | copy-start | bytes 1572868
  20.0 25.8 %copy-start.5 = (bf16[2,8,32,512]{3,2,1,0:T(8,128)(2,1)S(1)}, bf16[2,8,32,512]{3,2,1,0:T(8,128)(2,1)}, u32[]{:S(2)}) copy-start(bf16[2,8,32,512]{3,2,1,0:T(8,128)(2,1)} %param.8) | copy-start | bytes 1572868
  20.0 25.8 %copy-start.7 = (s32[1,2]{1,0:T(1,128)S(1)}, s32[1,2]{1,0:T(1,128)}, u32[]{:S(2)}) copy-start(s32[1,2]{1,0:T(1,128)} %param.9) | copy-start | bytes 28
  37.5 8.2 %collective-permute-start = (bf16[1024,512]{1,0:T(8,128)(2,1)S(1)}, bf16[1024,512]{1,0:T(8,128)(2,1)S(1)}, u32[]{:S(2)}, u32[]{:S(2)}) collective-permute-start(bf16[1024,512]{1,0:T(8,128)(2,1)S(1)} %bitcast.15), channel_id=1, source_target_pairs={{0,32},{32,0},{1,33},{33,1},{2,34},{34,2},{3,35},{35,3},{4,36},{36... | collective-permute-start | bytes 3145736 | tf_op jit(solution)/shard_map/ppermute | solution.py:182
  45.8 9.5 %copy-start.3 = (bf16[1024,512]{1,0:T(8,128)(2,1)}, bf16[1024,512]{1,0:T(8,128)(2,1)S(1)}, u32[]{:S(2)}) copy-start(bf16[1024,512]{1,0:T(8,128)(2,1)S(1)} %collective-permute-done.theirs_ref) | copy-start | bytes 3145732
  55.3 5.8 %copy-start.1 = (bf16[512,768]{1,0:T(8,128)(2,1)}, bf16[512,768]{1,0:T(8,128)(2,1)S(1)}, u32[]{:S(2)}) copy-start(bf16[512,768]{1,0:T(8,128)(2,1)S(1)} %get-tuple-element.13) | copy-start | bytes 2359300
  55.3 4.6 %collective-permute-start.1 = (bf16[1024,512]{1,0:T(8,128)(2,1)S(1)}, bf16[1024,512]{1,0:T(8,128)(2,1)S(1)}, u32[]{:S(2)}, u32[]{:S(2)}) collective-permute-start(bf16[1024,512]{1,0:T(8,128)(2,1)S(1)} %get-tuple-element.16), channel_id=1, source_target_pairs={{0,32},{32,0},{1,33},{33,1},{2,34},{34,2},{3,35},{35,3},{4,36},{36... | collective-permute-start | bytes 3145736 | tf_op jit(solution)/shard_map/ppermute | solution.py:182
  61.1 18.5 %all-to-all-start.2 = ((bf16[8,128,512]{2,1,0:T(8,128)(2,1)}), bf16[8,128,512]{2,1,0:T(8,128)(2,1)S(1)}, u32[]{:S(2)}, u32[]{:S(2)}) async-start(bf16[8,128,512]{2,1,0:T(8,128)(2,1)} %bitcast.21), calls=%async_computation.2 | async-start | bytes 2097152 | tf_op jit(solution)/shard_map/all_to_all | solution.py:186
  66.1 2.3 %copy-start.4 = (bf16[1024,512]{1,0:T(8,128)(2,1)S(1)}, bf16[1024,512]{1,0:T(8,128)(2,1)}, u32[]{:S(2)}) copy-start(bf16[1024,512]{1,0:T(8,128)(2,1)} %copy-done.3) | copy-start | bytes 3145732
  70.3 13.5 %copy-start.2 = (bf16[512,768]{1,0:T(8,128)(2,1)S(1)}, bf16[512,768]{1,0:T(8,128)(2,1)}, u32[]{:S(2)}) copy-start(bf16[512,768]{1,0:T(8,128)(2,1)} %copy-done.1) | copy-start | bytes 2359300
  80.4 11.1 %all-to-all-start.3 = ((bf16[8,16,512]{2,1,0:T(8,128)(2,1)}), bf16[8,16,512]{2,1,0:T(8,128)(2,1)S(1)}, u32[]{:S(2)}, u32[]{:S(2)}) async-start(bf16[8,16,512]{2,1,0:T(8,128)(2,1)} %bitcast.9), calls=%async_computation.3 | async-start | bytes 262144 | tf_op jit(solution)/shard_map/all_to_all | solution.py:186
  86.1 14.6 %copy-start.6 = (bf16[2,8,32,512]{3,2,1,0:T(8,128)(2,1)S(1)}, bf16[2,8,32,512]{3,2,1,0:T(8,128)(2,1)}, u32[]{:S(2)}) copy-start(bf16[2,8,32,512]{3,2,1,0:T(8,128)(2,1)} %param.8) | copy-start | bytes 1572868
  92.2 20.2 %all-to-all-start.4 = ((bf16[16,16,512]{2,1,0:T(8,128)(2,1)}), bf16[16,16,512]{2,1,0:T(8,128)(2,1)S(1)}, u32[]{:S(2)}, u32[]{:S(2)}) async-start(bf16[16,16,512]{2,1,0:T(8,128)(2,1)} %broadcast_in_dim.46), calls=%async_computation.4 | async-start | bytes 524288 | tf_op jit(solution)/shard_map/all_to_all | solution.py:186

commit v7 on v6

v7 whole, which is shorter than its diff:
```python
import functools
import math
import jax
import jax.numpy as jnp
from jax import lax
from jax.experimental import pallas as pl
from jax.experimental.pallas import tpu as pltpu
from jax.sharding import PartitionSpec as P

HEAD = 64
ROW = 32
SPAN = 128
STEP = 256
gain = 6.0 / HEAD
tiny_eps = 1e-06
f32, bf16 = jnp.float32, jnp.bfloat16


def dot_nn(a, b):
    return lax.dot_general(a, b, (((1,), (0,)), ((), ())), preferred_element_type=f32)


def dot_nt(a, b):
    return lax.dot_general(a, b, (((1,), (1,)), ((), ())), preferred_element_type=f32)


def dot_tn(a, b):
    return lax.dot_general(a, b, (((0,), (0,)), ((), ())), preferred_element_type=f32)


def head_ones(width):
    row = lax.broadcasted_iota(jnp.int32, (width, width), 0) // HEAD
    col = lax.broadcasted_iota(jnp.int32, (width, width), 1) // HEAD
    return jnp.where(row == col, 1.0, 0.0).astype(bf16)


def head_means(values, ones):
    return dot_nn(values.astype(bf16), ones) * (1.0 / HEAD)


def stacked(block):
    first = lax.broadcasted_iota(jnp.int32, block.shape, 1) < HEAD
    zero = jnp.zeros((), block.dtype)
    return jnp.concatenate((jnp.where(first, block, zero), jnp.where(first, zero, block)), axis=0)


def unstacked(block):
    span = block.shape[0] // 2
    first = lax.broadcasted_iota(jnp.int32, (span, block.shape[1]), 1) < HEAD
    return jnp.where(first, block[:span], block[span:])


def attention(q_half, k_half, v_half, grad_att, same_row):
    k_two, v_two = stacked(k_half), stacked(v_half)
    exps = jnp.where(same_row, jnp.exp(dot_nt(k_two, q_half) * gain), 0.0)
    grad_probs = dot_nt(v_two, grad_att)
    probs, d_scores = [], []
    for half in (slice(0, SPAN), slice(SPAN, 2 * SPAN)):
        part = exps[half] * (1.0 / jnp.sum(exps[half], axis=0, keepdims=True))
        weighted = part * grad_probs[half]
        total = jnp.sum(weighted, axis=0, keepdims=True)
        probs.append(part.astype(bf16))
        d_scores.append(((weighted - part * total) * gain).astype(bf16))
    probs, d_scores = jnp.concatenate(probs, axis=0), jnp.concatenate(d_scores, axis=0)
    return (
        dot_tn(probs, v_two).astype(bf16),
        dot_tn(d_scores, k_two),
        unstacked(dot_nn(d_scores, q_half)),
        unstacked(dot_nn(probs, grad_att)).astype(bf16),
    )


def layer_kernel(
    rows_a_ref, rows_b_ref, grads_a_ref, grads_b_ref, weights_ref,
    d_ref, out_ref, normed_ref, grads_ref, att_ref, wo_ref,
):
    step = pl.program_id(0)
    held, depth = rows_a_ref.shape
    width = depth // 2
    here = pl.ds(pl.multiple_of(step * STEP, STEP), STEP)

    @pl.when(step == 0)
    def _():
        for low, rows_ref, part_ref in (
            (0, rows_a_ref, grads_a_ref),
            (held, rows_b_ref, grads_b_ref),
        ):
            rows = rows_ref[...].astype(f32)
            inv_rms = lax.rsqrt(jnp.mean(rows * rows, axis=1, keepdims=True) + tiny_eps)
            normed_ref[low : low + held, :] = (rows * inv_rms).astype(bf16)
            grads_ref[low : low + held, :] = part_ref[...]
        for low in range(0, width, HEAD):
            for half in range(2):
                at = depth + 2 * low + half * HEAD
                wo_ref[low : low + HEAD, half * width : (half + 1) * width] = weights_ref[
                    at : at + HEAD, width:
                ]

    ones = head_ones(width)
    normed = normed_ref[here, :]
    row_of = lax.broadcasted_iota(jnp.int32, (2 * SPAN, SPAN), 0) % SPAN // ROW
    col_of = lax.broadcasted_iota(jnp.int32, (2 * SPAN, SPAN), 1) // ROW
    same_row = row_of == col_of

    query_key = dot_nn(normed, weights_ref[:depth])
    query, key = query_key[:, :width], query_key[:, width:]
    q_scale = lax.rsqrt(head_means(query * query, ones) + tiny_eps)
    k_scale = lax.rsqrt(head_means(key * key, ones) + tiny_eps)
    q_unit, k_unit = query * q_scale, key * k_scale
    q_half, k_half = q_unit.astype(bf16), k_unit.astype(bf16)
    v_half = dot_nn(normed, weights_ref[depth:, :width]).astype(bf16)
    grad_att = dot_nt(grads_ref[here, :], wo_ref[...]).astype(bf16)
    spans = []
    for low in range(0, STEP, SPAN):
        pairs = []
        for left in range(0, width, 2 * HEAD):
            at = (slice(low, low + SPAN), slice(left, left + 2 * HEAD))
            pairs.append(attention(q_half[at], k_half[at], v_half[at], grad_att[at], same_row))
        spans.append([jnp.concatenate(part, axis=1) for part in zip(*pairs)])
    attended, d_query, d_key, d_value = (jnp.concatenate(part, axis=0) for part in zip(*spans))
    att_ref[here, :] = attended
    d_ref[here, :width] = (
        q_scale * (d_query - q_unit * head_means(q_unit * d_query, ones))
    ).astype(bf16)
    d_ref[here, width:depth] = (
        k_scale * (d_key - k_unit * head_means(k_unit * d_key, ones))
    ).astype(bf16)
    d_ref[here, depth:] = d_value

    @pl.when(step == pl.num_programs(0) - 1)
    def _():
        terms = dot_tn(normed_ref[...], d_ref[...]).astype(bf16)
        out_ref[:depth, :] = terms[:, :depth]
        out_ref[depth:, :width] = terms[:, depth:]
        out_terms = dot_tn(att_ref[...], grads_ref[...]).astype(bf16)
        for low in range(0, width, HEAD):
            for half in range(2):
                at = depth + 2 * low + half * HEAD
                out_ref[at : at + HEAD, width:] = out_terms[
                    low : low + HEAD, half * width : (half + 1) * width
                ]


def layer(rows_a, rows_b, grads_a, grads_b, weights):
    held, depth = rows_a.shape
    tokens = 2 * held

    def whole(shape):
        return pl.BlockSpec(shape, lambda i: (0, 0))

    outs = [(tokens, 3 * depth // 2), weights.shape]
    ins = (rows_a, rows_b, grads_a, grads_b, weights)
    return pl.pallas_call(
        layer_kernel,
        grid=(tokens // STEP,),
        in_specs=[whole(array.shape) for array in ins],
        out_specs=[whole(shape) for shape in outs],
        out_shape=[jax.ShapeDtypeStruct(shape, bf16) for shape in outs],
        scratch_shapes=[
            pltpu.VMEM((tokens, depth), bf16),
            pltpu.VMEM((tokens, depth), bf16),
            pltpu.VMEM((tokens, depth // 2), bf16),
            pltpu.VMEM((depth // 2, depth), bf16),
        ],
        compiler_params=pltpu.CompilerParams(vmem_limit_bytes=40 * 1024 * 1024),
        cost_estimate=pl.CostEstimate(
            flops=10 * tokens * depth * depth, bytes_accessed=6 << 20, transcendentals=0
        ),
        name="attention_layer",
    )(*ins)


MESH_AXES = ("yh", "yl", "core", "x", "z")
ALL_Y = ("yh", "yl")
NEAR = ("yl", "x")


def swapped(block):
    return lax.ppermute(block, "core", [(0, 1), (1, 0)])


def sent(blocks, axis):
    return lax.all_to_all(blocks, axis, split_axis=0, concat_axis=0, tiled=True)


def blocks_of(terms, count):
    return terms.reshape(count, terms.shape[0] // count, terms.shape[1])


small = pltpu.CompilerParams(vmem_limit_bytes=8 * 1024 * 1024)


def head_lanes(shape):
    return lax.broadcasted_iota(jnp.int32, shape, 1) < HEAD


def core_heads(tiles, core):
    packed = []
    for low, high in zip(tiles[::2], tiles[1::2]):
        first = head_lanes(low.shape)
        moved = jnp.where(core == 0, high, low)
        kept = jnp.where(core == 0, low, high)
        moved = pltpu.roll(moved, HEAD, 1)
        packed.append(jnp.where(first == (core == 0), kept, moved))
    return jnp.concatenate(packed, axis=1)


def tiles_of(block):
    return [block[:, low : low + 2 * HEAD] for low in range(0, block.shape[1], 2 * HEAD)]


def copies_kernel(core_ref, yl_ref, wq_ref, wk_ref, wv_ref, wo_ref, out_ref):
    core, yl = core_ref[0], yl_ref[0]
    half = wq_ref.shape[1] // 2

    def write(parts):
        low = 0
        for part in parts:
            out_ref[:, :, low : low + part.shape[1]] = jnp.broadcast_to(
                part.astype(bf16)[None], (out_ref.shape[0],) + part.shape
            )
            low += part.shape[1]

    def own(weight_ref):
        return core_heads(tiles_of(weight_ref[...].astype(f32)), core)

    @pl.when(yl == 0)
    def _():
        write((own(wq_ref), own(wk_ref), wo_ref[:, :half]))

    @pl.when(yl == 1)
    def _():
        write((own(wv_ref), wo_ref[...]))


def weight_copies(core, yl, weights, count):
    rows, width = weights[0].shape
    smem, vmem = (pl.BlockSpec(memory_space=space) for space in (pltpu.SMEM, pltpu.VMEM))
    return pl.pallas_call(
        copies_kernel,
        in_specs=[smem, smem] + [vmem] * 4,
        out_specs=vmem,
        out_shape=jax.ShapeDtypeStruct((count, rows, 3 * width // 2), bf16),
        compiler_params=small,
        name="weight_copies",
    )(core, yl, *weights)


def lines_kernel(core_ref, yl_ref, blocks_ref, out_ref):
    count, rows, width = blocks_ref.shape
    depth, half = 2 * width // 3, width // 3
    near = out_ref.shape[0]

    def write(low, part):
        out_ref[:, :, low : low + part.shape[1]] = jnp.broadcast_to(
            part[None], (near,) + part.shape
        )

    @pl.when(yl_ref[0] == 0)
    def _():
        write(0, blocks_ref[:, :, :depth].reshape(count * rows, depth))

    @pl.when(yl_ref[0] == 1)
    def _():
        write(0, blocks_ref[:, :, :half].reshape(count * rows, half))
        heads = blocks_ref[pl.ds(core_ref[0] * (count // 2), count // 2), :, half:]
        heads = heads.reshape(count // 2 * rows, depth)
        write(half, jnp.concatenate((heads[:, :half], heads[:, half:]), axis=0))


def weight_lines(core, yl, blocks, copies):
    count, rows, width = blocks.shape
    smem, vmem = (pl.BlockSpec(memory_space=space) for space in (pltpu.SMEM, pltpu.VMEM))
    return pl.pallas_call(
        lines_kernel,
        in_specs=[smem, smem, vmem],
        out_specs=vmem,
        out_shape=jax.ShapeDtypeStruct((copies, count * rows, 2 * width // 3), bf16),
        compiler_params=small,
        name="weight_lines",
    )(core, yl, blocks)


def near_sum_kernel(core_ref, yl_ref, blocks_ref, out_ref):
    total = jnp.sum(blocks_ref[...].astype(f32), axis=0).astype(bf16)
    count, rows, _ = out_ref.shape
    depth = total.shape[1]
    half = depth // 2

    @pl.when(yl_ref[0] == 0)
    def _():
        out_ref[:, :, :depth] = total.reshape(count, rows, depth)
        out_ref[:, :, depth:] = jnp.zeros((count, rows, half), bf16)

    @pl.when(yl_ref[0] == 1)
    def _():
        out_ref[:, :, :half] = total[:, :half].reshape(count, rows, half)
        out_ref[:, :, half:] = jnp.zeros((count, rows, depth), bf16)
        here = pl.ds(core_ref[0] * (count // 2), count // 2)
        heads = total[:, half:].reshape(2, count // 2, rows, half)
        out_ref[here, :, half:depth] = heads[0]
        out_ref[here, :, depth:] = heads[1]


def near_sum(core, yl, blocks, count):
    _, rows, depth = blocks.shape
    smem, vmem = (pl.BlockSpec(memory_space=space) for space in (pltpu.SMEM, pltpu.VMEM))
    return pl.pallas_call(
        near_sum_kernel,
        in_specs=[smem, smem, vmem],
        out_specs=vmem,
        out_shape=jax.ShapeDtypeStruct((count, rows // count, 3 * depth // 2), bf16),
        compiler_params=small,
        name="near_sum",
    )(core, yl, blocks)


def final_kernel(scale, blocks_ref, *out_refs):
    count, _, width = blocks_ref.shape
    depth, half = 2 * width // 3, width // 3
    totals = []
    for place in range(4):
        total = blocks_ref[place].astype(f32)
        for yh in range(1, count // 4):
            total = total + blocks_ref[4 * yh + place].astype(f32)
        totals.append(total * scale)
    (first_a, first_b), (second_a, second_b) = totals[:2], totals[2:]
    for out_ref, one, two in (
        (out_refs[0], first_a[:, :half], first_b[:, :half]),
        (out_refs[1], first_a[:, half:depth], first_b[:, half:depth]),
        (out_refs[2], second_a[:, :half], second_b[:, :half]),
    ):
        low = 0
        for tile_one, tile_two in zip(tiles_of(one), tiles_of(two)):
            first = head_lanes(tile_one.shape)
            for place, pair in enumerate(
                ((tile_one, pltpu.roll(tile_two, HEAD, 1)), (pltpu.roll(tile_one, HEAD, 1), tile_two))
            ):
                out_ref[:, low : low + 2 * HEAD] = jnp.where(first, *pair)
                low += 2 * HEAD
    out_refs[3][...] = second_a[:, half:] + second_b[:, half:]


def final_sum(blocks, scale):
    _, rows, width = blocks.shape
    width = 2 * width // 3
    vmem = pl.BlockSpec(memory_space=pltpu.VMEM)
    return pl.pallas_call(
        functools.partial(final_kernel, scale),
        in_specs=[vmem],
        out_specs=[vmem] * 4,
        out_shape=[jax.ShapeDtypeStruct((rows, width), f32)] * 4,
        compiler_params=small,
        name="final_sum",
    )(blocks)


def local(trace_rows, upstream, counts, w_query, w_key, w_value, w_out):
    core, yl = lax.axis_index("core").reshape(1), lax.axis_index("yl").reshape(1)
    view_count, most_rows, row_length, depth = trace_rows.shape
    tokens = view_count * most_rows * row_length
    view_counts = counts.reshape(view_count)

    copies = weight_copies(core, yl, (w_query, w_key, w_value, w_out), lax.axis_size("z"))
    rows, up = trace_rows.reshape(tokens, depth), upstream.reshape(tokens, depth)
    is_live = lax.iota(jnp.int32, most_rows)[None, :] < view_counts[:, None]
    is_live = jnp.repeat(is_live.reshape(-1), row_length)[:, None]
    masked = jnp.where(is_live, up, jnp.zeros((), up.dtype))
    blocks, other_rows, other_masked = lax.optimization_barrier(
        (sent(copies, "z"), swapped(rows), swapped(masked))
    )
    lines = weight_lines(core, yl, blocks, lax.axis_size(NEAR))
    weights = sent(lines, NEAR).reshape(-1, depth)

    d_qkv, terms = layer(rows, other_rows, masked, other_masked, weights)

    z_count = lax.axis_size("z")
    total = near_sum(core, yl, sent(blocks_of(terms, lax.axis_size(NEAR)), NEAR), z_count)
    total = jnp.sum(sent(total, "z").astype(f32), axis=0).astype(bf16)
    total = jnp.broadcast_to(total[None], (lax.axis_size(ALL_Y + ("core",)),) + total.shape)
    devices = math.prod(lax.axis_size(name) for name in MESH_AXES)
    weight_grads = final_sum(
        sent(total, ALL_Y + ("core",)), 1.0 / math.sqrt(devices * tokens // 2)
    )

    grad_norm = dot_nt(d_qkv[:, :depth], weights[:depth]) + dot_nt(
        d_qkv[:, depth:], weights[depth:, : depth // 2]
    )
    grad_norm = grad_norm[:tokens] + swapped(grad_norm[tokens:].astype(bf16)).astype(f32)
    rows = rows.astype(f32)
    inv_rms = lax.rsqrt(jnp.mean(rows * rows, axis=-1, keepdims=True) + tiny_eps)
    scaled = rows * inv_rms
    done = masked.astype(f32) + inv_rms * (
        grad_norm - scaled * jnp.mean(scaled * grad_norm, axis=-1, keepdims=True)
    )
    return (done.astype(bf16).reshape(trace_rows.shape), *weight_grads)


def solution(mesh):
    fine_mesh = jax.sharding.Mesh(mesh.devices.reshape(4, 2, 2, 4, 8), MESH_AXES)
    every, peer = P(MESH_AXES), P(("x", "z"), None)
    in_specs = (every, every, P(("yh", "yl", "core"), ("x", "z")), peer, peer, peer, peer)
    out_specs = (every, peer, peer, peer, peer)
    return jax.shard_map(
        local, mesh=fine_mesh, in_specs=in_specs, out_specs=out_specs, check_vma=False
    )
```

time: 114 us -> 118 us (1.035)
  starting transfers between devices: 23.7 us -> 37.2 us
  waiting for transfers between devices: 29.7 us -> 19.3 us
  local copies, waits for them, and re-layouts: 2.03 us -> 7.62 us
  blocking collectives: 35.9 us -> 31.2 us
  matrix products: 6.47 us -> 3.47 us
  other arithmetic: 3.55 us -> 5.75 us
    ppermute x2 -> x3, starting transfers between devices: 8.24 us -> 16.7 us  [swapped(): return lax.ppermute(block, 'core', [(0, 1), (1, 0)])]
    all_to_all x3, waiting for transfers between devices: 25.2 us -> 19.2 us  [sent(): return lax.all_to_all(blocks, axis, split_axis=0, concat_axis=0, tiled=True)]
    unnamed x16 -> x20, local copies, waits for them, and re-layouts: 0.04 us -> 5.53 us
    all_to_all x3, starting transfers between devices: 15.4 us -> 20.5 us  [sent(): return lax.all_to_all(blocks, axis, split_axis=0, concat_axis=0, tiled=True)]
    all_to_all x2, blocking collectives: 35.9 us -> 31.2 us  [sent(): return lax.all_to_all(blocks, axis, split_axis=0, concat_axis=0, tiled=True)]
    ppermute x2 -> x3, waiting for transfers between devices: 4.53 us -> 0.01 us  [swapped(): return lax.ppermute(block, 'core', [(0, 1), (1, 0)])]
    dot_general x4 -> x2, matrix products: 6.47 us -> 3.47 us  [dot_nt(): lax.dot_general(a, b, (((1,), (1,)), ((), ())), preferred_element_type=f32)]
    reduce_sum x1 -> x2, other arithmetic: 0.02 us -> 1.41 us  [the longest x1 1.37 us: local(): jnp.mean(scaled * grad_norm, axis=-1, keepdims=True)]
  transfers between devices with their start and end apart: 5 -> 6, of which waited for: 5 -> 2; matrix products, arithmetic and copies ran while one was open for 8% -> 8% of each run, Pallas kernels for 0% -> 1%
where the time goes in v7:
time: 118 us; the launch traced here: 117 us
  starting transfers between devices  37.2 us (32%)
  blocking collectives  31.2 us (26%)
  waiting for transfers between devices  19.3 us (16%)
  Pallas kernels  11.4 us (10%)
  local copies, waits for them, and re-layouts  7.62 us (6%)
  other arithmetic  5.75 us (5%)
  matrix products  3.47 us (3%)
    all_to_all x2, blocking collectives, sent(): return lax.all_to_all(blocks, axis, split_axis=0, concat_axis=0, tiled=True)  31.2 us
    all_to_all x3, starting transfers between devices, sent(): return lax.all_to_all(blocks, axis, split_axis=0, concat_axis=0, tiled=True)  20.5 us
    all_to_all x3, waiting for transfers between devices, sent(): return lax.all_to_all(blocks, axis, split_axis=0, concat_axis=0, tiled=True)  19.2 us
    ppermute x3, starting transfers between devices, swapped(): return lax.ppermute(block, 'core', [(0, 1), (1, 0)])  16.7 us
    pallas_call x1, Pallas kernels, layer(): pl.pallas_call(layer_kernel, grid=(tokens // STEP,), in_specs=[whole(arra...  9.61 us
    unnamed x20, local copies, waits for them, and re-layouts  5.53 us
    dot_general x2, matrix products, dot_nt(): lax.dot_general(a, b, (((1,), (1,)), ((), ())), preferred_element_type=f32)  3.47 us
  transfers between devices with their start and end apart: 6, of which 2 were waited for; matrix products, arithmetic and copies ran while one was open for 8% of the time, Pallas kernels for 1%

profile of v7, /device:TPU:1, one launch (start us, length us, event | category | flops | bytes accessed | tf_op | source)
XLA Modules:
  0.0 116.7 jit_solution(8474902392903043809)
XLA Ops:
  0.6 0.7 iota_compare_fusion
  1.4 0.1 lt.23
  1.4 0.1 broadcast_in_dim.26
  1.5 0.1 broadcast_in_dim.27
  1.6 1.2 %bitcast_select_fusion.grads_a_ref = bf16[512,512]{1,0:T(8,128)(2,1)S(1)} fusion(bf16[2,8,32,512]{3,2,1,0:T(8,128)(2,1)} %param.8, pred[512]{0:T(512)(128)(4,1)S(1)} %broadcast_in_dim.27), kind=kLoop, calls=%fused_computation.9 | loop fusion | flops 262144 | bytes 1049088 | tf_op jit(solution)/shard_map/jit(_where)/select_n | solution.py:368
  2.8 0.0 copy-start
  2.8 8.9 %collective-permute-start.1 = (bf16[512,512]{1,0:T(8,128)(2,1)S(1)}, bf16[512,512]{1,0:T(8,128)(2,1)S(1)}, u32[]{:S(2)}, u32[]{:S(2)}) collective-permute-start(bf16[512,512]{1,0:T(8,128)(2,1)S(1)} %bitcast_select_fusion.grads_a_ref), channel_id=1, source_target_pairs={{0,32},{32,0},{1,33},{33,1},{2,34},{34,2},{3,35},{35,3},{4,36},{36... | collective-permute-start | bytes 1572872 | tf_op jit(solution)/shard_map/ppermute | solution.py:179
  11.7 1.9 %collective-permute-start = (bf16[512,512]{1,0:T(8,128)(2,1)}, bf16[512,512]{1,0:T(8,128)(2,1)S(1)}, u32[]{:S(2)}, u32[]{:S(2)}) collective-permute-start(bf16[512,512]{1,0:T(8,128)(2,1)} %bitcast.15), channel_id=1, source_target_pairs={{0,32},{32,0},{1,33},{33,1},{2,34},{34,2},{3,35},{35,3},{4,36},{36... | collective-permute-start | bytes 1572872 | tf_op jit(solution)/shard_map/ppermute | solution.py:179
  13.7 0.0 copy-start.3
  13.7 0.7 copy-done.3
  14.4 0.0 copy-start.4
  14.4 0.7 copy-done.4
  15.1 0.0 copy-start.5
  15.1 0.7 copy-done.5
  15.8 0.7 copy-done.6
  16.5 0.1 weight_copies.1
  16.6 13.7 %all_to_all.25.blocks_ref = bf16[8,16,768]{2,1,0:T(8,128)(2,1)S(1)} all-to-all(bf16[8,16,768]{2,1,0:T(8,128)(2,1)S(1)} %weight_copies.1), channel_id=1, replica_groups=mesh['yh'=4,'yl'=2,'core'=2,'x'=4,'z'=8] {'z'}, dimensions={0} | all-to-all | bytes 393216 | tf_op jit(solution)/shard_map/all_to_all | solution.py:183
  30.3 0.0 collective-permute-done.1.grads_b_ref
  30.3 0.0 collective-permute-done.rows_b_ref
  30.3 0.1 weight_lines.1
  30.4 17.5 %all_to_all.26 = bf16[8,128,512]{2,1,0:T(8,128)(2,1)S(1)} all-to-all(bf16[8,128,512]{2,1,0:T(8,128)(2,1)S(1)} %weight_lines.1), channel_id=1, replica_groups=mesh['yh'=4,'yl'=2,'core'=2,'x'=4,'z'=8] {'yl','x'}, dimensions={0} | all-to-all | bytes 2097152 | tf_op jit(solution)/shard_map/all_to_all | solution.py:183
  47.9 0.0 copy-done
  47.9 9.6 %attention_layer.1 = (bf16[1024,768]{1,0:T(8,128)(2,1)S(1)}, bf16[1024,512]{1,0:T(8,128)(2,1)S(1)}) custom-call(bf16[512,512]{1,0:T(8,128)(2,1)S(1)} %bitcast.16, bf16[512,512]{1,0:T(8,128)(2,1)S(1)} %collective-permute-done.rows_b_ref, bf16[512,512]{1,0:T(8,128)(2,1)S(1)} %bitcast_select_fusion.grads_a_ref, ...), custom_call_target="tpu_custom_call" | custom-call | flops 2684354560 | bytes 6291456 | tf_op jit(solution)/shard_map/attention_layer/pallas_call | solution.py:153
  57.6 0.0 copy-start.1
  57.6 1.2 copy-done.1
  58.7 1.0 copy-done.2
  59.7 3.6 %all-to-all-start.2 = ((bf16[8,128,512]{2,1,0:T(8,128)(2,1)}), bf16[8,128,512]{2,1,0:T(8,128)(2,1)S(1)}, u32[]{:S(2)}, u32[]{:S(2)}) async-start(bf16[8,128,512]{2,1,0:T(8,128)(2,1)} %bitcast.19), calls=%async_computation.2 | async-start | bytes 2097152 | tf_op jit(solution)/shard_map/all_to_all | solution.py:183
  63.3 2.0 %fusion = f32[1024,512]{1,0:T(8,128)S(1)} fusion(bf16[512,512]{1,0:T(8,128)(2,1)S(1)} %bitcast.20, bf16[1024,768]{1,0:T(8,128)(2,1)} %copy-done.1), kind=kOutput, calls=%fused_computation.6 | convolution fusion | flops 536870912 | bytes 3670016 | tf_op jit(solution)/shard_map/dot_general | solution.py:24
  65.3 1.5 %convolution_add_fusion = f32[1024,512]{1,0:T(8,128)S(1)} fusion(f32[1024,512]{1,0:T(8,128)S(1)} %fusion, bf16[1024,768]{1,0:T(8,128)(2,1)} %copy-done.1, bf16[1024,512]{1,0:T(8,128)(2,1)S(1)} %bitcast.18), kind=kOutput, calls=%fused_computation | convolution fusion | flops 268959744 | bytes 4980736 | tf_op jit(solution)/shard_map/dot_general | solution.py:24
  66.8 0.0 copy-start.7
  66.8 1.0 slice.45
  67.8 0.5 copy-done.7
  68.3 5.9 %collective-permute-start.2 = (bf16[512,512]{1,0:T(8,128)(2,1)}, bf16[512,512]{1,0:T(8,128)(2,1)}, u32[]{:S(2)}, u32[]{:S(2)}) collective-permute-start(bf16[512,512]{1,0:T(8,128)(2,1)} %slice.45), channel_id=1, source_target_pairs={{0,32},{32,0},{1,33},{33,1},{2,34},{34,2},{3,35},{35,3},{4,36},{36... | collective-permute-start | bytes 1572872 | tf_op jit(solution)/shard_map/ppermute | solution.py:179
  74.2 0.0 all-to-all-done.2.blocks_ref
  74.2 0.9 near_sum.1
  75.1 4.1 %all-to-all-start.3 = ((bf16[8,16,768]{2,1,0:T(8,128)(2,1)}), bf16[8,16,768]{2,1,0:T(8,128)(2,1)S(1)}, u32[]{:S(2)}, u32[]{:S(2)}) async-start(bf16[8,16,768]{2,1,0:T(8,128)(2,1)} %near_sum.1), calls=%async_computation.3 | async-start | bytes 393216 | tf_op jit(solution)/shard_map/all_to_all | solution.py:183
  79.1 0.2 multiply_reduce_fusion.1
  79.3 0.1 rsqrt.12
  79.4 8.4 %all-to-all-done.3 = bf16[8,16,768]{2,1,0:T(8,128)(2,1)S(1)} async-done(((bf16[8,16,768]{2,1,0:T(8,128)(2,1)}), bf16[8,16,768]{2,1,0:T(8,128)(2,1)S(1)}, u32[]{:S(2)}, u32[]{:S(2)}) %all-to-all-start.3) | async-done | bytes 196640 | tf_op jit(solution)/shard_map/all_to_all | solution.py:183
  87.8 0.8 broadcast_in_dim.30
  88.6 12.9 %all-to-all-start.4 = ((bf16[16,16,768]{2,1,0:T(8,128)(2,1)}), bf16[16,16,768]{2,1,0:T(8,128)(2,1)S(1)}, u32[]{:S(2)}, u32[]{:S(2)}) async-start(bf16[16,16,768]{2,1,0:T(8,128)(2,1)} %broadcast_in_dim.30), calls=%async_computation.4 | async-start | bytes 786432 | tf_op jit(solution)/shard_map/all_to_all | solution.py:183
  101.5 0.0 collective-permute-done.2
  101.5 0.0 copy-done.8
  101.5 1.4 %multiply_reduce_fusion = f32[512]{0:T(512)S(1)} fusion(bf16[512,512]{1,0:T(8,128)(2,1)} %collective-permute-done.2, f32[1024,512]{1,0:T(8,128)S(1)} %copy-done.8, f32[512]{0:T(512)S(1)} %rsqrt.12, bf16[2,8,32,512]{3,2,1,0:T(8,128)(2,1)S(1)} %copy-done), kind=kLoop, calls=%fused_computation.4 | loop fusion | flops 1572352 | bytes 2101248 | tf_op jit(solution)/shard_map/reduce_sum | solution.py:394
  102.8 0.0 copy-done.9
  102.9 2.3 %add_convert_fusion = bf16[512,512]{1,0:T(8,128)(2,1)} fusion(bf16[512,512]{1,0:T(8,128)(2,1)} %collective-permute-done.2, f32[1024,512]{1,0:T(8,128)S(1)} %copy-done.8, f32[512]{0:T(512)S(1)} %broadcast_multiply_fusion, f32[512]{0:T(512)S(1)} %rsqrt.12, bf16[2,8,32,512]{3,2,1,0:T(8,128)(2,1)S(1)} %copy-done, bf16[2,8,32,512]{3,2,1,0:T(8,128)(2,1)S(1)} %copy-done.9, ...), kind=kLoop, calls=%fused_computation.3 | loop fusion | flops 2883584 | bytes 3150336 | tf_op jit(solution)/shard_map/convert_element_type | solution.py:396
  105.1 10.9 %all-to-all-done.4.blocks_ref = bf16[16,16,768]{2,1,0:T(8,128)(2,1)S(1)} async-done(((bf16[16,16,768]{2,1,0:T(8,128)(2,1)}), bf16[16,16,768]{2,1,0:T(8,128)(2,1)S(1)}, u32[]{:S(2)}, u32[]{:S(2)}) %all-to-all-start.4) | async-done | bytes 393248 | tf_op jit(solution)/shard_map/all_to_all | solution.py:183
  116.0 0.7 final_sum.1
  (8 shorter events, 0.1 us)
Async XLA Ops:
  2.8 45.1 %copy-start = (bf16[2,8,32,512]{3,2,1,0:T(8,128)(2,1)S(1)}, bf16[2,8,32,512]{3,2,1,0:T(8,128)(2,1)}, u32[]{:S(2)}) copy-start(bf16[2,8,32,512]{3,2,1,0:T(8,128)(2,1)} %param.7) | copy-start | bytes 1572868
  2.8 27.5 %collective-permute-start.1 = (bf16[512,512]{1,0:T(8,128)(2,1)S(1)}, bf16[512,512]{1,0:T(8,128)(2,1)S(1)}, u32[]{:S(2)}, u32[]{:S(2)}) collective-permute-start(bf16[512,512]{1,0:T(8,128)(2,1)S(1)} %bitcast_select_fusion.grads_a_ref), channel_id=1, source_target_pairs={{0,32},{32,0},{1,33},{33,1},{2,34},{34,2},{3,35},{35,3},{4,36},{36... | collective-permute-start | bytes 1572872 | tf_op jit(solution)/shard_map/ppermute | solution.py:179
  11.7 18.6 %collective-permute-start = (bf16[512,512]{1,0:T(8,128)(2,1)}, bf16[512,512]{1,0:T(8,128)(2,1)S(1)}, u32[]{:S(2)}, u32[]{:S(2)}) collective-permute-start(bf16[512,512]{1,0:T(8,128)(2,1)} %bitcast.15), channel_id=1, source_target_pairs={{0,32},{32,0},{1,33},{33,1},{2,34},{34,2},{3,35},{35,3},{4,36},{36... | collective-permute-start | bytes 1572872 | tf_op jit(solution)/shard_map/ppermute | solution.py:179
  13.7 0.7 copy-start.3
  14.4 0.7 copy-start.4
  15.1 0.7 copy-start.5
  15.8 0.7 copy-start.6
  57.6 1.2 %copy-start.1 = (bf16[1024,768]{1,0:T(8,128)(2,1)}, bf16[1024,768]{1,0:T(8,128)(2,1)S(1)}, u32[]{:S(2)}) copy-start(bf16[1024,768]{1,0:T(8,128)(2,1)S(1)} %get-tuple-element.17) | copy-start | bytes 4718596
  58.7 1.0 copy-start.2
  59.7 14.5 %all-to-all-start.2 = ((bf16[8,128,512]{2,1,0:T(8,128)(2,1)}), bf16[8,128,512]{2,1,0:T(8,128)(2,1)S(1)}, u32[]{:S(2)}, u32[]{:S(2)}) async-start(bf16[8,128,512]{2,1,0:T(8,128)(2,1)} %bitcast.19), calls=%async_computation.2 | async-start | bytes 2097152 | tf_op jit(solution)/shard_map/all_to_all | solution.py:183
  66.8 1.5 %copy-start.7 = (f32[1024,512]{1,0:T(8,128)}, f32[1024,512]{1,0:T(8,128)S(1)}, u32[]{:S(2)}) copy-start(f32[1024,512]{1,0:T(8,128)S(1)} %convolution_add_fusion) | copy-start | bytes 6291460
  68.3 33.2 %collective-permute-start.2 = (bf16[512,512]{1,0:T(8,128)(2,1)}, bf16[512,512]{1,0:T(8,128)(2,1)}, u32[]{:S(2)}, u32[]{:S(2)}) collective-permute-start(bf16[512,512]{1,0:T(8,128)(2,1)} %slice.45), channel_id=1, source_target_pairs={{0,32},{32,0},{1,33},{33,1},{2,34},{34,2},{3,35},{35,3},{4,36},{36... | collective-permute-start | bytes 1572872 | tf_op jit(solution)/shard_map/ppermute | solution.py:179
  75.1 26.4 %copy-start.8 = (f32[1024,512]{1,0:T(8,128)S(1)}, f32[1024,512]{1,0:T(8,128)}, u32[]{:S(2)}) copy-start(f32[1024,512]{1,0:T(8,128)} %copy-done.7) | copy-start | bytes 6291460
  75.1 12.7 %all-to-all-start.3 = ((bf16[8,16,768]{2,1,0:T(8,128)(2,1)}), bf16[8,16,768]{2,1,0:T(8,128)(2,1)S(1)}, u32[]{:S(2)}, u32[]{:S(2)}) async-start(bf16[8,16,768]{2,1,0:T(8,128)(2,1)} %near_sum.1), calls=%async_computation.3 | async-start | bytes 393216 | tf_op jit(solution)/shard_map/all_to_all | solution.py:183
  79.1 23.7 %copy-start.9 = (bf16[2,8,32,512]{3,2,1,0:T(8,128)(2,1)S(1)}, bf16[2,8,32,512]{3,2,1,0:T(8,128)(2,1)}, u32[]{:S(2)}) copy-start(bf16[2,8,32,512]{3,2,1,0:T(8,128)(2,1)} %param.8) | copy-start | bytes 1572868
  88.6 27.4 %all-to-all-start.4 = ((bf16[16,16,768]{2,1,0:T(8,128)(2,1)}), bf16[16,16,768]{2,1,0:T(8,128)(2,1)S(1)}, u32[]{:S(2)}, u32[]{:S(2)}) async-start(bf16[16,16,768]{2,1,0:T(8,128)(2,1)} %broadcast_in_dim.30), calls=%async_computation.4 | async-start | bytes 786432 | tf_op jit(solution)/shard_map/all_to_all | solution.py:183

commit v8 on v7

v8 whole, which is shorter than its diff:
```python
import functools
import math
import jax
import jax.numpy as jnp
from jax import lax
from jax.experimental import pallas as pl
from jax.experimental.pallas import tpu as pltpu
from jax.sharding import PartitionSpec as P

HEAD = 64
ROW = 32
SPAN = 128
STEP = 256
gain = 6.0 / HEAD
tiny_eps = 1e-06
f32, bf16 = jnp.float32, jnp.bfloat16


def dot_nn(a, b):
    return lax.dot_general(a, b, (((1,), (0,)), ((), ())), preferred_element_type=f32)


def dot_nt(a, b):
    return lax.dot_general(a, b, (((1,), (1,)), ((), ())), preferred_element_type=f32)


def dot_tn(a, b):
    return lax.dot_general(a, b, (((0,), (0,)), ((), ())), preferred_element_type=f32)


def head_ones(width):
    row = lax.broadcasted_iota(jnp.int32, (width, width), 0) // HEAD
    col = lax.broadcasted_iota(jnp.int32, (width, width), 1) // HEAD
    return jnp.where(row == col, 1.0, 0.0).astype(bf16)


def head_means(values, ones):
    return dot_nn(values.astype(bf16), ones) * (1.0 / HEAD)


def stacked(block):
    first = lax.broadcasted_iota(jnp.int32, block.shape, 1) < HEAD
    zero = jnp.zeros((), block.dtype)
    return jnp.concatenate((jnp.where(first, block, zero), jnp.where(first, zero, block)), axis=0)


def unstacked(block):
    span = block.shape[0] // 2
    first = lax.broadcasted_iota(jnp.int32, (span, block.shape[1]), 1) < HEAD
    return jnp.where(first, block[:span], block[span:])


def attention(q_half, k_half, v_half, grad_att, same_row):
    k_two, v_two = stacked(k_half), stacked(v_half)
    exps = jnp.where(same_row, jnp.exp(dot_nt(k_two, q_half) * gain), 0.0)
    grad_probs = dot_nt(v_two, grad_att)
    probs, d_scores = [], []
    for half in (slice(0, SPAN), slice(SPAN, 2 * SPAN)):
        part = exps[half] * (1.0 / jnp.sum(exps[half], axis=0, keepdims=True))
        weighted = part * grad_probs[half]
        total = jnp.sum(weighted, axis=0, keepdims=True)
        probs.append(part.astype(bf16))
        d_scores.append(((weighted - part * total) * gain).astype(bf16))
    probs, d_scores = jnp.concatenate(probs, axis=0), jnp.concatenate(d_scores, axis=0)
    return (
        dot_tn(probs, v_two).astype(bf16),
        dot_tn(d_scores, k_two),
        unstacked(dot_nn(d_scores, q_half)),
        unstacked(dot_nn(probs, grad_att)).astype(bf16),
    )


def layer_kernel(
    normed_ref, grads_ref, weights_ref, d_out_ref, terms_ref, d_ref, out_ref, att_ref, wo_ref, sems
):
    step = pl.program_id(0)
    depth = normed_ref.shape[1]
    width, tile = depth // 2, 2 * HEAD
    used = width + tile
    here = pl.ds(pl.multiple_of(step * STEP, STEP), STEP)

    def wo_parts():
        for low in range(0, width, HEAD):
            for part in range(4):
                at = part // 2 * depth + 2 * low + part % 2 * HEAD
                rows, cols = slice(low, low + HEAD), slice(part * tile, (part + 1) * tile)
                yield (rows, cols), (slice(at, at + HEAD), slice(used, depth))

    @pl.when(step == 0)
    def _():
        for inner, outer in wo_parts():
            wo_ref[inner] = weights_ref[outer]

    ones = head_ones(width)
    normed = normed_ref[here, :]
    row_of = lax.broadcasted_iota(jnp.int32, (2 * SPAN, SPAN), 0) % SPAN // ROW
    col_of = lax.broadcasted_iota(jnp.int32, (2 * SPAN, SPAN), 1) // ROW
    same_row = row_of == col_of

    first = dot_nn(normed, weights_ref[:depth, :used])
    second = dot_nn(normed, weights_ref[depth:, :used])
    query, key = first[:, :width], jnp.concatenate((first[:, width:], second[:, width:]), axis=1)
    q_scale = lax.rsqrt(head_means(query * query, ones) + tiny_eps)
    k_scale = lax.rsqrt(head_means(key * key, ones) + tiny_eps)
    q_unit, k_unit = query * q_scale, key * k_scale
    q_half, k_half = q_unit.astype(bf16), k_unit.astype(bf16)
    v_half = second[:, :width].astype(bf16)
    grad_att = dot_nt(grads_ref[here, :], wo_ref[...]).astype(bf16)
    spans = []
    for low in range(0, STEP, SPAN):
        pairs = []
        for left in range(0, width, tile):
            at = (slice(low, low + SPAN), slice(left, left + tile))
            pairs.append(attention(q_half[at], k_half[at], v_half[at], grad_att[at], same_row))
        spans.append([jnp.concatenate(part, axis=1) for part in zip(*pairs)])
    attended, d_query, d_key, d_value = (jnp.concatenate(part, axis=0) for part in zip(*spans))
    att_ref[here, :] = attended
    d_query = (q_scale * (d_query - q_unit * head_means(q_unit * d_query, ones))).astype(bf16)
    d_key = (k_scale * (d_key - k_unit * head_means(k_unit * d_key, ones))).astype(bf16)
    d_ref[here, :width] = d_query
    d_ref[here, width:used] = d_key[:, :tile]
    d_ref[here, used : used + width] = d_value
    d_ref[here, used + width :] = d_key[:, tile:]

    @pl.when(step == pl.num_programs(0) - 1)
    def _():
        def sent_out(part):
            rows = pl.ds(part * depth, depth)
            return pltpu.make_async_copy(out_ref.at[rows], terms_ref.at[rows], sems.at[part])

        d_sent = pltpu.make_async_copy(d_ref, d_out_ref, sems.at[2])
        d_sent.start()
        out_terms = dot_tn(att_ref[...], grads_ref[...]).astype(bf16)
        for inner, outer in wo_parts():
            out_ref[outer] = out_terms[inner]
        out_ref[:depth, :used] = dot_tn(normed_ref[...], d_ref[:, :used]).astype(bf16)
        sent_out(0).start()
        out_ref[depth:, :used] = dot_tn(normed_ref[...], d_ref[:, used:]).astype(bf16)
        sent_out(1).start()
        d_sent.wait()
        sent_out(0).wait()
        sent_out(1).wait()


def layer(normed, grads, weights):
    tokens, depth = normed.shape

    def whole(shape):
        return pl.BlockSpec(shape, lambda i: (0, 0))

    outs = [(tokens, 3 * depth // 2), weights.shape]
    ins = (normed, grads, weights)
    return pl.pallas_call(
        layer_kernel,
        grid=(tokens // STEP,),
        in_specs=[whole(array.shape) for array in ins],
        out_specs=[pl.BlockSpec(memory_space=pltpu.HBM)] * 2,
        out_shape=[jax.ShapeDtypeStruct(shape, bf16) for shape in outs],
        scratch_shapes=[pltpu.VMEM(shape, bf16) for shape in outs]
        + [
            pltpu.VMEM((tokens, depth // 2), bf16),
            pltpu.VMEM((depth // 2, depth), bf16),
            pltpu.SemaphoreType.DMA((3,)),
        ],
        compiler_params=pltpu.CompilerParams(vmem_limit_bytes=40 * 1024 * 1024),
        cost_estimate=pl.CostEstimate(
            flops=10 * tokens * depth * depth, bytes_accessed=6 << 20, transcendentals=0
        ),
        name="attention_layer",
    )(*ins)


MESH_AXES = ("yh", "yl", "core", "x", "z")
ALL_Y = ("yh", "yl")
NEAR = ("yl", "x")


def swapped(block):
    return lax.ppermute(block, "core", [(0, 1), (1, 0)])


def sent(blocks, axis):
    return lax.all_to_all(blocks, axis, split_axis=0, concat_axis=0, tiled=True)


def blocks_of(terms, count):
    return terms.reshape(count, terms.shape[0] // count, terms.shape[1])


small = pltpu.CompilerParams(vmem_limit_bytes=8 * 1024 * 1024)


def head_lanes(shape):
    return lax.broadcasted_iota(jnp.int32, shape, 1) < HEAD


def core_heads(tiles, core):
    packed = []
    for low, high in zip(tiles[::2], tiles[1::2]):
        first = head_lanes(low.shape)
        moved = jnp.where(core == 0, high, low)
        kept = jnp.where(core == 0, low, high)
        moved = pltpu.roll(moved, HEAD, 1)
        packed.append(jnp.where(first == (core == 0), kept, moved))
    return jnp.concatenate(packed, axis=1)


def tiles_of(block):
    return [block[:, low : low + 2 * HEAD] for low in range(0, block.shape[1], 2 * HEAD)]


def copies_kernel(core_ref, yl_ref, wq_ref, wk_ref, wv_ref, wo_ref, out_ref):
    core = core_ref[0]
    width, tile = wq_ref.shape[1] // 2, 2 * HEAD

    def own(weight_ref):
        return core_heads(tiles_of(weight_ref[...].astype(f32)), core)

    for yl, first_ref in enumerate((wq_ref, wv_ref)):

        @pl.when(yl_ref[0] == yl)
        def _():
            low = 0
            for part in (
                own(first_ref),
                own(wk_ref)[:, yl * tile : (yl + 1) * tile],
                wo_ref[:, yl * width : (yl + 1) * width],
            ):
                out_ref[:, :, low : low + part.shape[1]] = jnp.broadcast_to(
                    part.astype(bf16)[None], (out_ref.shape[0],) + part.shape
                )
                low += part.shape[1]


def weight_copies(core, yl, weights, count):
    rows, width = weights[0].shape
    smem = pl.BlockSpec(memory_space=pltpu.SMEM)
    out = (count, rows, width + 2 * HEAD)
    return pl.pallas_call(
        copies_kernel,
        grid=(1,),
        in_specs=[smem, smem] + [pl.BlockSpec((rows, width), lambda i: (0, 0))] * 4,
        out_specs=pl.BlockSpec(out, lambda i: (0, 0, 0)),
        out_shape=jax.ShapeDtypeStruct(out, bf16),
        name="weight_copies",
    )(core, yl, *weights)


def lines_kernel(core_ref, blocks_ref, out_ref):
    count, rows, _ = blocks_ref.shape
    near, _, depth = out_ref.shape
    tile = 2 * HEAD
    used = depth - tile

    def write(low, part):
        out_ref[:, :, low : low + part.shape[1]] = jnp.broadcast_to(
            part[None], (near,) + part.shape
        )

    write(0, blocks_ref[:, :, :used].reshape(count * rows, used))
    heads = blocks_ref[pl.ds(core_ref[0] * (count // 2), count // 2), :, used:]
    heads = heads.reshape(count // 2 * rows, 2 * tile)
    write(used, jnp.concatenate((heads[:, :tile], heads[:, tile:]), axis=0))


def weight_lines(core, blocks, copies):
    count, rows, width = blocks.shape
    smem, vmem = (pl.BlockSpec(memory_space=space) for space in (pltpu.SMEM, pltpu.VMEM))
    return pl.pallas_call(
        lines_kernel,
        in_specs=[smem, vmem],
        out_specs=vmem,
        out_shape=jax.ShapeDtypeStruct((copies, count * rows, width - 2 * HEAD), bf16),
        compiler_params=small,
        name="weight_lines",
    )(core, blocks)


def near_sum_kernel(core_ref, blocks_ref, out_ref):
    total = jnp.sum(blocks_ref[...].astype(f32), axis=0).astype(bf16)
    count, rows, width = out_ref.shape
    tile = 2 * HEAD
    used = width - 2 * tile
    out_ref[:, :, :used] = total[:, :used].reshape(count, rows, used)
    out_ref[:, :, used:] = jnp.zeros((count, rows, 2 * tile), bf16)
    here = pl.ds(core_ref[0] * (count // 2), count // 2)
    heads = total[:, used:].reshape(2, count // 2, rows, tile)
    out_ref[here, :, used : used + tile] = heads[0]
    out_ref[here, :, used + tile :] = heads[1]


def near_sum(core, blocks, count):
    _, rows, depth = blocks.shape
    smem, vmem = (pl.BlockSpec(memory_space=space) for space in (pltpu.SMEM, pltpu.VMEM))
    return pl.pallas_call(
        near_sum_kernel,
        in_specs=[smem, vmem],
        out_specs=vmem,
        out_shape=jax.ShapeDtypeStruct((count, rows // count, depth + 2 * HEAD), bf16),
        compiler_params=small,
        name="near_sum",
    )(core, blocks)


def final_kernel(scale, blocks_ref, *out_refs):
    count, _, width = blocks_ref.shape
    tile = 2 * HEAD
    half = 2 * tile
    totals = []
    for place in range(4):
        total = blocks_ref[place].astype(f32)
        for yh in range(1, count // 4):
            total = total + blocks_ref[4 * yh + place].astype(f32)
        totals.append(total * scale)
    (first_a, first_b), (second_a, second_b) = totals[:2], totals[2:]
    for out_ref, pairs in (
        (out_refs[0], [(first_a, first_b, low) for low in (0, tile)]),
        (out_refs[1], [(first_a, first_b, half), (second_a, second_b, half)]),
        (out_refs[2], [(second_a, second_b, low) for low in (0, tile)]),
    ):
        at = 0
        for one, two, low in pairs:
            one, two = one[:, low : low + tile], two[:, low : low + tile]
            first = head_lanes(one.shape)
            for blended in ((one, pltpu.roll(two, HEAD, 1)), (pltpu.roll(one, HEAD, 1), two)):
                out_ref[:, at : at + tile] = jnp.where(first, *blended)
                at += tile
    for yl, (one, two) in enumerate(((first_a, first_b), (second_a, second_b))):
        out_refs[3][:, yl * half : (yl + 1) * half] = one[:, half + tile :] + two[:, half + tile :]


def final_sum(blocks, scale):
    _, rows, width = blocks.shape
    width = width - 2 * HEAD
    vmem = pl.BlockSpec(memory_space=pltpu.VMEM)
    return pl.pallas_call(
        functools.partial(final_kernel, scale),
        in_specs=[vmem],
        out_specs=[vmem] * 4,
        out_shape=[jax.ShapeDtypeStruct((rows, width), f32)] * 4,
        compiler_params=small,
        name="final_sum",
    )(blocks)


def local(trace_rows, upstream, counts, w_query, w_key, w_value, w_out):
    core, yl = lax.axis_index("core").reshape(1), lax.axis_index("yl").reshape(1)
    view_count, most_rows, row_length, depth = trace_rows.shape
    tokens = view_count * most_rows * row_length
    view_counts = counts.reshape(view_count)

    copies = weight_copies(core, yl, (w_query, w_key, w_value, w_out), lax.axis_size("z"))
    rows, up = trace_rows.reshape(tokens, depth), upstream.reshape(tokens, depth)
    is_live = lax.iota(jnp.int32, most_rows)[None, :] < view_counts[:, None]
    is_live = jnp.repeat(is_live.reshape(-1), row_length)[:, None]
    masked = jnp.where(is_live, up, jnp.zeros((), up.dtype))
    blocks = sent(copies, "z")
    lines = weight_lines(core, blocks, lax.axis_size(NEAR))
    weights = sent(lines, NEAR).reshape(-1, depth)

    both_rows = jnp.concatenate((rows, swapped(rows)), axis=0).astype(f32)
    both_masked = jnp.concatenate((masked, swapped(masked)), axis=0)
    inv_rms = lax.rsqrt(jnp.mean(both_rows * both_rows, axis=-1, keepdims=True) + tiny_eps)
    normed = (both_rows * inv_rms).astype(bf16)
    d_qkv, terms = layer(normed, both_masked, weights)

    z_count = lax.axis_size("z")
    total = near_sum(core, sent(blocks_of(terms, lax.axis_size(NEAR)), NEAR), z_count)
    total = jnp.sum(sent(total, "z").astype(f32), axis=0).astype(bf16)
    total = jnp.broadcast_to(total[None], (lax.axis_size(ALL_Y + ("core",)),) + total.shape)
    devices = math.prod(lax.axis_size(name) for name in MESH_AXES)
    weight_grads = final_sum(
        sent(total, ALL_Y + ("core",)), 1.0 / math.sqrt(devices * tokens // 2)
    )

    used = d_qkv.shape[1] // 2
    grad_norm = dot_nt(d_qkv[:, :used], weights[:depth, :used]) + dot_nt(
        d_qkv[:, used:], weights[depth:, :used]
    )
    grad_norm = grad_norm[:tokens] + swapped(grad_norm[tokens:].astype(bf16)).astype(f32)
    inv_rms = inv_rms[:tokens]
    scaled = both_rows[:tokens] * inv_rms
    done = masked.astype(f32) + inv_rms * (
        grad_norm - scaled * jnp.mean(scaled * grad_norm, axis=-1, keepdims=True)
    )
    return (done.astype(bf16).reshape(trace_rows.shape), *weight_grads)


def solution(mesh):
    fine_mesh = jax.sharding.Mesh(mesh.devices.reshape(4, 2, 2, 4, 8), MESH_AXES)
    every, peer = P(MESH_AXES), P(("x", "z"), None)
    in_specs = (every, every, P(("yh", "yl", "core"), ("x", "z")), peer, peer, peer, peer)
    out_specs = (every, peer, peer, peer, peer)
    return jax.shard_map(
        local, mesh=fine_mesh, in_specs=in_specs, out_specs=out_specs, check_vma=False
    )
```

time: 118 us -> 108 us (0.915)
  blocking collectives: 31.2 us -> 19 us
  waiting for transfers between devices: 19.3 us -> 23.8 us
  Pallas kernels: 11.4 us -> 14.7 us
  starting transfers between devices: 37.2 us -> 34.7 us
  local copies, waits for them, and re-layouts: 7.62 us -> 5.4 us
    all_to_all x2 -> x1, blocking collectives: 31.2 us -> 19 us  [sent(): return lax.all_to_all(blocks, axis, split_axis=0, concat_axis=0, tiled=True)]
    ppermute x3, starting transfers between devices: 16.7 us -> 9.97 us  [swapped(): return lax.ppermute(block, 'core', [(0, 1), (1, 0)])]
    all_to_all x3 -> x4, starting transfers between devices: 20.5 us -> 24.7 us  [sent(): return lax.all_to_all(blocks, axis, split_axis=0, concat_axis=0, tiled=True)]
    all_to_all x3 -> x4, waiting for transfers between devices: 19.2 us -> 22.7 us  [sent(): return lax.all_to_all(blocks, axis, split_axis=0, concat_axis=0, tiled=True)]
    pallas_call x3, Pallas kernels: 1.05 us -> 3.53 us  [the longest x1 1.61 us: weight_copies(): pl.pallas_call(copies_kernel, grid=(1,), in_specs=[smem, smem] + [pl.Bloc...]
    unnamed x20 -> x28, local copies, waits for them, and re-layouts: 5.53 us -> 3.51 us
    convert_element_type x0 -> x2, other arithmetic: none -> 1.9 us  [the longest x1 1.61 us: local(): both_rows = jnp.concatenate((rows, swapped(rows)), axis=0).astype(f32)]
  transfers between devices with their start and end apart: 6 -> 7, of which waited for: 2 -> 5; matrix products, arithmetic and copies ran while one was open for 8% -> 10% of each run, Pallas kernels for 1% -> 1%
where the time goes in v8:
time: 108 us
  starting transfers between devices  34.7 us (32%)
  waiting for transfers between devices  23.8 us (22%)
  blocking collectives  19 us (18%)
  Pallas kernels  14.7 us (14%)
  other arithmetic  6.52 us (6%)
  local copies, waits for them, and re-layouts  5.4 us (5%)
  matrix products  2.72 us (3%)
    all_to_all x4, starting transfers between devices, sent(): return lax.all_to_all(blocks, axis, split_axis=0, concat_axis=0, tiled=True)  24.7 us
    all_to_all x4, waiting for transfers between devices, sent(): return lax.all_to_all(blocks, axis, split_axis=0, concat_axis=0, tiled=True)  22.7 us
    all_to_all x1, blocking collectives, sent(): return lax.all_to_all(blocks, axis, split_axis=0, concat_axis=0, tiled=True)  19 us
    pallas_call x1, Pallas kernels, layer(): pl.pallas_call(layer_kernel, grid=(tokens // STEP,), in_specs=[whole(arra...  10.5 us
    ppermute x3, starting transfers between devices, swapped(): return lax.ppermute(block, 'core', [(0, 1), (1, 0)])  9.97 us
    unnamed x28, local copies, waits for them, and re-layouts  3.51 us
    dot_general x2, matrix products, dot_nt(): lax.dot_general(a, b, (((1,), (1,)), ((), ())), preferred_element_type=f32)  2.72 us
    convert_element_type x1, other arithmetic, local(): return (done.astype(bf16).reshape(trace_rows.shape), *weight_grads)  2.24 us
  transfers between devices with their start and end apart: 7, of which 5 were waited for; matrix products, arithmetic and copies ran while one was open for 10% of the time, Pallas kernels for 1%

profile of v8, /device:TPU:1, one launch (start us, length us, event | category | flops | bytes accessed | tf_op | source)
XLA Modules:
  0.0 107.8 jit_solution(2689499085606635011)
XLA Ops:
  0.6 0.0 copy-start.5
  0.7 0.0 copy-start.11
  0.7 1.6 %weight_copies.1 = bf16[8,16,640]{2,1,0:T(8,128)(2,1)} custom-call(s32[1]{0:T(128)} %bitcast.3.core_ref, s32[1]{0:T(128)} %bitcast.4.yl_ref, bf16[16,512]{1,0:T(8,128)(2,1)} %wq_ref.1, bf16[16,512]{1,0:T(8,128)(2,1)} %wk_ref.1, bf16[16,512]{1,0:T(8,128)(2,1)} %wv_ref.1, bf16[16,512]{1,0:T(8,128)(2,1)} %wo_ref.1), custom_call_target="tpu_custom_call" | custom-call | tf_op jit(solution)/shard_map/weight_copies/pallas_call | solution.py:239
  2.3 19.0 %all_to_all.25.blocks_ref = bf16[8,16,640]{2,1,0:T(8,128)(2,1)S(1)} all-to-all(bf16[8,16,640]{2,1,0:T(8,128)(2,1)} %weight_copies.1), channel_id=1, replica_groups=mesh['yh'=4,'yl'=2,'core'=2,'x'=4,'z'=8] {'z'}, dimensions={0} | all-to-all | bytes 327680 | tf_op jit(solution)/shard_map/all_to_all | solution.py:183
  21.3 1.1 %weight_lines.1 = bf16[8,128,512]{2,1,0:T(8,128)(2,1)} custom-call(s32[1]{0:T(128)} %bitcast.3.core_ref, bf16[8,16,640]{2,1,0:T(8,128)(2,1)S(1)} %all_to_all.25.blocks_ref), custom_call_target="tpu_custom_call" | custom-call | tf_op jit(solution)/shard_map/weight_lines/pallas_call | solution.py:269
  22.4 5.0 %all-to-all-start.1 = ((bf16[8,128,512]{2,1,0:T(8,128)(2,1)}), bf16[8,128,512]{2,1,0:T(8,128)(2,1)S(1)}, u32[]{:S(2)}, u32[]{:S(2)}) async-start(bf16[8,128,512]{2,1,0:T(8,128)(2,1)} %weight_lines.1), calls=%async_computation.1 | async-start | bytes 2097152 | tf_op jit(solution)/shard_map/all_to_all | solution.py:183
  27.4 4.8 %collective-permute-start = (bf16[512,512]{1,0:T(8,128)(2,1)S(1)}, bf16[512,512]{1,0:T(8,128)(2,1)S(1)}, u32[]{:S(2)}, u32[]{:S(2)}) collective-permute-start(bf16[512,512]{1,0:T(8,128)(2,1)S(1)} %bitcast.14), channel_id=1, source_target_pairs={{0,32},{32,0},{1,33},{33,1},{2,34},{34,2},{3,35},{35,3},{4,36},{36... | collective-permute-start | bytes 1572872 | tf_op jit(solution)/shard_map/ppermute | solution.py:179
  32.2 0.1 iota_compare_fusion
  32.3 0.1 lt.23
  32.4 0.1 broadcast_in_dim.26
  32.4 0.1 broadcast_in_dim.27
  32.5 0.0 copy-done.11
  32.5 0.1 bitcast_select_fusion
  32.7 2.1 %collective-permute-start.1 = (bf16[512,512]{1,0:T(8,128)(2,1)S(1)}, bf16[512,512]{1,0:T(8,128)(2,1)S(1)}, u32[]{:S(2)}, u32[]{:S(2)}) collective-permute-start(bf16[512,512]{1,0:T(8,128)(2,1)S(1)} %bitcast_select_fusion), channel_id=1, source_target_pairs={{0,32},{32,0},{1,33},{33,1},{2,34},{34,2},{3,35},{35,3},{4,36},{36... | collective-permute-start | bytes 1572872 | tf_op jit(solution)/shard_map/ppermute | solution.py:179
  34.7 0.0 collective-permute-done
  34.8 0.0 copy-start.8
  34.8 0.3 multiply_reduce_fusion
  35.0 0.5 copy-done.8
  35.6 1.1 collective-permute-done.1
  36.6 0.1 pad_maximum_fusion.grads_ref
  36.7 0.9 copy-done.9
  37.7 0.3 multiply_convert_fusion.normed_ref
  38.0 0.4 all-to-all-done.1
  38.4 10.5 %attention_layer.1 = (bf16[1024,768]{1,0:T(8,128)(2,1)S(1)}, bf16[1024,512]{1,0:T(8,128)(2,1)}) custom-call(bf16[1024,512]{1,0:T(8,128)(2,1)S(1)} %multiply_convert_fusion.normed_ref, bf16[1024,512]{1,0:T(8,128)(2,1)S(1)} %pad_maximum_fusion.grads_ref, bf16[1024,512]{1,0:T(8,128)(2,1)S(1)} %bitcast.11), custom_call_target="tpu_custom_call" | custom-call | flops 2684354560 | bytes 6291456 | tf_op jit(solution)/shard_map/attention_layer/pallas_call | solution.py:153
  48.8 1.2 %copy-done = bf16[1024,768]{1,0:T(8,128)(2,1)} copy-done((bf16[1024,768]{1,0:T(8,128)(2,1)}, bf16[1024,768]{1,0:T(8,128)(2,1)S(1)}, u32[]{:S(2)}) %copy-start) | copy-done | bytes 1572888
  50.0 7.2 %all-to-all-start.2 = ((bf16[8,128,512]{2,1,0:T(8,128)(2,1)}), bf16[8,128,512]{2,1,0:T(8,128)(2,1)S(1)}, u32[]{:S(2)}, u32[]{:S(2)}) async-start(bf16[8,128,512]{2,1,0:T(8,128)(2,1)} %bitcast.7), calls=%async_computation.2 | async-start | bytes 2097152 | tf_op jit(solution)/shard_map/all_to_all | solution.py:183
  57.2 2.0 %fusion.1 = f32[1024,512]{1,0:T(8,128)S(1)} fusion(bf16[1024,768]{1,0:T(8,128)(2,1)} %copy-done, bf16[1024,512]{1,0:T(8,128)(2,1)S(1)} %bitcast.12), kind=kOutput, calls=%fused_computation.11 | convolution fusion | flops 402653184 | bytes 3276800 | tf_op jit(solution)/shard_map/dot_general | solution.py:24
  59.2 0.7 convolution_add_fusion
  60.0 0.0 copy-start.7
  60.0 0.0 copy-start.10
  60.0 0.9 slice.58
  60.9 0.6 copy-done.2
  61.5 3.2 %collective-permute-start.2 = (bf16[512,512]{1,0:T(8,128)(2,1)}, bf16[512,512]{1,0:T(8,128)(2,1)}, u32[]{:S(2)}, u32[]{:S(2)}) collective-permute-start(bf16[512,512]{1,0:T(8,128)(2,1)} %slice.58), channel_id=1, source_target_pairs={{0,32},{32,0},{1,33},{33,1},{2,34},{34,2},{3,35},{35,3},{4,36},{36... | collective-permute-start | bytes 1572872 | tf_op jit(solution)/shard_map/ppermute | solution.py:179
  64.6 7.1 %all-to-all-done.2.blocks_ref = bf16[8,128,512]{2,1,0:T(8,128)(2,1)S(1)} async-done(((bf16[8,128,512]{2,1,0:T(8,128)(2,1)}), bf16[8,128,512]{2,1,0:T(8,128)(2,1)S(1)}, u32[]{:S(2)}, u32[]{:S(2)}) %all-to-all-start.2) | async-done | bytes 1048608 | tf_op jit(solution)/shard_map/all_to_all | solution.py:183
  71.8 0.8 near_sum.1
  72.6 3.5 %all-to-all-start.3 = ((bf16[8,16,640]{2,1,0:T(8,128)(2,1)}), bf16[8,16,640]{2,1,0:T(8,128)(2,1)S(1)}, u32[]{:S(2)}, u32[]{:S(2)}) async-start(bf16[8,16,640]{2,1,0:T(8,128)(2,1)} %near_sum.1), calls=%async_computation.3 | async-start | bytes 327680 | tf_op jit(solution)/shard_map/all_to_all | solution.py:183
  76.1 0.0 copy-done.7
  76.1 0.0 copy-done.10
  76.2 1.6 %maximum_convert_fusion = f32[1024,512]{1,0:T(8,128)} fusion(bf16[512,512]{1,0:T(8,128)(2,1)S(1)} %copy-done.10, bf16[512,512]{1,0:T(8,128)(2,1)S(1)} %bitcast.17), kind=kLoop, calls=%fused_computation.6 | loop fusion | flops 2097152 | bytes 3145728 | tf_op jit(solution)/shard_map/convert_element_type | solution.py:361
  77.8 6.4 %all-to-all-done.3 = bf16[8,16,640]{2,1,0:T(8,128)(2,1)S(1)} async-done(((bf16[8,16,640]{2,1,0:T(8,128)(2,1)}), bf16[8,16,640]{2,1,0:T(8,128)(2,1)S(1)}, u32[]{:S(2)}, u32[]{:S(2)}) %all-to-all-start.3) | async-done | bytes 163872 | tf_op jit(solution)/shard_map/all_to_all | solution.py:183
  84.2 0.8 broadcast_in_dim.30
  85.0 9.0 %all-to-all-start.4 = ((bf16[16,16,640]{2,1,0:T(8,128)(2,1)}), bf16[16,16,640]{2,1,0:T(8,128)(2,1)S(1)}, u32[]{:S(2)}, u32[]{:S(2)}) async-start(bf16[16,16,640]{2,1,0:T(8,128)(2,1)} %broadcast_in_dim.30), calls=%async_computation.4 | async-start | bytes 655360 | tf_op jit(solution)/shard_map/all_to_all | solution.py:183
  94.0 0.0 collective-permute-done.2
  94.0 1.8 %multiply_reduce_fusion.1 = f32[512]{0:T(512)S(1)} fusion(f32[1024,512]{1,0:T(8,128)} %maximum_convert_fusion, bf16[512,512]{1,0:T(8,128)(2,1)} %collective-permute-done.2, f32[1024,512]{1,0:T(8,128)S(1)} %copy-done.3, f32[512]{0:T(512)S(1)} %slice.26), kind=kLoop, calls=%fused_computation.9 | loop fusion | flops 1310208 | bytes 2625536 | tf_op jit(solution)/shard_map/reduce_sum | solution.py:384
  95.8 0.2 copy-done.4
  96.0 2.2 %add_convert_fusion = bf16[512,512]{1,0:T(8,128)(2,1)} fusion(f32[1024,512]{1,0:T(8,128)S(1)} %copy-done.4, bf16[512,512]{1,0:T(8,128)(2,1)} %collective-permute-done.2, f32[1024,512]{1,0:T(8,128)S(1)} %copy-done.3, f32[512]{0:T(512)S(1)} %broadcast_multiply_fusion, f32[512]{0:T(512)S(1)} %slice.26, bf16[2,8,32,512]{3,2,1,0:T(8,128)(2,1)S(1)} %copy-done.12, ...), kind=kLoop, calls=%fused_computation.8 | loop fusion | flops 2621440 | bytes 3674624 | tf_op jit(solution)/shard_map/convert_element_type | solution.py:386
  98.3 8.8 %all-to-all-done.4.blocks_ref = bf16[16,16,640]{2,1,0:T(8,128)(2,1)S(1)} async-done(((bf16[16,16,640]{2,1,0:T(8,128)(2,1)}), bf16[16,16,640]{2,1,0:T(8,128)(2,1)S(1)}, u32[]{:S(2)}, u32[]{:S(2)}) %all-to-all-start.4) | async-done | bytes 327712 | tf_op jit(solution)/shard_map/all_to_all | solution.py:183
  107.0 0.7 final_sum.1
  (19 shorter events, 0.1 us)
Async XLA Ops:
  0.6 26.8 %copy-start.5 = (bf16[2,8,32,512]{3,2,1,0:T(8,128)(2,1)S(1)}, bf16[2,8,32,512]{3,2,1,0:T(8,128)(2,1)}, u32[]{:S(2)}) copy-start(bf16[2,8,32,512]{3,2,1,0:T(8,128)(2,1)} %param.7) | copy-start | bytes 1572868
  0.6 31.6 %copy-start.13 = (s32[1,2]{1,0:T(1,128)S(1)}, s32[1,2]{1,0:T(1,128)}, u32[]{:S(2)}) copy-start(s32[1,2]{1,0:T(1,128)} %param.9) | copy-start | bytes 28
  0.7 31.9 %copy-start.11 = (bf16[2,8,32,512]{3,2,1,0:T(8,128)(2,1)S(1)}, bf16[2,8,32,512]{3,2,1,0:T(8,128)(2,1)}, u32[]{:S(2)}) copy-start(bf16[2,8,32,512]{3,2,1,0:T(8,128)(2,1)} %param.8) | copy-start | bytes 1572868
  22.4 16.0 %all-to-all-start.1 = ((bf16[8,128,512]{2,1,0:T(8,128)(2,1)}), bf16[8,128,512]{2,1,0:T(8,128)(2,1)S(1)}, u32[]{:S(2)}, u32[]{:S(2)}) async-start(bf16[8,128,512]{2,1,0:T(8,128)(2,1)} %weight_lines.1), calls=%async_computation.1 | async-start | bytes 2097152 | tf_op jit(solution)/shard_map/all_to_all | solution.py:183
  27.4 7.3 %collective-permute-start = (bf16[512,512]{1,0:T(8,128)(2,1)S(1)}, bf16[512,512]{1,0:T(8,128)(2,1)S(1)}, u32[]{:S(2)}, u32[]{:S(2)}) collective-permute-start(bf16[512,512]{1,0:T(8,128)(2,1)S(1)} %bitcast.14), channel_id=1, source_target_pairs={{0,32},{32,0},{1,33},{33,1},{2,34},{34,2},{3,35},{35,3},{4,36},{36... | collective-permute-start | bytes 1572872 | tf_op jit(solution)/shard_map/ppermute | solution.py:179
  32.5 4.2 %copy-start.6 = (bf16[2,8,32,512]{3,2,1,0:T(8,128)(2,1)S(1)}, bf16[2,8,32,512]{3,2,1,0:T(8,128)(2,1)}, u32[]{:S(2)}) copy-start(bf16[2,8,32,512]{3,2,1,0:T(8,128)(2,1)} %param.7) | copy-start | bytes 1572868
  32.7 3.9 %collective-permute-start.1 = (bf16[512,512]{1,0:T(8,128)(2,1)S(1)}, bf16[512,512]{1,0:T(8,128)(2,1)S(1)}, u32[]{:S(2)}, u32[]{:S(2)}) collective-permute-start(bf16[512,512]{1,0:T(8,128)(2,1)S(1)} %bitcast_select_fusion), channel_id=1, source_target_pairs={{0,32},{32,0},{1,33},{33,1},{2,34},{34,2},{3,35},{35,3},{4,36},{36... | collective-permute-start | bytes 1572872 | tf_op jit(solution)/shard_map/ppermute | solution.py:179
  34.8 0.8 copy-start.8
  36.6 1.0 copy-start.9
  48.8 1.2 %copy-start = (bf16[1024,768]{1,0:T(8,128)(2,1)}, bf16[1024,768]{1,0:T(8,128)(2,1)S(1)}, u32[]{:S(2)}) copy-start(bf16[1024,768]{1,0:T(8,128)(2,1)S(1)} %get-tuple-element.11) | copy-start | bytes 4718596
  50.0 21.8 %all-to-all-start.2 = ((bf16[8,128,512]{2,1,0:T(8,128)(2,1)}), bf16[8,128,512]{2,1,0:T(8,128)(2,1)S(1)}, u32[]{:S(2)}, u32[]{:S(2)}) async-start(bf16[8,128,512]{2,1,0:T(8,128)(2,1)} %bitcast.7), calls=%async_computation.2 | async-start | bytes 2097152 | tf_op jit(solution)/shard_map/all_to_all | solution.py:183
  57.2 2.0 %copy-start.1 = (bf16[1024,768]{1,0:T(8,128)(2,1)S(1)}, bf16[1024,768]{1,0:T(8,128)(2,1)}, u32[]{:S(2)}) copy-start(bf16[1024,768]{1,0:T(8,128)(2,1)} %copy-done) | copy-start | bytes 4718596
  60.0 1.5 %copy-start.2 = (f32[1024,512]{1,0:T(8,128)}, f32[1024,512]{1,0:T(8,128)S(1)}, u32[]{:S(2)}) copy-start(f32[1024,512]{1,0:T(8,128)S(1)} %convolution_add_fusion) | copy-start | bytes 6291460
  60.0 16.2 %copy-start.7 = (bf16[2,8,32,512]{3,2,1,0:T(8,128)(2,1)S(1)}, bf16[2,8,32,512]{3,2,1,0:T(8,128)(2,1)}, u32[]{:S(2)}) copy-start(bf16[2,8,32,512]{3,2,1,0:T(8,128)(2,1)} %param.7) | copy-start | bytes 1572868
  60.0 16.2 %copy-start.10 = (bf16[512,512]{1,0:T(8,128)(2,1)S(1)}, bf16[512,512]{1,0:T(8,128)(2,1)}, u32[]{:S(2)}) copy-start(bf16[512,512]{1,0:T(8,128)(2,1)} %copy-done.8) | copy-start | bytes 1572868
  61.5 32.5 %collective-permute-start.2 = (bf16[512,512]{1,0:T(8,128)(2,1)}, bf16[512,512]{1,0:T(8,128)(2,1)}, u32[]{:S(2)}, u32[]{:S(2)}) collective-permute-start(bf16[512,512]{1,0:T(8,128)(2,1)} %slice.58), channel_id=1, source_target_pairs={{0,32},{32,0},{1,33},{33,1},{2,34},{34,2},{3,35},{35,3},{4,36},{36... | collective-permute-start | bytes 1572872 | tf_op jit(solution)/shard_map/ppermute | solution.py:179
  72.6 11.6 %all-to-all-start.3 = ((bf16[8,16,640]{2,1,0:T(8,128)(2,1)}), bf16[8,16,640]{2,1,0:T(8,128)(2,1)S(1)}, u32[]{:S(2)}, u32[]{:S(2)}) async-start(bf16[8,16,640]{2,1,0:T(8,128)(2,1)} %near_sum.1), calls=%async_computation.3 | async-start | bytes 327680 | tf_op jit(solution)/shard_map/all_to_all | solution.py:183
  76.1 17.8 %copy-start.3 = (f32[1024,512]{1,0:T(8,128)S(1)}, f32[1024,512]{1,0:T(8,128)}, u32[]{:S(2)}) copy-start(f32[1024,512]{1,0:T(8,128)} %copy-done.2) | copy-start | bytes 6291460
  77.8 18.0 %copy-start.12 = (bf16[2,8,32,512]{3,2,1,0:T(8,128)(2,1)S(1)}, bf16[2,8,32,512]{3,2,1,0:T(8,128)(2,1)}, u32[]{:S(2)}) copy-start(bf16[2,8,32,512]{3,2,1,0:T(8,128)(2,1)} %param.8) | copy-start | bytes 1572868
  85.0 22.0 %all-to-all-start.4 = ((bf16[16,16,640]{2,1,0:T(8,128)(2,1)}), bf16[16,16,640]{2,1,0:T(8,128)(2,1)S(1)}, u32[]{:S(2)}, u32[]{:S(2)}) async-start(bf16[16,16,640]{2,1,0:T(8,128)(2,1)} %broadcast_in_dim.30), calls=%async_computation.4 | async-start | bytes 655360 | tf_op jit(solution)/shard_map/all_to_all | solution.py:183
  94.0 2.1 %copy-start.4 = (f32[1024,512]{1,0:T(8,128)S(1)}, f32[1024,512]{1,0:T(8,128)}, u32[]{:S(2)}) copy-start(f32[1024,512]{1,0:T(8,128)} %maximum_convert_fusion) | copy-start | bytes 6291460

commit v9 on v8

--- a/solution.py
+++ b/solution.py
@@ -10,7 +10,7 @@
 HEAD = 64
 ROW = 32
 SPAN = 128
-STEP = 256
+STEP = 512
 gain = 6.0 / HEAD
 tiny_eps = 1e-06
 f32, bf16 = jnp.float32, jnp.bfloat16
@@ -50,10 +50,12 @@
     return jnp.where(first, block[:span], block[span:])
 
 
-def attention(q_half, k_half, v_half, grad_att, same_row):
-    k_two, v_two = stacked(k_half), stacked(v_half)
-    exps = jnp.where(same_row, jnp.exp(dot_nt(k_two, q_half) * gain), 0.0)
-    grad_probs = dot_nt(v_two, grad_att)
+def scores_of(q_half, k_two, v_two, grad_att):
+    return dot_nt(k_two, q_half), dot_nt(v_two, grad_att)
+
+
+def softmax_of(scores, grad_probs, same_row):
+    exps = jnp.where(same_row, jnp.exp(scores * gain), 0.0)
     probs, d_scores = [], []
     for half in (slice(0, SPAN), slice(SPAN, 2 * SPAN)):
         part = exps[half] * (1.0 / jnp.sum(exps[half], axis=0, keepdims=True))
@@ -61,13 +63,24 @@
         total = jnp.sum(weighted, axis=0, keepdims=True)
         probs.append(part.astype(bf16))
         d_scores.append(((weighted - part * total) * gain).astype(bf16))
-    probs, d_scores = jnp.concatenate(probs, axis=0), jnp.concatenate(d_scores, axis=0)
-    return (
-        dot_tn(probs, v_two).astype(bf16),
-        dot_tn(d_scores, k_two),
-        unstacked(dot_nn(d_scores, q_half)),
-        unstacked(dot_nn(probs, grad_att)).astype(bf16),
-    )
+    return jnp.concatenate(probs, axis=0), jnp.concatenate(d_scores, axis=0)
+
+
+def attention(blocks, same_row):
+    twos = [(stacked(k_half), stacked(v_half)) for _, k_half, v_half, _ in blocks]
+    scores = [
+        scores_of(q_half, *two, grad_att) for (q_half, _, _, grad_att), two in zip(blocks, twos)
+    ]
+    parts = [softmax_of(*pair, same_row) for pair in scores]
+    return [
+        (
+            dot_tn(probs, v_two).astype(bf16),
+            dot_tn(d_scores, k_two),
+            unstacked(dot_nn(d_scores, q_half)),
+            unstacked(dot_nn(probs, grad_att)).astype(bf16),
+        )
+        for (q_half, _, _, grad_att), (k_two, v_two), (probs, d_scores) in zip(blocks, twos, parts)
+    ]
 
 
 def layer_kernel(
@@ -106,13 +119,18 @@
     q_half, k_half = q_unit.astype(bf16), k_unit.astype(bf16)
     v_half = second[:, :width].astype(bf16)
     grad_att = dot_nt(grads_ref[here, :], wo_ref[...]).astype(bf16)
-    spans = []
-    for low in range(0, STEP, SPAN):
-        pairs = []
-        for left in range(0, width, tile):
-            at = (slice(low, low + SPAN), slice(left, left + tile))
-            pairs.append(attention(q_half[at], k_half[at], v_half[at], grad_att[at], same_row))
-        spans.append([jnp.concatenate(part, axis=1) for part in zip(*pairs)])
+    places = [
+        (slice(low, low + SPAN), slice(left, left + tile))
+        for low in range(0, STEP, SPAN)
+        for left in range(0, width, tile)
+    ]
+    found = attention(
+        [(q_half[at], k_half[at], v_half[at], grad_att[at]) for at in places], same_row
+    )
+    spans = [
+        [jnp.concatenate(part, axis=1) for part in zip(*found[i : i + 2])]
+        for i in range(0, len(found), 2)
+    ]
     attended, d_query, d_key, d_value = (jnp.concatenate(part, axis=0) for part in zip(*spans))
     att_ref[here, :] = attended
     d_query = (q_scale * (d_query - q_unit * head_means(q_unit * d_query, ones))).astype(bf16)

time: 108 us -> 105 us (0.972)
  Pallas kernels: 14.7 us -> 11.6 us
    pallas_call x1, Pallas kernels: 10.5 us -> 7.3 us  [layer(): pl.pallas_call(layer_kernel, grid=(tokens // STEP,), in_specs=[whole(arra...]
  transfers between devices with their start and end apart: 7 -> 7, of which waited for: 5 -> 5; matrix products, arithmetic and copies ran while one was open for 10% -> 11% of each run, Pallas kernels for 1% -> 1%
where the time goes in v9:
time: 105 us
  starting transfers between devices  34.7 us (33%)
  waiting for transfers between devices  23.8 us (23%)
  blocking collectives  19 us (18%)
  Pallas kernels  11.6 us (11%)
  other arithmetic  6.52 us (6%)
  local copies, waits for them, and re-layouts  5.4 us (5%)
  matrix products  2.72 us (3%)
    all_to_all x4, starting transfers between devices, sent(): return lax.all_to_all(blocks, axis, split_axis=0, concat_axis=0, tiled=True)  24.7 us
    all_to_all x4, waiting for transfers between devices, sent(): return lax.all_to_all(blocks, axis, split_axis=0, concat_axis=0, tiled=True)  22.8 us
    all_to_all x1, blocking collectives, sent(): return lax.all_to_all(blocks, axis, split_axis=0, concat_axis=0, tiled=True)  19 us
    ppermute x3, starting transfers between devices, swapped(): return lax.ppermute(block, 'core', [(0, 1), (1, 0)])  9.96 us
    pallas_call x1, Pallas kernels, layer(): pl.pallas_call(layer_kernel, grid=(tokens // STEP,), in_specs=[whole(arra...  7.3 us
    unnamed x28, local copies, waits for them, and re-layouts  3.51 us
    dot_general x2, matrix products, dot_nt(): lax.dot_general(a, b, (((1,), (1,)), ((), ())), preferred_element_type=f32)  2.72 us
    convert_element_type x1, other arithmetic, local(): return (done.astype(bf16).reshape(trace_rows.shape), *weight_grads)  2.24 us
  transfers between devices with their start and end apart: 7, of which 5 were waited for; matrix products, arithmetic and copies ran while one was open for 11% of the time, Pallas kernels for 1%

profile of v9, /device:TPU:1, one launch (start us, length us, event | category | flops | bytes accessed | tf_op | source)
XLA Modules:
  0.0 104.6 jit_solution(4017682435754067847)
XLA Ops:
  0.6 0.0 copy-start.5
  0.7 0.0 copy-start.11
  0.7 1.6 %weight_copies.1 = bf16[8,16,640]{2,1,0:T(8,128)(2,1)} custom-call(s32[1]{0:T(128)} %bitcast.3.core_ref, s32[1]{0:T(128)} %bitcast.4.yl_ref, bf16[16,512]{1,0:T(8,128)(2,1)} %wq_ref.1, bf16[16,512]{1,0:T(8,128)(2,1)} %wk_ref.1, bf16[16,512]{1,0:T(8,128)(2,1)} %wv_ref.1, bf16[16,512]{1,0:T(8,128)(2,1)} %wo_ref.1), custom_call_target="tpu_custom_call" | custom-call | tf_op jit(solution)/shard_map/weight_copies/pallas_call | solution.py:257
  2.3 19.0 %all_to_all.25.blocks_ref = bf16[8,16,640]{2,1,0:T(8,128)(2,1)S(1)} all-to-all(bf16[8,16,640]{2,1,0:T(8,128)(2,1)} %weight_copies.1), channel_id=1, replica_groups=mesh['yh'=4,'yl'=2,'core'=2,'x'=4,'z'=8] {'z'}, dimensions={0} | all-to-all | bytes 327680 | tf_op jit(solution)/shard_map/all_to_all | solution.py:201
  21.3 1.1 %weight_lines.1 = bf16[8,128,512]{2,1,0:T(8,128)(2,1)} custom-call(s32[1]{0:T(128)} %bitcast.3.core_ref, bf16[8,16,640]{2,1,0:T(8,128)(2,1)S(1)} %all_to_all.25.blocks_ref), custom_call_target="tpu_custom_call" | custom-call | tf_op jit(solution)/shard_map/weight_lines/pallas_call | solution.py:287
  22.4 5.0 %all-to-all-start.1 = ((bf16[8,128,512]{2,1,0:T(8,128)(2,1)}), bf16[8,128,512]{2,1,0:T(8,128)(2,1)S(1)}, u32[]{:S(2)}, u32[]{:S(2)}) async-start(bf16[8,128,512]{2,1,0:T(8,128)(2,1)} %weight_lines.1), calls=%async_computation.1 | async-start | bytes 2097152 | tf_op jit(solution)/shard_map/all_to_all | solution.py:201
  27.4 4.8 %collective-permute-start = (bf16[512,512]{1,0:T(8,128)(2,1)S(1)}, bf16[512,512]{1,0:T(8,128)(2,1)S(1)}, u32[]{:S(2)}, u32[]{:S(2)}) collective-permute-start(bf16[512,512]{1,0:T(8,128)(2,1)S(1)} %bitcast.14), channel_id=1, source_target_pairs={{0,32},{32,0},{1,33},{33,1},{2,34},{34,2},{3,35},{35,3},{4,36},{36... | collective-permute-start | bytes 1572872 | tf_op jit(solution)/shard_map/ppermute | solution.py:197
  32.2 0.1 iota_compare_fusion
  32.3 0.1 lt.23
  32.4 0.1 broadcast_in_dim.26
  32.4 0.1 broadcast_in_dim.27
  32.5 0.0 copy-done.11
  32.5 0.1 bitcast_select_fusion
  32.7 2.1 %collective-permute-start.1 = (bf16[512,512]{1,0:T(8,128)(2,1)S(1)}, bf16[512,512]{1,0:T(8,128)(2,1)S(1)}, u32[]{:S(2)}, u32[]{:S(2)}) collective-permute-start(bf16[512,512]{1,0:T(8,128)(2,1)S(1)} %bitcast_select_fusion), channel_id=1, source_target_pairs={{0,32},{32,0},{1,33},{33,1},{2,34},{34,2},{3,35},{35,3},{4,36},{36... | collective-permute-start | bytes 1572872 | tf_op jit(solution)/shard_map/ppermute | solution.py:197
  34.7 0.0 collective-permute-done
  34.8 0.0 copy-start.8
  34.8 0.3 multiply_reduce_fusion
  35.0 0.5 copy-done.8
  35.6 1.1 %collective-permute-done.1 = bf16[512,512]{1,0:T(8,128)(2,1)S(1)} collective-permute-done((bf16[512,512]{1,0:T(8,128)(2,1)S(1)}, bf16[512,512]{1,0:T(8,128)(2,1)S(1)}, u32[]{:S(2)}, u32[]{:S(2)}) %collective-permute-start.1) | collective-permute-done | bytes 524320 | tf_op jit(solution)/shard_map/ppermute | solution.py:197
  36.6 0.1 pad_maximum_fusion.grads_ref
  36.7 0.9 copy-done.9
  37.7 0.3 multiply_convert_fusion.normed_ref
  38.0 0.4 all-to-all-done.1
  38.4 7.3 %attention_layer.1 = (bf16[1024,768]{1,0:T(8,128)(2,1)S(1)}, bf16[1024,512]{1,0:T(8,128)(2,1)}) custom-call(bf16[1024,512]{1,0:T(8,128)(2,1)S(1)} %multiply_convert_fusion.normed_ref, bf16[1024,512]{1,0:T(8,128)(2,1)S(1)} %pad_maximum_fusion.grads_ref, bf16[1024,512]{1,0:T(8,128)(2,1)S(1)} %bitcast.11), custom_call_target="tpu_custom_call" | custom-call | flops 2684354560 | bytes 6291456 | tf_op jit(solution)/shard_map/attention_layer/pallas_call | solution.py:171
  45.7 1.2 %copy-done = bf16[1024,768]{1,0:T(8,128)(2,1)} copy-done((bf16[1024,768]{1,0:T(8,128)(2,1)}, bf16[1024,768]{1,0:T(8,128)(2,1)S(1)}, u32[]{:S(2)}) %copy-start) | copy-done | bytes 1572888
  46.8 7.2 %all-to-all-start.2 = ((bf16[8,128,512]{2,1,0:T(8,128)(2,1)}), bf16[8,128,512]{2,1,0:T(8,128)(2,1)S(1)}, u32[]{:S(2)}, u32[]{:S(2)}) async-start(bf16[8,128,512]{2,1,0:T(8,128)(2,1)} %bitcast.7), calls=%async_computation.2 | async-start | bytes 2097152 | tf_op jit(solution)/shard_map/all_to_all | solution.py:201
  54.1 2.0 %fusion.1 = f32[1024,512]{1,0:T(8,128)S(1)} fusion(bf16[1024,768]{1,0:T(8,128)(2,1)} %copy-done, bf16[1024,512]{1,0:T(8,128)(2,1)S(1)} %bitcast.12), kind=kOutput, calls=%fused_computation.11 | convolution fusion | flops 402653184 | bytes 3276800 | tf_op jit(solution)/shard_map/dot_general | solution.py:24
  56.0 0.0 copy-done.1
  56.1 0.7 convolution_add_fusion
  56.8 0.0 copy-start.7
  56.8 0.0 copy-start.10
  56.8 0.9 slice.58
  57.7 0.6 copy-done.2
  58.3 3.1 %collective-permute-start.2 = (bf16[512,512]{1,0:T(8,128)(2,1)}, bf16[512,512]{1,0:T(8,128)(2,1)}, u32[]{:S(2)}, u32[]{:S(2)}) collective-permute-start(bf16[512,512]{1,0:T(8,128)(2,1)} %slice.58), channel_id=1, source_target_pairs={{0,32},{32,0},{1,33},{33,1},{2,34},{34,2},{3,35},{35,3},{4,36},{36... | collective-permute-start | bytes 1572872 | tf_op jit(solution)/shard_map/ppermute | solution.py:197
  61.5 7.2 %all-to-all-done.2.blocks_ref = bf16[8,128,512]{2,1,0:T(8,128)(2,1)S(1)} async-done(((bf16[8,128,512]{2,1,0:T(8,128)(2,1)}), bf16[8,128,512]{2,1,0:T(8,128)(2,1)S(1)}, u32[]{:S(2)}, u32[]{:S(2)}) %all-to-all-start.2) | async-done | bytes 1048608 | tf_op jit(solution)/shard_map/all_to_all | solution.py:201
  68.6 0.8 near_sum.1
  69.4 3.5 %all-to-all-start.3 = ((bf16[8,16,640]{2,1,0:T(8,128)(2,1)}), bf16[8,16,640]{2,1,0:T(8,128)(2,1)S(1)}, u32[]{:S(2)}, u32[]{:S(2)}) async-start(bf16[8,16,640]{2,1,0:T(8,128)(2,1)} %near_sum.1), calls=%async_computation.3 | async-start | bytes 327680 | tf_op jit(solution)/shard_map/all_to_all | solution.py:201
  73.0 1.6 %maximum_convert_fusion = f32[1024,512]{1,0:T(8,128)} fusion(bf16[512,512]{1,0:T(8,128)(2,1)S(1)} %copy-done.10, bf16[512,512]{1,0:T(8,128)(2,1)S(1)} %bitcast.17), kind=kLoop, calls=%fused_computation.6 | loop fusion | flops 2097152 | bytes 3145728 | tf_op jit(solution)/shard_map/convert_element_type | solution.py:379
  74.6 6.4 %all-to-all-done.3 = bf16[8,16,640]{2,1,0:T(8,128)(2,1)S(1)} async-done(((bf16[8,16,640]{2,1,0:T(8,128)(2,1)}), bf16[8,16,640]{2,1,0:T(8,128)(2,1)S(1)}, u32[]{:S(2)}, u32[]{:S(2)}) %all-to-all-start.3) | async-done | bytes 163872 | tf_op jit(solution)/shard_map/all_to_all | solution.py:201
  81.1 0.8 broadcast_in_dim.30
  81.8 9.0 %all-to-all-start.4 = ((bf16[16,16,640]{2,1,0:T(8,128)(2,1)}), bf16[16,16,640]{2,1,0:T(8,128)(2,1)S(1)}, u32[]{:S(2)}, u32[]{:S(2)}) async-start(bf16[16,16,640]{2,1,0:T(8,128)(2,1)} %broadcast_in_dim.30), calls=%async_computation.4 | async-start | bytes 655360 | tf_op jit(solution)/shard_map/all_to_all | solution.py:201
  90.8 0.0 collective-permute-done.2
  90.8 0.0 copy-done.3
  90.8 1.8 %multiply_reduce_fusion.1 = f32[512]{0:T(512)S(1)} fusion(f32[1024,512]{1,0:T(8,128)} %maximum_convert_fusion, bf16[512,512]{1,0:T(8,128)(2,1)} %collective-permute-done.2, f32[1024,512]{1,0:T(8,128)S(1)} %copy-done.3, f32[512]{0:T(512)S(1)} %slice.26), kind=kLoop, calls=%fused_computation.9 | loop fusion | flops 1310208 | bytes 2625536 | tf_op jit(solution)/shard_map/reduce_sum | solution.py:402
  92.6 0.2 copy-done.4
  92.9 2.2 %add_convert_fusion = bf16[512,512]{1,0:T(8,128)(2,1)} fusion(f32[1024,512]{1,0:T(8,128)S(1)} %copy-done.4, bf16[512,512]{1,0:T(8,128)(2,1)} %collective-permute-done.2, f32[1024,512]{1,0:T(8,128)S(1)} %copy-done.3, f32[512]{0:T(512)S(1)} %broadcast_multiply_fusion, f32[512]{0:T(512)S(1)} %slice.26, bf16[2,8,32,512]{3,2,1,0:T(8,128)(2,1)S(1)} %copy-done.12, ...), kind=kLoop, calls=%fused_computation.8 | loop fusion | flops 2621440 | bytes 3674624 | tf_op jit(solution)/shard_map/convert_element_type | solution.py:404
  95.1 8.8 %all-to-all-done.4.blocks_ref = bf16[16,16,640]{2,1,0:T(8,128)(2,1)S(1)} async-done(((bf16[16,16,640]{2,1,0:T(8,128)(2,1)}), bf16[16,16,640]{2,1,0:T(8,128)(2,1)S(1)}, u32[]{:S(2)}, u32[]{:S(2)}) %all-to-all-start.4) | async-done | bytes 327712 | tf_op jit(solution)/shard_map/all_to_all | solution.py:201
  103.9 0.7 final_sum.1
  (19 shorter events, 0.1 us)
Async XLA Ops:
  0.6 26.8 %copy-start.5 = (bf16[2,8,32,512]{3,2,1,0:T(8,128)(2,1)S(1)}, bf16[2,8,32,512]{3,2,1,0:T(8,128)(2,1)}, u32[]{:S(2)}) copy-start(bf16[2,8,32,512]{3,2,1,0:T(8,128)(2,1)} %param.7) | copy-start | bytes 1572868
  0.6 31.6 %copy-start.13 = (s32[1,2]{1,0:T(1,128)S(1)}, s32[1,2]{1,0:T(1,128)}, u32[]{:S(2)}) copy-start(s32[1,2]{1,0:T(1,128)} %param.9) | copy-start | bytes 28
  0.7 31.9 %copy-start.11 = (bf16[2,8,32,512]{3,2,1,0:T(8,128)(2,1)S(1)}, bf16[2,8,32,512]{3,2,1,0:T(8,128)(2,1)}, u32[]{:S(2)}) copy-start(bf16[2,8,32,512]{3,2,1,0:T(8,128)(2,1)} %param.8) | copy-start | bytes 1572868
  22.4 16.0 %all-to-all-start.1 = ((bf16[8,128,512]{2,1,0:T(8,128)(2,1)}), bf16[8,128,512]{2,1,0:T(8,128)(2,1)S(1)}, u32[]{:S(2)}, u32[]{:S(2)}) async-start(bf16[8,128,512]{2,1,0:T(8,128)(2,1)} %weight_lines.1), calls=%async_computation.1 | async-start | bytes 2097152 | tf_op jit(solution)/shard_map/all_to_all | solution.py:201
  27.4 7.3 %collective-permute-start = (bf16[512,512]{1,0:T(8,128)(2,1)S(1)}, bf16[512,512]{1,0:T(8,128)(2,1)S(1)}, u32[]{:S(2)}, u32[]{:S(2)}) collective-permute-start(bf16[512,512]{1,0:T(8,128)(2,1)S(1)} %bitcast.14), channel_id=1, source_target_pairs={{0,32},{32,0},{1,33},{33,1},{2,34},{34,2},{3,35},{35,3},{4,36},{36... | collective-permute-start | bytes 1572872 | tf_op jit(solution)/shard_map/ppermute | solution.py:197
  32.5 4.2 %copy-start.6 = (bf16[2,8,32,512]{3,2,1,0:T(8,128)(2,1)S(1)}, bf16[2,8,32,512]{3,2,1,0:T(8,128)(2,1)}, u32[]{:S(2)}) copy-start(bf16[2,8,32,512]{3,2,1,0:T(8,128)(2,1)} %param.7) | copy-start | bytes 1572868
  32.7 3.9 %collective-permute-start.1 = (bf16[512,512]{1,0:T(8,128)(2,1)S(1)}, bf16[512,512]{1,0:T(8,128)(2,1)S(1)}, u32[]{:S(2)}, u32[]{:S(2)}) collective-permute-start(bf16[512,512]{1,0:T(8,128)(2,1)S(1)} %bitcast_select_fusion), channel_id=1, source_target_pairs={{0,32},{32,0},{1,33},{33,1},{2,34},{34,2},{3,35},{35,3},{4,36},{36... | collective-permute-start | bytes 1572872 | tf_op jit(solution)/shard_map/ppermute | solution.py:197
  34.8 0.8 copy-start.8
  36.6 1.0 copy-start.9
  45.7 1.2 %copy-start = (bf16[1024,768]{1,0:T(8,128)(2,1)}, bf16[1024,768]{1,0:T(8,128)(2,1)S(1)}, u32[]{:S(2)}) copy-start(bf16[1024,768]{1,0:T(8,128)(2,1)S(1)} %get-tuple-element.11) | copy-start | bytes 4718596
  46.8 21.8 %all-to-all-start.2 = ((bf16[8,128,512]{2,1,0:T(8,128)(2,1)}), bf16[8,128,512]{2,1,0:T(8,128)(2,1)S(1)}, u32[]{:S(2)}, u32[]{:S(2)}) async-start(bf16[8,128,512]{2,1,0:T(8,128)(2,1)} %bitcast.7), calls=%async_computation.2 | async-start | bytes 2097152 | tf_op jit(solution)/shard_map/all_to_all | solution.py:201
  54.0 2.0 %copy-start.1 = (bf16[1024,768]{1,0:T(8,128)(2,1)S(1)}, bf16[1024,768]{1,0:T(8,128)(2,1)}, u32[]{:S(2)}) copy-start(bf16[1024,768]{1,0:T(8,128)(2,1)} %copy-done) | copy-start | bytes 4718596
  56.8 1.5 %copy-start.2 = (f32[1024,512]{1,0:T(8,128)}, f32[1024,512]{1,0:T(8,128)S(1)}, u32[]{:S(2)}) copy-start(f32[1024,512]{1,0:T(8,128)S(1)} %convolution_add_fusion) | copy-start | bytes 6291460
  56.8 16.1 %copy-start.7 = (bf16[2,8,32,512]{3,2,1,0:T(8,128)(2,1)S(1)}, bf16[2,8,32,512]{3,2,1,0:T(8,128)(2,1)}, u32[]{:S(2)}) copy-start(bf16[2,8,32,512]{3,2,1,0:T(8,128)(2,1)} %param.7) | copy-start | bytes 1572868
  56.8 16.1 %copy-start.10 = (bf16[512,512]{1,0:T(8,128)(2,1)S(1)}, bf16[512,512]{1,0:T(8,128)(2,1)}, u32[]{:S(2)}) copy-start(bf16[512,512]{1,0:T(8,128)(2,1)} %copy-done.8) | copy-start | bytes 1572868
  58.3 32.5 %collective-permute-start.2 = (bf16[512,512]{1,0:T(8,128)(2,1)}, bf16[512,512]{1,0:T(8,128)(2,1)}, u32[]{:S(2)}, u32[]{:S(2)}) collective-permute-start(bf16[512,512]{1,0:T(8,128)(2,1)} %slice.58), channel_id=1, source_target_pairs={{0,32},{32,0},{1,33},{33,1},{2,34},{34,2},{3,35},{35,3},{4,36},{36... | collective-permute-start | bytes 1572872 | tf_op jit(solution)/shard_map/ppermute | solution.py:197
  69.4 11.6 %all-to-all-start.3 = ((bf16[8,16,640]{2,1,0:T(8,128)(2,1)}), bf16[8,16,640]{2,1,0:T(8,128)(2,1)S(1)}, u32[]{:S(2)}, u32[]{:S(2)}) async-start(bf16[8,16,640]{2,1,0:T(8,128)(2,1)} %near_sum.1), calls=%async_computation.3 | async-start | bytes 327680 | tf_op jit(solution)/shard_map/all_to_all | solution.py:201
  73.0 17.8 %copy-start.3 = (f32[1024,512]{1,0:T(8,128)S(1)}, f32[1024,512]{1,0:T(8,128)}, u32[]{:S(2)}) copy-start(f32[1024,512]{1,0:T(8,128)} %copy-done.2) | copy-start | bytes 6291460
  74.6 18.0 %copy-start.12 = (bf16[2,8,32,512]{3,2,1,0:T(8,128)(2,1)S(1)}, bf16[2,8,32,512]{3,2,1,0:T(8,128)(2,1)}, u32[]{:S(2)}) copy-start(bf16[2,8,32,512]{3,2,1,0:T(8,128)(2,1)} %param.8) | copy-start | bytes 1572868
  81.8 22.0 %all-to-all-start.4 = ((bf16[16,16,640]{2,1,0:T(8,128)(2,1)}), bf16[16,16,640]{2,1,0:T(8,128)(2,1)S(1)}, u32[]{:S(2)}, u32[]{:S(2)}) async-start(bf16[16,16,640]{2,1,0:T(8,128)(2,1)} %broadcast_in_dim.30), calls=%async_computation.4 | async-start | bytes 655360 | tf_op jit(solution)/shard_map/all_to_all | solution.py:201
  90.8 2.1 %copy-start.4 = (f32[1024,512]{1,0:T(8,128)S(1)}, f32[1024,512]{1,0:T(8,128)}, u32[]{:S(2)}) copy-start(f32[1024,512]{1,0:T(8,128)} %maximum_convert_fusion) | copy-start | bytes 6291460

commit v10 on v9

--- a/solution.py
+++ b/solution.py
@@ -173,7 +173,7 @@
         grid=(tokens // STEP,),
         in_specs=[whole(array.shape) for array in ins],
         out_specs=[pl.BlockSpec(memory_space=pltpu.HBM)] * 2,
-        out_shape=[jax.ShapeDtypeStruct(shape, bf16) for shape in outs],
+        out_shape=[pltpu.HBM(shape, bf16) for shape in outs],
         scratch_shapes=[pltpu.VMEM(shape, bf16) for shape in outs]
         + [
             pltpu.VMEM((tokens, depth // 2), bf16),

time: 105 us -> 104 us (level)
  local copies, waits for them, and re-layouts: 5.4 us -> 4.25 us
    unnamed x28 -> x26, local copies, waits for them, and re-layouts: 3.51 us -> 2.34 us
where the time goes in v10:
time: 104 us; the launch traced here: 103 us
  starting transfers between devices  34.7 us (33%)
  waiting for transfers between devices  23.8 us (23%)
  blocking collectives  19 us (18%)
  Pallas kernels  11.4 us (11%)
  other arithmetic  6.52 us (6%)
  local copies, waits for them, and re-layouts  4.25 us (4%)
  matrix products  2.72 us (3%)
    all_to_all x4, starting transfers between devices, sent(): return lax.all_to_all(blocks, axis, split_axis=0, concat_axis=0, tiled=True)  24.7 us
    all_to_all x4, waiting for transfers between devices, sent(): return lax.all_to_all(blocks, axis, split_axis=0, concat_axis=0, tiled=True)  22.7 us
    all_to_all x1, blocking collectives, sent(): return lax.all_to_all(blocks, axis, split_axis=0, concat_axis=0, tiled=True)  19 us
    ppermute x3, starting transfers between devices, swapped(): return lax.ppermute(block, 'core', [(0, 1), (1, 0)])  9.97 us
    pallas_call x1, Pallas kernels, layer(): pl.pallas_call(layer_kernel, grid=(tokens // STEP,), in_specs=[whole(arra...  7.18 us
    dot_general x2, matrix products, dot_nt(): lax.dot_general(a, b, (((1,), (1,)), ((), ())), preferred_element_type=f32)  2.72 us
    unnamed x26, local copies, waits for them, and re-layouts  2.34 us
    convert_element_type x1, other arithmetic, local(): return (done.astype(bf16).reshape(trace_rows.shape), *weight_grads)  2.24 us
  transfers between devices with their start and end apart: 7, of which 5 were waited for; matrix products, arithmetic and copies ran while one was open for 11% of the time, Pallas kernels for 1%

profile of v10, /device:TPU:1, one launch (start us, length us, event | category | flops | bytes accessed | tf_op | source)
XLA Modules:
  0.0 103.3 jit_solution(8966267727735817572)
XLA Ops:
  0.6 0.0 copy-start.3
  0.7 0.0 copy-start.9
  0.7 1.6 %weight_copies.1 = bf16[8,16,640]{2,1,0:T(8,128)(2,1)} custom-call(s32[1]{0:T(128)} %bitcast.3.core_ref, s32[1]{0:T(128)} %bitcast.4.yl_ref, bf16[16,512]{1,0:T(8,128)(2,1)} %wq_ref.1, bf16[16,512]{1,0:T(8,128)(2,1)} %wk_ref.1, bf16[16,512]{1,0:T(8,128)(2,1)} %wv_ref.1, bf16[16,512]{1,0:T(8,128)(2,1)} %wo_ref.1), custom_call_target="tpu_custom_call" | custom-call | tf_op jit(solution)/shard_map/weight_copies/pallas_call | solution.py:257
  2.3 19.0 %all_to_all.25.blocks_ref = bf16[8,16,640]{2,1,0:T(8,128)(2,1)S(1)} all-to-all(bf16[8,16,640]{2,1,0:T(8,128)(2,1)} %weight_copies.1), channel_id=1, replica_groups=mesh['yh'=4,'yl'=2,'core'=2,'x'=4,'z'=8] {'z'}, dimensions={0} | all-to-all | bytes 327680 | tf_op jit(solution)/shard_map/all_to_all | solution.py:201
  21.3 1.1 %weight_lines.1 = bf16[8,128,512]{2,1,0:T(8,128)(2,1)} custom-call(s32[1]{0:T(128)} %bitcast.3.core_ref, bf16[8,16,640]{2,1,0:T(8,128)(2,1)S(1)} %all_to_all.25.blocks_ref), custom_call_target="tpu_custom_call" | custom-call | tf_op jit(solution)/shard_map/weight_lines/pallas_call | solution.py:287
  22.4 5.0 %all-to-all-start.1 = ((bf16[8,128,512]{2,1,0:T(8,128)(2,1)}), bf16[8,128,512]{2,1,0:T(8,128)(2,1)S(1)}, u32[]{:S(2)}, u32[]{:S(2)}) async-start(bf16[8,128,512]{2,1,0:T(8,128)(2,1)} %weight_lines.1), calls=%async_computation.1 | async-start | bytes 2097152 | tf_op jit(solution)/shard_map/all_to_all | solution.py:201
  27.4 0.0 copy-done.3
  27.4 4.8 %collective-permute-start = (bf16[512,512]{1,0:T(8,128)(2,1)S(1)}, bf16[512,512]{1,0:T(8,128)(2,1)S(1)}, u32[]{:S(2)}, u32[]{:S(2)}) collective-permute-start(bf16[512,512]{1,0:T(8,128)(2,1)S(1)} %bitcast.14), channel_id=1, source_target_pairs={{0,32},{32,0},{1,33},{33,1},{2,34},{34,2},{3,35},{35,3},{4,36},{36... | collective-permute-start | bytes 1572872 | tf_op jit(solution)/shard_map/ppermute | solution.py:197
  32.2 0.0 copy-done.12
  32.2 0.1 iota_compare_fusion
  32.3 0.1 lt.23
  32.4 0.1 broadcast_in_dim.26
  32.5 0.1 broadcast_in_dim.27
  32.5 0.1 bitcast_select_fusion
  32.7 2.1 %collective-permute-start.1 = (bf16[512,512]{1,0:T(8,128)(2,1)S(1)}, bf16[512,512]{1,0:T(8,128)(2,1)S(1)}, u32[]{:S(2)}, u32[]{:S(2)}) collective-permute-start(bf16[512,512]{1,0:T(8,128)(2,1)S(1)} %bitcast_select_fusion), channel_id=1, source_target_pairs={{0,32},{32,0},{1,33},{33,1},{2,34},{34,2},{3,35},{35,3},{4,36},{36... | collective-permute-start | bytes 1572872 | tf_op jit(solution)/shard_map/ppermute | solution.py:197
  34.8 0.0 collective-permute-done
  34.8 0.0 copy-start.6
  34.8 0.3 multiply_reduce_fusion
  35.0 0.5 copy-done.6
  35.6 1.1 %collective-permute-done.1 = bf16[512,512]{1,0:T(8,128)(2,1)S(1)} collective-permute-done((bf16[512,512]{1,0:T(8,128)(2,1)S(1)}, bf16[512,512]{1,0:T(8,128)(2,1)S(1)}, u32[]{:S(2)}, u32[]{:S(2)}) %collective-permute-start.1) | collective-permute-done | bytes 524320 | tf_op jit(solution)/shard_map/ppermute | solution.py:197
  36.6 0.1 pad_maximum_fusion.grads_ref
  36.7 0.9 copy-done.7
  37.7 0.3 multiply_convert_fusion.normed_ref
  38.0 0.4 all-to-all-done.1
  38.4 7.2 %attention_layer.1 = (bf16[1024,768]{1,0:T(8,128)(2,1)}, bf16[1024,512]{1,0:T(8,128)(2,1)}) custom-call(bf16[1024,512]{1,0:T(8,128)(2,1)S(1)} %multiply_convert_fusion.normed_ref, bf16[1024,512]{1,0:T(8,128)(2,1)S(1)} %pad_maximum_fusion.grads_ref, bf16[1024,512]{1,0:T(8,128)(2,1)S(1)} %bitcast.11), custom_call_target="tpu_custom_call" | custom-call | flops 2684354560 | bytes 6291456 | tf_op jit(solution)/shard_map/attention_layer/pallas_call | solution.py:171
  45.6 7.2 %all-to-all-start.2 = ((bf16[8,128,512]{2,1,0:T(8,128)(2,1)}), bf16[8,128,512]{2,1,0:T(8,128)(2,1)S(1)}, u32[]{:S(2)}, u32[]{:S(2)}) async-start(bf16[8,128,512]{2,1,0:T(8,128)(2,1)} %bitcast.18), calls=%async_computation.2 | async-start | bytes 2097152 | tf_op jit(solution)/shard_map/all_to_all | solution.py:201
  52.8 2.0 %fusion.1 = f32[1024,512]{1,0:T(8,128)S(1)} fusion(bf16[1024,768]{1,0:T(8,128)(2,1)} %get-tuple-element.11, bf16[1024,512]{1,0:T(8,128)(2,1)S(1)} %bitcast.12), kind=kOutput, calls=%fused_computation.11 | convolution fusion | flops 402653184 | bytes 3276800 | tf_op jit(solution)/shard_map/dot_general | solution.py:24
  54.8 0.7 convolution_add_fusion
  55.5 0.0 copy-start
  55.5 0.0 copy-start.5
  55.5 0.0 copy-start.8
  55.5 0.9 slice.58
  56.4 0.6 copy-done
  57.0 3.2 %collective-permute-start.2 = (bf16[512,512]{1,0:T(8,128)(2,1)}, bf16[512,512]{1,0:T(8,128)(2,1)}, u32[]{:S(2)}, u32[]{:S(2)}) collective-permute-start(bf16[512,512]{1,0:T(8,128)(2,1)} %slice.58), channel_id=1, source_target_pairs={{0,32},{32,0},{1,33},{33,1},{2,34},{34,2},{3,35},{35,3},{4,36},{36... | collective-permute-start | bytes 1572872 | tf_op jit(solution)/shard_map/ppermute | solution.py:197
  60.2 7.1 %all-to-all-done.2.blocks_ref = bf16[8,128,512]{2,1,0:T(8,128)(2,1)S(1)} async-done(((bf16[8,128,512]{2,1,0:T(8,128)(2,1)}), bf16[8,128,512]{2,1,0:T(8,128)(2,1)S(1)}, u32[]{:S(2)}, u32[]{:S(2)}) %all-to-all-start.2) | async-done | bytes 1048608 | tf_op jit(solution)/shard_map/all_to_all | solution.py:201
  67.3 0.8 near_sum.1
  68.1 3.5 %all-to-all-start.3 = ((bf16[8,16,640]{2,1,0:T(8,128)(2,1)}), bf16[8,16,640]{2,1,0:T(8,128)(2,1)S(1)}, u32[]{:S(2)}, u32[]{:S(2)}) async-start(bf16[8,16,640]{2,1,0:T(8,128)(2,1)} %near_sum.1), calls=%async_computation.3 | async-start | bytes 327680 | tf_op jit(solution)/shard_map/all_to_all | solution.py:201
  71.7 0.0 copy-done.5
  71.7 1.6 %maximum_convert_fusion = f32[1024,512]{1,0:T(8,128)} fusion(bf16[512,512]{1,0:T(8,128)(2,1)S(1)} %copy-done.8, bf16[512,512]{1,0:T(8,128)(2,1)S(1)} %bitcast.17), kind=kLoop, calls=%fused_computation.6 | loop fusion | flops 2097152 | bytes 3145728 | tf_op jit(solution)/shard_map/convert_element_type | solution.py:379
  73.3 6.4 %all-to-all-done.3 = bf16[8,16,640]{2,1,0:T(8,128)(2,1)S(1)} async-done(((bf16[8,16,640]{2,1,0:T(8,128)(2,1)}), bf16[8,16,640]{2,1,0:T(8,128)(2,1)S(1)}, u32[]{:S(2)}, u32[]{:S(2)}) %all-to-all-start.3) | async-done | bytes 163872 | tf_op jit(solution)/shard_map/all_to_all | solution.py:201
  79.8 0.8 broadcast_in_dim.30
  80.5 9.0 %all-to-all-start.4 = ((bf16[16,16,640]{2,1,0:T(8,128)(2,1)}), bf16[16,16,640]{2,1,0:T(8,128)(2,1)S(1)}, u32[]{:S(2)}, u32[]{:S(2)}) async-start(bf16[16,16,640]{2,1,0:T(8,128)(2,1)} %broadcast_in_dim.30), calls=%async_computation.4 | async-start | bytes 655360 | tf_op jit(solution)/shard_map/all_to_all | solution.py:201
  89.5 0.0 collective-permute-done.2
  89.5 1.8 %multiply_reduce_fusion.1 = f32[512]{0:T(512)S(1)} fusion(f32[1024,512]{1,0:T(8,128)} %maximum_convert_fusion, bf16[512,512]{1,0:T(8,128)(2,1)} %collective-permute-done.2, f32[1024,512]{1,0:T(8,128)S(1)} %copy-done.1, f32[512]{0:T(512)S(1)} %slice.26), kind=kLoop, calls=%fused_computation.9 | loop fusion | flops 1310208 | bytes 2625536 | tf_op jit(solution)/shard_map/reduce_sum | solution.py:402
  91.3 0.2 copy-done.2
  91.6 2.2 %add_convert_fusion = bf16[512,512]{1,0:T(8,128)(2,1)} fusion(f32[1024,512]{1,0:T(8,128)S(1)} %copy-done.2, bf16[512,512]{1,0:T(8,128)(2,1)} %collective-permute-done.2, f32[1024,512]{1,0:T(8,128)S(1)} %copy-done.1, f32[512]{0:T(512)S(1)} %broadcast_multiply_fusion, f32[512]{0:T(512)S(1)} %slice.26, bf16[2,8,32,512]{3,2,1,0:T(8,128)(2,1)S(1)} %copy-done.10, ...), kind=kLoop, calls=%fused_computation.8 | loop fusion | flops 2621440 | bytes 3674624 | tf_op jit(solution)/shard_map/convert_element_type | solution.py:404
  93.8 8.8 %all-to-all-done.4.blocks_ref = bf16[16,16,640]{2,1,0:T(8,128)(2,1)S(1)} async-done(((bf16[16,16,640]{2,1,0:T(8,128)(2,1)}), bf16[16,16,640]{2,1,0:T(8,128)(2,1)S(1)}, u32[]{:S(2)}, u32[]{:S(2)}) %all-to-all-start.4) | async-done | bytes 327712 | tf_op jit(solution)/shard_map/all_to_all | solution.py:201
  102.6 0.7 final_sum.1
  (17 shorter events, 0.1 us)
Async XLA Ops:
  0.6 26.8 %copy-start.3 = (bf16[2,8,32,512]{3,2,1,0:T(8,128)(2,1)S(1)}, bf16[2,8,32,512]{3,2,1,0:T(8,128)(2,1)}, u32[]{:S(2)}) copy-start(bf16[2,8,32,512]{3,2,1,0:T(8,128)(2,1)} %param.7) | copy-start | bytes 1572868
  0.6 31.6 %copy-start.12 = (s32[1,2]{1,0:T(1,128)S(1)}, s32[1,2]{1,0:T(1,128)}, u32[]{:S(2)}) copy-start(s32[1,2]{1,0:T(1,128)} %param.9) | copy-start | bytes 28
  0.7 31.9 %copy-start.9 = (bf16[2,8,32,512]{3,2,1,0:T(8,128)(2,1)S(1)}, bf16[2,8,32,512]{3,2,1,0:T(8,128)(2,1)}, u32[]{:S(2)}) copy-start(bf16[2,8,32,512]{3,2,1,0:T(8,128)(2,1)} %param.8) | copy-start | bytes 1572868
  22.4 16.0 %all-to-all-start.1 = ((bf16[8,128,512]{2,1,0:T(8,128)(2,1)}), bf16[8,128,512]{2,1,0:T(8,128)(2,1)S(1)}, u32[]{:S(2)}, u32[]{:S(2)}) async-start(bf16[8,128,512]{2,1,0:T(8,128)(2,1)} %weight_lines.1), calls=%async_computation.1 | async-start | bytes 2097152 | tf_op jit(solution)/shard_map/all_to_all | solution.py:201
  27.4 7.3 %collective-permute-start = (bf16[512,512]{1,0:T(8,128)(2,1)S(1)}, bf16[512,512]{1,0:T(8,128)(2,1)S(1)}, u32[]{:S(2)}, u32[]{:S(2)}) collective-permute-start(bf16[512,512]{1,0:T(8,128)(2,1)S(1)} %bitcast.14), channel_id=1, source_target_pairs={{0,32},{32,0},{1,33},{33,1},{2,34},{34,2},{3,35},{35,3},{4,36},{36... | collective-permute-start | bytes 1572872 | tf_op jit(solution)/shard_map/ppermute | solution.py:197
  32.5 4.2 %copy-start.4 = (bf16[2,8,32,512]{3,2,1,0:T(8,128)(2,1)S(1)}, bf16[2,8,32,512]{3,2,1,0:T(8,128)(2,1)}, u32[]{:S(2)}) copy-start(bf16[2,8,32,512]{3,2,1,0:T(8,128)(2,1)} %param.7) | copy-start | bytes 1572868
  32.7 3.9 %collective-permute-start.1 = (bf16[512,512]{1,0:T(8,128)(2,1)S(1)}, bf16[512,512]{1,0:T(8,128)(2,1)S(1)}, u32[]{:S(2)}, u32[]{:S(2)}) collective-permute-start(bf16[512,512]{1,0:T(8,128)(2,1)S(1)} %bitcast_select_fusion), channel_id=1, source_target_pairs={{0,32},{32,0},{1,33},{33,1},{2,34},{34,2},{3,35},{35,3},{4,36},{36... | collective-permute-start | bytes 1572872 | tf_op jit(solution)/shard_map/ppermute | solution.py:197
  34.8 0.8 copy-start.6
  36.6 1.0 %copy-start.7 = (bf16[512,512]{1,0:T(8,128)(2,1)S(1)}, bf16[512,512]{1,0:T(8,128)(2,1)}, u32[]{:S(2)}) copy-start(bf16[512,512]{1,0:T(8,128)(2,1)} %copy-done.6) | copy-start | bytes 1572868
  45.6 21.8 %all-to-all-start.2 = ((bf16[8,128,512]{2,1,0:T(8,128)(2,1)}), bf16[8,128,512]{2,1,0:T(8,128)(2,1)S(1)}, u32[]{:S(2)}, u32[]{:S(2)}) async-start(bf16[8,128,512]{2,1,0:T(8,128)(2,1)} %bitcast.18), calls=%async_computation.2 | async-start | bytes 2097152 | tf_op jit(solution)/shard_map/all_to_all | solution.py:201
  52.8 2.0 %copy-start.11 = (bf16[1024,768]{1,0:T(8,128)(2,1)S(1)}, bf16[1024,768]{1,0:T(8,128)(2,1)}, u32[]{:S(2)}) copy-start(bf16[1024,768]{1,0:T(8,128)(2,1)} %get-tuple-element.11) | copy-start | bytes 4718596
  55.5 1.5 %copy-start = (f32[1024,512]{1,0:T(8,128)}, f32[1024,512]{1,0:T(8,128)S(1)}, u32[]{:S(2)}) copy-start(f32[1024,512]{1,0:T(8,128)S(1)} %convolution_add_fusion) | copy-start | bytes 6291460
  55.5 16.1 %copy-start.5 = (bf16[2,8,32,512]{3,2,1,0:T(8,128)(2,1)S(1)}, bf16[2,8,32,512]{3,2,1,0:T(8,128)(2,1)}, u32[]{:S(2)}) copy-start(bf16[2,8,32,512]{3,2,1,0:T(8,128)(2,1)} %param.7) | copy-start | bytes 1572868
  55.5 16.1 %copy-start.8 = (bf16[512,512]{1,0:T(8,128)(2,1)S(1)}, bf16[512,512]{1,0:T(8,128)(2,1)}, u32[]{:S(2)}) copy-start(bf16[512,512]{1,0:T(8,128)(2,1)} %copy-done.6) | copy-start | bytes 1572868
  57.0 32.5 %collective-permute-start.2 = (bf16[512,512]{1,0:T(8,128)(2,1)}, bf16[512,512]{1,0:T(8,128)(2,1)}, u32[]{:S(2)}, u32[]{:S(2)}) collective-permute-start(bf16[512,512]{1,0:T(8,128)(2,1)} %slice.58), channel_id=1, source_target_pairs={{0,32},{32,0},{1,33},{33,1},{2,34},{34,2},{3,35},{35,3},{4,36},{36... | collective-permute-start | bytes 1572872 | tf_op jit(solution)/shard_map/ppermute | solution.py:197
  68.1 11.6 %all-to-all-start.3 = ((bf16[8,16,640]{2,1,0:T(8,128)(2,1)}), bf16[8,16,640]{2,1,0:T(8,128)(2,1)S(1)}, u32[]{:S(2)}, u32[]{:S(2)}) async-start(bf16[8,16,640]{2,1,0:T(8,128)(2,1)} %near_sum.1), calls=%async_computation.3 | async-start | bytes 327680 | tf_op jit(solution)/shard_map/all_to_all | solution.py:201
  71.7 17.8 %copy-start.1 = (f32[1024,512]{1,0:T(8,128)S(1)}, f32[1024,512]{1,0:T(8,128)}, u32[]{:S(2)}) copy-start(f32[1024,512]{1,0:T(8,128)} %copy-done) | copy-start | bytes 6291460
  73.3 18.0 %copy-start.10 = (bf16[2,8,32,512]{3,2,1,0:T(8,128)(2,1)S(1)}, bf16[2,8,32,512]{3,2,1,0:T(8,128)(2,1)}, u32[]{:S(2)}) copy-start(bf16[2,8,32,512]{3,2,1,0:T(8,128)(2,1)} %param.8) | copy-start | bytes 1572868
  80.5 22.0 %all-to-all-start.4 = ((bf16[16,16,640]{2,1,0:T(8,128)(2,1)}), bf16[16,16,640]{2,1,0:T(8,128)(2,1)S(1)}, u32[]{:S(2)}, u32[]{:S(2)}) async-start(bf16[16,16,640]{2,1,0:T(8,128)(2,1)} %broadcast_in_dim.30), calls=%async_computation.4 | async-start | bytes 655360 | tf_op jit(solution)/shard_map/all_to_all | solution.py:201
  89.5 2.1 %copy-start.2 = (f32[1024,512]{1,0:T(8,128)S(1)}, f32[1024,512]{1,0:T(8,128)}, u32[]{:S(2)}) copy-start(f32[1024,512]{1,0:T(8,128)} %maximum_convert_fusion) | copy-start | bytes 6291460
